TPU v7x, 32 devices: a whole 2x2x4 slice. The times are simulated.
32 devices in a mesh: seq: 16 (over z, y, x), tp: 2 (over core).
Axes of the slice: x: 2, y: 2, z: 4, core: 2. Of those that a mesh axis runs over, the one named last changes fastest.
Arguments:
- hidden_in: bfloat16 [4096, 1536], P('seq'), may hold values from -6 to 6
- gate_proj: float32 [1536, 3072], P(('seq', 'tp')), may hold values from -0.15625 to 0.15625
- inner_proj: float32 [1536, 3072], P(('seq', 'tp')), may hold values from -0.15625 to 0.15625
- small_proj: float32 [1536, 304], P(('seq', 'tp')), may hold values from -0.15625 to 0.15625
- row_layout: int32 [32], replicated, may hold values from 0 to 31, each once
- conv_inner: float32 [4, 3072], P(None, 'tp'), may hold values from -3 to 3
- conv_shared: float32 [4, 256], replicated, may hold values from -3 to 3
- bias_inner: float32 [3072], P('tp'), may hold values from -3 to 3
- bias_shared: float32 [256], replicated, may hold values from -3 to 3
- dt_bias: float32 [48], P('tp'), may hold values from -4 to -1
- decay_log: float32 [48], P('tp'), may hold values from -8 to 0
- skip_gain: float32 [48], P('tp'), may hold values from 0.5 to 2
- norm_gain: float32 [3072], P('tp'), may hold values from 0.1 to 1.9
- out_proj: float32 [3072, 1536], P('tp', 'seq'), may hold values from -0.109375 to 0.109375
- prompt_lengths: int32 [8], replicated, may hold values from 1 to 2048, 4096 in all
- group_map: int32 [8], replicated, may hold values from 0 to 3
- init_states: float32 [4, 48, 64, 128], P(None, 'tp'), may hold values from -12 to 12
- page_table: int32 [32], P('seq'), may hold values from 0 to 31, as said below
Outputs:
- mixed_out: bfloat16 [4096, 1536], P(('seq', 'tp'))
- state_pages: float32 [32, 48, 64, 128], P('seq', 'tp')
Inputs may be any that keep to these rules, and one draw needn't show every extreme that they name: `prompt_lengths`: the lengths sum to 4096; the longest prompt has exactly 2048 tokens. `row_layout`: a permutation. `page_table`: no two snapshots share a slot; snapshot k goes to one of the 2 slots of the aligned block of 2 snapshots that holds k.
All inputs are finite; a program needn't handle non-finite values.
Results may differ from a plain program's by a relative error of at most 0.018.
Values may be sent and summed in bfloat16 or wider, within the bound.
No kernel may reach another device: no remote copies, remote signals or barrier semaphores. Data moves between devices by JAX's collectives and lax.ppermute only.
A program may use at most 192 MiB of HBM per device.

v0:
```python
import jax
import jax.numpy as jnp
from jax import lax
from jax.sharding import PartitionSpec as P

N = 128
CONV = 4
PAGE = 128
DI = 3072


epsilon = 1e-05


def from_behind(array, axis, by):
    count = lax.axis_size(axis)
    pairs = [(i, i + by) for i in range(count) if 0 <= i + by < count]
    return lax.ppermute(array, axis, pairs)


def entering(array, axis, combine, identity):
    count, mine = (lax.axis_size(axis), lax.axis_index(axis))
    everything = jax.tree.map(lambda part: lax.all_gather(part, axis), array)
    start = jax.tree.map(
        lambda part, zero: jnp.broadcast_to(jnp.asarray(zero, part.dtype), part.shape),
        array,
        identity,
    )

    def hop(k, before):
        reached = k < mine
        new = combine(before, jax.tree.map(lambda part: part[k], everything))
        return jax.tree.map(lambda a, b: jnp.where(reached, a, b), new, before)

    return lax.fori_loop(0, count, hop, start)


def token_meta(positions, lengths, groups, group_count):
    starts = jnp.cumsum(lengths) - lengths
    prompt_id = jnp.sum((starts[None, :] <= positions[:, None]).astype(jnp.int32), axis=1) - 1
    prompt_hot = prompt_id[:, None] == jnp.arange(lengths.shape[0], dtype=jnp.int32)[None, :]
    first_pos = jnp.sum(jnp.where(prompt_hot, starts[None, :], 0), axis=1)
    group_id = jnp.sum(jnp.where(prompt_hot, groups[None, :], 0), axis=1)
    group_hot = (group_id[:, None] == jnp.arange(group_count, dtype=jnp.int32)[None, :]).astype(
        jnp.float32
    )
    offset = positions - first_pos
    is_start = (offset == 0).astype(jnp.float32)
    return (prompt_id, offset, is_start, group_hot)


def conv_apply(source, edges, taps, conv_bias, offset):
    padded = jnp.concatenate([edges, source], axis=0).astype(jnp.float32)
    total_rows = source.shape[0]
    width = taps.shape[0]
    result = conv_bias[None, :] + jnp.zeros((total_rows, source.shape[1]), jnp.float32)
    for lag_index in range(width):
        within = (offset >= lag_index).astype(jnp.float32)[:, None]
        lo_row = width - 1 - lag_index
        result = result + taps[lag_index][None, :] * padded[lo_row : lo_row + total_rows] * within
    return jax.nn.silu(result)


def span_terms(
    x_span,
    b_span,
    c_span,
    dt_span,
    log_span,
    pid_span,
    start_span,
    group_span,
    init_states,
    skip_gain,
):
    highest = lax.Precision.HIGHEST
    length = x_span.shape[0]
    cumulative = jnp.cumsum(log_span, axis=0)
    before_log = cumulative - log_span
    slots = jnp.arange(length, dtype=jnp.int32)
    causal = (slots[:, None] >= slots[None, :]) & (pid_span[:, None] == pid_span[None, :])
    within = causal[:, :, None]
    decays = jnp.where(
        within,
        jnp.exp(jnp.where(within, cumulative[:, None, :] - cumulative[None, :, :], 0.0)),
        0.0,
    )
    scores = jnp.dot(c_span, b_span.T, precision=highest)
    mixing = decays * dt_span[None, :, :] * scores[:, :, None]
    y_part = jnp.einsum("tsh,shp->thp", mixing, x_span, precision=highest)
    opening = jnp.where(
        within,
        jnp.exp(jnp.where(within, cumulative[:, None, :] - before_log[None, :, :], 0.0)),
        0.0,
    )
    opening = jnp.sum(opening * start_span[None, :, None], axis=1)
    read_init = jnp.einsum("tn,ghpn->tghp", c_span, init_states, precision=highest)
    read_init = jnp.einsum("tg,tghp->thp", group_span, read_init, precision=highest)
    y_part = y_part + opening[:, :, None] * read_init + skip_gain[None, :, None] * x_span
    weights_last = decays[length - 1] * dt_span
    summary = jnp.einsum("sh,shp,sn->hpn", weights_last, x_span, b_span, precision=highest)
    init_last = jnp.einsum("g,ghpn->hpn", group_span[length - 1], init_states, precision=highest)
    summary = summary + opening[length - 1][:, None, None] * init_last
    alive_mask = (pid_span == pid_span[0]).astype(jnp.float32) * (1.0 - start_span[0])
    carried = alive_mask[:, None] * jnp.exp(cumulative)
    return (y_part, summary, carried[length - 1], carried)


def compose(earlier, later):
    return (earlier[0] * later[0], later[0][:, None, None] * earlier[1] + later[1])


def on_device(
    hidden_in,
    gate_proj,
    inner_proj,
    small_proj,
    row_layout,
    conv_inner,
    conv_shared,
    bias_inner,
    bias_shared,
    dt_bias,
    decay_log,
    skip_gain,
    norm_gain,
    out_proj,
    prompt_lengths,
    group_map,
    init_states,
    page_table,
):
    highest = lax.Precision.HIGHEST
    tok_rows = hidden_in.shape[0]
    block_rows = gate_proj.shape[0]
    half_heads = dt_bias.shape[0]
    head_dim = inner_proj.shape[1] // (2 * half_heads)
    spans = tok_rows // PAGE

    def fold_rows(pieces):
        row_count = pieces[0].shape[0]
        row_ids = jnp.arange(row_count, dtype=jnp.int32)
        logical = row_layout[row_ids // block_rows] * block_rows + row_ids % block_rows
        columns = jnp.take(hidden_in, logical, axis=1)
        return tuple(
            (
                jnp.dot(columns, weight_piece, preferred_element_type=jnp.float32)
                for weight_piece in pieces
            )
        )

    gate_blocks, inner_blocks = (
        lax.all_to_all(
            gate_proj.astype(jnp.bfloat16), "tp", split_axis=1, concat_axis=0, tiled=True
        ),
        lax.all_to_all(
            inner_proj.astype(jnp.bfloat16), "tp", split_axis=1, concat_axis=0, tiled=True
        ),
    )
    gate_sum, inner_sum = fold_rows(
        (
            lax.all_gather(gate_blocks, "seq", axis=0, tiled=True),
            lax.all_gather(inner_blocks, "seq", axis=0, tiled=True),
        )
    )
    shared_sum = fold_rows(
        (lax.all_gather(small_proj.astype(jnp.bfloat16), ("seq", "tp"), axis=0, tiled=True),)
    )[0]
    gate_val = gate_sum.astype(jnp.bfloat16)
    inner_val = inner_sum.astype(jnp.bfloat16)
    shared_val = shared_sum.astype(jnp.bfloat16)
    shared_bc = shared_val[:, : 2 * N]
    dt_raw = lax.dynamic_slice_in_dim(
        shared_val, 2 * N + lax.axis_index("tp") * half_heads, half_heads, 1
    )
    seq_index = lax.axis_index("seq")
    positions = seq_index * tok_rows + jnp.arange(tok_rows, dtype=jnp.int32)
    prompt_id, offset, is_start, group_hot = token_meta(
        positions, prompt_lengths, group_map, init_states.shape[0]
    )
    edge_inner, edge_shared = from_behind(
        (inner_val[tok_rows - (CONV - 1) :], shared_bc[tok_rows - (CONV - 1) :]), "seq", 1
    )
    x_conv = conv_apply(inner_val, edge_inner, conv_inner, bias_inner, offset)
    bc_conv = conv_apply(shared_bc, edge_shared, conv_shared, bias_shared, offset)
    dt_val = jax.nn.softplus(dt_raw.astype(jnp.float32) + dt_bias[None, :])
    log_rate = -jnp.exp(decay_log)[None, :] * dt_val
    c_spans = bc_conv[:, N:].reshape(spans, PAGE, N)
    items = (
        x_conv.reshape(spans, PAGE, half_heads, head_dim),
        bc_conv[:, :N].reshape(spans, PAGE, N),
        c_spans,
        dt_val.reshape(spans, PAGE, half_heads),
        log_rate.reshape(spans, PAGE, half_heads),
        prompt_id.reshape(spans, PAGE),
        is_start.reshape(spans, PAGE),
        group_hot.reshape(spans, PAGE, group_hot.shape[1]),
    )

    def run_span(span_items):
        return span_terms(*span_items, init_states, skip_gain)

    y_parts, summaries, span_decay, carried = lax.map(run_span, items)

    def advance(running, span_items):
        run_decay, run_state = running
        summary, decays = span_items
        return (
            (run_decay * decays, decays[:, None, None] * run_state + summary),
            (run_decay, run_state),
        )

    unit_decay = jnp.ones((half_heads,), jnp.float32)
    zero_state = jnp.zeros((half_heads, head_dim, N), jnp.float32)
    (dev_decay, dev_state), (in_decay, in_state) = lax.scan(
        advance, (unit_decay, zero_state), (summaries, span_decay)
    )
    carried_in = entering((dev_decay, dev_state), "seq", compose, (unit_decay, zero_state))
    incoming = in_state + in_decay[:, :, None, None] * carried_in[1][None]
    y_full = y_parts + carried[..., None] * jnp.einsum(
        "ctn,chpn->cthp", c_spans, incoming, precision=highest
    )
    endings = span_decay[:, :, None, None] * incoming + summaries
    page_slots = page_table - seq_index * spans
    state_pages = jnp.zeros_like(endings).at[page_slots].set(endings)
    gated = y_full.reshape(tok_rows, -1) * jax.nn.silu(gate_val.astype(jnp.float32))
    squares = lax.psum(jnp.sum(gated * gated, axis=1), "tp")
    normed = (gated * lax.rsqrt(squares / DI + epsilon)[:, None] * norm_gain[None, :]).astype(
        jnp.bfloat16
    )
    out_columns = lax.all_gather(out_proj.astype(jnp.bfloat16), "seq", axis=1, tiled=True)
    mixed_out = lax.psum_scatter(
        jnp.dot(normed, out_columns, preferred_element_type=jnp.float32).astype(jnp.bfloat16),
        "tp",
        scatter_dimension=0,
        tiled=True,
    )
    return (mixed_out, state_pages)


def solution(mesh):
    placed = (
        P("seq", None),
        P(("seq", "tp"), None),
        P(("seq", "tp"), None),
        P(("seq", "tp"), None),
        P(),
        P(None, "tp"),
        P(),
        P("tp"),
        P(),
        P("tp"),
        P("tp"),
        P("tp"),
        P("tp"),
        P("tp", "seq"),
        P(),
        P(),
        P(None, "tp", None, None),
        P("seq"),
    )
    return jax.shard_map(
        on_device,
        mesh=mesh,
        in_specs=placed,
        out_specs=(P(("seq", "tp"), None), P("seq", "tp", None, None)),
        check_vma=False,
    )
```

profile of v0, /device:TPU:0, one launch (start us, length us, event | category | flops | bytes accessed | tf_op | source)
XLA Modules:
  0.0 522.0 jit_solution(7343516775920000753)
XLA Ops:
  7.2 1.2 convert_element_type.83
  8.4 4.7 all_to_all.38
  15.8 4.5 fusion.78
  21.1 15.6 %compare_and_fusion = (pred[1536]{0:T(1024)(128)(4,1)S(1)}, s32[1536]{0:T(1024)S(1)}) fusion(pred[1536]{0:T(1024)(128)(4,1)S(1)} %compare_reduce_fusion, pred[1536]{0:T(1024)(128)(4,1)S(1)} %compare_reduce_fusion.1, pred[1536]{0:T(1024)(128)(4,1)S(1)} %compare_reduce_fusion.2, pred[1536]{0:T(1024)(128)(4,1)S(1)} %compare_reduce_fusion.3, ...), kind=kLoop, calls=%fused_computation.168 | loop fusion | flops 59904 | bytes 52324 | tf_op jit(solution)/shard_map/jit(_take)/and | solution.py:144
  36.7 4.8 gather_fusion
  41.5 50.2 %all_gather.25 = bf16[1536,304]{1,0:T(8,128)(2,1)S(1)} all-gather(bf16[48,304]{1,0:T(8,128)(2,1)S(1)} %convert_element_type.91), channel_id=1, replica_groups=mesh['seq'=16,'tp'=2] {'seq','tp'}, dimensions={0}, use_global_device_ids=true | all-gather | bytes 963072 | tf_op jit(solution)/shard_map/all_gather | solution.py:167
  92.6 1.3 collective-permute-start.1
  97.3 6.8 %all-gather.7.cloned.1.call-done = bf16[1536,1536]{1,0:T(8,128)(2,1)} async-done(((bf16[96,1536]{1,0:T(8,128)(2,1)}), bf16[1536,1536]{1,0:T(8,128)(2,1)}) %all-gather.7.cloned.1.call-update) | async-done | bytes 4718608 | tf_op jit(solution)/shard_map/all_gather | solution.py:163
  104.1 3.8 convolution_convert_fusion.2
  108.0 1.7 collective-permute-start
  111.3 1.3 divide_multiply_fusion
  112.6 2.0 reshape.425
  114.6 3.4 copy.103
  118.0 1.4 broadcast.219.clone
  120.0 58.6 %while.47 = (s32[]{:T(128)}, f32[2,128,24,64]{1,3,2,0:T(8,128)}, f32[2,24,64,128]{3,2,1,0:T(8,128)}, f32[2,24]{1,0:T(2,128)}, f32[2,128,24]{1,2,0:T(8,128)}, /*i...) while((s32[]{:T(128)}, f32[2,128,24,64]{1,3,2,0:T(8,128)}, ...), condition=%wide.region_7.9_spmd, body=%wide.region_4.8_spmd.sunk | while | flops 1854852352 | bytes 60997984 | solution.py:203
  122.3 2.6 exponential_select_fusion.3
  125.1 4.3 fusion.127
  129.5 2.4 fusion.128
  132.3 3.3 fusion.134
  135.7 1.1 copy-done.18
  137.9 7.2 %fusion.135 = f32[1,24,64,128]{3,0,2,1:T(1,128)S(1)} fusion(f32[4,24,64,128]{3,2,1,0:T(8,128)S(1)} %get-tuple-element.707, f32[2,128,4]{2,1,0:T(8,128)} %get-tuple-element.706, s32[]{:T(128)} %get-tuple-element.674, s32[]{:T(128)S(6)} %add.462), kind=kOutput, calls=%fused_computation.14.clone.1 | convolution fusion | flops 9437184 | bytes 3933188 | tf_op jit(solution)/shard_map/while/body/eval_jaxpr/g,ghpn->hpn/dot_general | solution.py:102
  146.0 1.2 copy-done.4
  151.7 2.6 exponential_select_fusion.3
  154.4 4.3 fusion.127
  158.8 2.4 fusion.128
  161.7 3.3 fusion.134
  165.0 1.1 copy-done.18
  167.2 7.2 %fusion.135 = f32[1,24,64,128]{3,0,2,1:T(1,128)S(1)} fusion(f32[4,24,64,128]{3,2,1,0:T(8,128)S(1)} %get-tuple-element.707, f32[2,128,4]{2,1,0:T(8,128)} %get-tuple-element.706, s32[]{:T(128)} %get-tuple-element.674, s32[]{:T(128)S(6)} %add.462), kind=kOutput, calls=%fused_computation.14.clone.1 | convolution fusion | flops 9437184 | bytes 3933188 | tf_op jit(solution)/shard_map/while/body/eval_jaxpr/g,ghpn->hpn/dot_general | solution.py:102
  175.3 1.2 copy-done.4
  178.7 1.3 broadcast.219.clone.1
  180.0 3.8 while.48
  180.0 1.0 bitcast_dynamic-update-slice_fusion.2
  181.9 0.9 bitcast_dynamic-update-slice_fusion.2
  184.8 4.7 all_to_all.39
  192.2 43.5 %all-reduce = f32[384]{0:T(512)S(1)} all-reduce(f32[384]{0:T(512)S(1)} %dynamic-update-slice), channel_id=2, replica_groups=mesh['seq'=16,'tp'=2] {'seq'}, use_global_device_ids=true, to_apply=%add | all-reduce | flops 384 | bytes 3072
  235.8 103.5 %all-gather.13.cloned.1.call-done = f32[384,64,128]{2,1,0:T(8,128)} async-done(((f32[24,64,128]{2,1,0:T(8,128)}), f32[384,64,128]{2,1,0:T(8,128)}) %all-gather.13.cloned.1.call-update) | async-done | bytes 12582928 | tf_op jit(solution)/shard_map/all_gather | solution.py:23
  339.3 21.7 %while.49 = (s32[]{:T(128)}, f32[24,64,128]{2,1,0:T(8,128)S(1)}, s32[]{:T(128)}, f32[16,24]{1,0:T(8,128)S(1)}, f32[16,24,64,128]{3,2,1,0:T(8,128)}, /*index=5*/s32[]{:T(128)}, s32[]{:T(128)}) while((s32[]{:T(128)}, f32[24,64,128]{2,1,0:T(8,128)S(1)}, s32[]{:T(128)}, f32[16,24]{1,0:T(8,128)S(1)}, f32[16,24,64,128]{3,2,1,0:T(8,128)}, ...), condition=%wide.region_11.13_spmd.clone, body=%wide.region_10.12_spmd.clone.sunk | while | flops 786436 | bytes 2359689 | solution.py:35
  339.3 1.4 fusion.139
  340.8 1.3 fusion.139
  342.1 1.3 fusion.139
  343.5 1.3 fusion.139
  344.8 1.3 fusion.139
  346.1 1.3 fusion.139
  347.5 1.3 fusion.139
  348.9 1.3 fusion.139
  350.2 1.3 fusion.139
  351.6 1.3 fusion.139
  352.9 1.3 fusion.139
  354.3 1.3 fusion.139
  355.6 1.3 fusion.139
  357.0 1.3 fusion.139
  358.3 1.3 fusion.139
  359.6 1.3 fusion.139
  361.0 4.0 multiply_add_fusion.1
  365.0 3.3 copy.130
  368.3 2.9 reshape.426
  371.2 49.6 %all-gather.9.cloned.1.call-done = bf16[1536,1536]{1,0:T(8,128)(2,1)} async-done(((bf16[96,1536]{1,0:T(8,128)(2,1)}), bf16[1536,1536]{1,0:T(8,128)(2,1)}) %all-gather.9.cloned.1.call-update) | async-done | bytes 4718608 | tf_op jit(solution)/shard_map/all_gather | solution.py:162
  420.8 5.2 %multiply_reduce_fusion.1 = (f32[256]{0:T(256)S(1)}, f32[256,1536]{1,0:T(8,128)}) fusion(f32[256,1536]{1,0:T(8,128)S(1)} %reshape.426, bf16[1536,1536]{1,0:T(8,128)(2,1)} %all-gather.9.cloned.1.call-done, bf16[1536,256]{1,0:T(8,128)(2,1)S(1)} %copy-done.22, pred[1536]{0:T(1024)(128)(4,1)S(1)} %copy-done.43), kind=kOutput, calls=%fused_computation.83 | convolution fusion | flops 1211891456 | bytes 8653312 | tf_op jit(solution)/shard_map/dot_general | solution.py:147
  426.0 2.4 psum.7
  428.5 74.7 %all-gather.11.cloned.1.call-done = bf16[1536,1536]{0,1:T(8,128)(2,1)} async-done(((bf16[1536,96]{0,1:T(8,128)(2,1)}), bf16[1536,1536]{0,1:T(8,128)(2,1)}) %all-gather.11.cloned.1.call-update) | async-done | bytes 4718608 | tf_op jit(solution)/shard_map/all_gather | solution.py:231
  503.1 5.3 %convolution_convert_fusion = bf16[256,1536]{1,0:T(8,128)(2,1)} fusion(bf16[1536,1536]{0,1:T(8,128)(2,1)} %all-gather.11.cloned.1.call-done, f32[256,1536]{1,0:T(8,128)} %get-tuple-element.474, f32[1536]{0:T(1024)S(1)} %copy-done.49, f32[256]{0:T(256)S(1)} %add_rsqrt_fusion), kind=kOutput, calls=%fused_computation.65 | convolution fusion | flops 1209532416 | bytes 7085056 | tf_op jit(solution)/shard_map/dot_general | solution.py:233
  508.5 2.9 multiply_add_fusion
  511.5 1.2 copy-done.10
  513.6 1.8 reduce-scatter.2.cloned.1.call-done
  (311 shorter events, 29.5 us)
Async XLA Ops:
  7.2 6.1 %copy-start.20 = (bf16[256,1536]{1,0:T(8,128)(2,1)S(1)}, bf16[256,1536]{1,0:T(8,128)(2,1)}, u32[]{:S(2)}) copy-start(bf16[256,1536]{1,0:T(8,128)(2,1)} %param.26) | copy-start | bytes 2359300
  7.2 96.9 %all-gather.7.cloned.1.call-start = ((), (), s32[]{:S(2)}) async-start(), calls=%async_computation.3 | async-start | bytes 5013504 | tf_op jit(solution)/shard_map/all_gather | solution.py:163
  8.4 5.1 copy-start.27
  8.4 6.7 %copy-start.25 = (s32[32]{0:T(128)S(1)}, s32[32]{0:T(128)}, u32[]{:S(2)}) copy-start(s32[32]{0:T(128)} %param.30) | copy-start | bytes 388
  13.2 326.1 %all-gather.13.cloned.1.call-start = ((), (), s32[]{:S(2)}) async-start(), calls=%async_computation.7 | async-start | bytes 13369344 | tf_op jit(solution)/shard_map/all_gather | solution.py:23
  36.7 67.4 %copy-start.42 = (pred[1536]{0:T(1024)(128)(4,1)}, pred[1536]{0:T(1024)(128)(4,1)S(1)}, u32[]{:S(2)}) copy-start(pred[1536]{0:T(1024)(128)(4,1)S(1)} %get-tuple-element.420) | copy-start | bytes 4612
  41.5 62.6 %copy-start.21 = (bf16[1536,256]{1,0:T(8,128)(2,1)}, bf16[1536,256]{1,0:T(8,128)(2,1)S(1)}, u32[]{:S(2)}) copy-start(bf16[1536,256]{1,0:T(8,128)(2,1)S(1)} %gather_fusion) | copy-start | bytes 2359300
  91.7 2.2 copy-start.50
  91.7 2.5 copy-start.48
  91.7 2.6 copy-start.51
  91.7 2.6 copy-start.41
  91.7 2.7 copy-start.47
  91.7 3.5 copy-start.33
  91.7 5.1 copy-start.46
  92.6 4.1 collective-permute-start.1
  108.0 3.1 collective-permute-start
  114.6 5.3 %copy-start = (f32[4,24,64,128]{3,2,1,0:T(8,128)S(1)}, f32[4,24,64,128]{3,2,1,0:T(8,128)}, u32[]{:S(2)}) copy-start(f32[4,24,64,128]{3,2,1,0:T(8,128)} %param.42) | copy-start | bytes 9437188
  120.0 9.4 %copy-start.38 = (s32[2,128]{1,0:T(2,128)}, s32[2,128]{1,0:T(2,128)S(1)}, u32[]{:S(2)}) copy-start(s32[2,128]{1,0:T(2,128)S(1)} %get-tuple-element.700) | copy-start | bytes 3076 | tf_op jit(solution)/shard_map/while
  120.0 9.4 %copy-start.44 = (f32[2,128]{1,0:T(2,128)}, f32[2,128]{1,0:T(2,128)S(1)}, u32[]{:S(2)}) copy-start(f32[2,128]{1,0:T(2,128)S(1)} %get-tuple-element.705) | copy-start | bytes 3076 | tf_op jit(solution)/shard_map/while
  122.2 2.8 copy-start.12
  122.3 2.7 copy-start.14
  125.1 4.3 copy-start.16
  129.4 2.7 copy-start.26
  129.4 2.7 copy-start.7
  129.4 2.8 copy-start.15
  129.5 2.9 copy-start.17
  129.5 2.9 copy-start.19
  129.5 2.8 copy-start.52
  137.9 7.3 %copy-start.3 = (f32[2,24,64,128]{3,2,1,0:T(8,128)S(1)}, f32[2,24,64,128]{3,2,1,0:T(8,128)}, u32[]{:S(2)}) copy-start(f32[2,24,64,128]{3,2,1,0:T(8,128)} %get-tuple-element.676) | copy-start | bytes 4718596 | tf_op jit(solution)/shard_map/while
  137.9 7.3 %copy-start.8 = (f32[2,128,24,64]{1,3,2,0:T(8,128)S(1)}, f32[2,128,24,64]{1,3,2,0:T(8,128)}, u32[]{:S(2)}) copy-start(f32[2,128,24,64]{1,3,2,0:T(8,128)} %get-tuple-element.699) | copy-start | bytes 4718596 | tf_op jit(solution)/shard_map/while
  145.1 2.1 copy-start.29
  145.1 3.5 copy-start.35
  145.2 4.1 copy-start.39
  145.2 4.1 copy-start.45
  149.3 9.4 %copy-start.38 = (s32[2,128]{1,0:T(2,128)}, s32[2,128]{1,0:T(2,128)S(1)}, u32[]{:S(2)}) copy-start(s32[2,128]{1,0:T(2,128)S(1)} %get-tuple-element.700) | copy-start | bytes 3076 | tf_op jit(solution)/shard_map/while
  149.3 9.4 %copy-start.44 = (f32[2,128]{1,0:T(2,128)}, f32[2,128]{1,0:T(2,128)S(1)}, u32[]{:S(2)}) copy-start(f32[2,128]{1,0:T(2,128)S(1)} %get-tuple-element.705) | copy-start | bytes 3076 | tf_op jit(solution)/shard_map/while
  151.5 2.8 copy-start.12
  151.6 2.7 copy-start.14
  154.4 4.3 copy-start.16
  158.8 2.7 copy-start.26
  158.8 2.7 copy-start.7
  158.8 2.8 copy-start.15
  158.8 2.9 copy-start.17
  158.8 2.9 copy-start.19
  158.8 2.8 copy-start.52
  167.2 7.3 %copy-start.3 = (f32[2,24,64,128]{3,2,1,0:T(8,128)S(1)}, f32[2,24,64,128]{3,2,1,0:T(8,128)}, u32[]{:S(2)}) copy-start(f32[2,24,64,128]{3,2,1,0:T(8,128)} %get-tuple-element.676) | copy-start | bytes 4718596 | tf_op jit(solution)/shard_map/while
  167.2 7.3 %copy-start.8 = (f32[2,128,24,64]{1,3,2,0:T(8,128)S(1)}, f32[2,128,24,64]{1,3,2,0:T(8,128)}, u32[]{:S(2)}) copy-start(f32[2,128,24,64]{1,3,2,0:T(8,128)} %get-tuple-element.699) | copy-start | bytes 4718596 | tf_op jit(solution)/shard_map/while
  174.5 3.5 copy-start.35
  174.5 4.1 copy-start.39
  174.5 4.1 copy-start.45
  178.6 6.1 %copy-start.23 = (f32[48,3072]{1,0:T(8,128)S(1)}, f32[48,3072]{1,0:T(8,128)}, u32[]{:S(2)}) copy-start(f32[48,3072]{1,0:T(8,128)} %param.27) | copy-start | bytes 1769476
  183.8 5.8 %copy-start.24 = (f32[1536,96]{0,1:T(8,128)S(1)}, f32[1536,96]{0,1:T(8,128)}, u32[]{:S(2)}) copy-start(f32[1536,96]{0,1:T(8,128)} %param.39) | copy-start | bytes 1769476
  184.7 5.8 %copy-start.54 = (u32[32]{0:T(128)S(1)}, u32[32]{0:T(128)}, u32[]{:S(2)}) copy-start(u32[32]{0:T(128)} %constant.198) | copy-start | bytes 388
  184.7 236.1 %all-gather.9.cloned.1.call-start = ((), (), s32[]{:S(2)}) async-start(), calls=%async_computation.4 | async-start | bytes 5013504 | tf_op jit(solution)/shard_map/all_gather | solution.py:162
  189.6 313.6 %all-gather.11.cloned.1.call-start = ((), (), s32[]{:S(2)}) async-start(), calls=%async_computation.5 | async-start | bytes 5013504 | tf_op jit(solution)/shard_map/all_gather | solution.py:231
  190.4 325.1 %reduce-scatter.2.cloned.1.call-start = ((), (), s32[]{:S(2)}) async-start(), calls=%async_computation.6 | async-start | bytes 1179648 | tf_op jit(solution)/shard_map/reduce_scatter | solution.py:232
  339.3 21.7 %copy-start.9 = (f32[2,24,64,128]{3,2,1,0:T(8,128)S(1)}, f32[2,24,64,128]{3,2,1,0:T(8,128)}, u32[]{:S(2)}) copy-start(f32[2,24,64,128]{3,2,1,0:T(8,128)} %get-tuple-element.221) | copy-start | bytes 4718596
  339.3 21.7 %copy-start.13 = (f32[2,128,128]{1,0,2:T(2,128)S(1)}, f32[2,128,128]{1,0,2:T(2,128)}, u32[]{:S(2)}) copy-start(f32[2,128,128]{1,0,2:T(2,128)} %get-tuple-element.770) | copy-start | bytes 393220
  339.3 21.7 %copy-start.32 = (f32[2,128,24]{1,2,0:T(8,128)S(1)}, f32[2,128,24]{1,2,0:T(8,128)}, u32[]{:S(2)}) copy-start(f32[2,128,24]{1,2,0:T(8,128)} %get-tuple-element.218) | copy-start | bytes 73732
  368.3 52.5 %copy-start.22 = (bf16[1536,256]{1,0:T(8,128)(2,1)S(1)}, bf16[1536,256]{1,0:T(8,128)(2,1)}, u32[]{:S(2)}) copy-start(bf16[1536,256]{1,0:T(8,128)(2,1)} %copy-done.21) | copy-start | bytes 2359300
  368.3 52.5 %copy-start.43 = (pred[1536]{0:T(1024)(128)(4,1)S(1)}, pred[1536]{0:T(1024)(128)(4,1)}, u32[]{:S(2)}) copy-start(pred[1536]{0:T(1024)(128)(4,1)} %copy-done.42) | copy-start | bytes 4612
  371.2 132.0 %copy-start.49 = (f32[1536]{0:T(1024)S(1)}, f32[1536]{0:T(1024)}, u32[]{:S(2)}) copy-start(f32[1536]{0:T(1024)} %param.38) | copy-start | bytes 18436
  503.1 5.3 %copy-start.53 = (s32[2]{0:T(128)S(1)}, s32[2]{0:T(128)}, u32[]{:S(2)}) copy-start(s32[2]{0:T(128)} %param.43) | copy-start | bytes 28
  503.1 5.3 %copy-start.6 = (f32[2,24,64,128]{3,2,1,0:T(8,128)S(1)}, f32[2,24,64,128]{3,2,1,0:T(8,128)}, u32[]{:S(2)}) copy-start(f32[2,24,64,128]{3,2,1,0:T(8,128)} %get-tuple-element.769) | copy-start | bytes 4718596
  (22 other events, 32.3 us)
Sparse Core Ops, SparseCore 0:
  13.3 90.7 all-gather.6
  184.8 154.4 all-gather.12
  342.1 78.6 all-gather.8
  424.0 79.0 all-gather.10
  508.6 6.8 reduce-scatter.1
where the time goes:
time: 524 us; the launch traced here: 522 us
  waiting for transfers between devices  237 us (45%)
  blocking collectives  106 us (20%)
  other arithmetic  67 us (13%)
  matrix products  50.9 us (10%)
  local copies, waits for them, and re-layouts  42.1 us (8%)
  between operations  15 us (3%)
    all_gather x1, waiting for transfers between devices, entering(): everything = jax.tree.map(lambda part: lax.all_gather(part, axis), array)  104 us
    all_gather x1, waiting for transfers between devices, on_device(): lax.all_gather(out_proj.astype(jnp.bfloat16), 'seq', axis=1, tiled=True)  74.7 us
    all_gather x1, blocking collectives, on_device(): lax.all_gather(small_proj.astype(jnp.bfloat16), ('seq', 'tp'), axis=0, ti...  50.2 us
    all_gather x1, waiting for transfers between devices, on_device(): lax.all_gather(gate_blocks, 'seq', axis=0, tiled=True)  49.6 us
    unnamed x1, blocking collectives  43.5 us
    select_n x16, other arithmetic, hop(): return jax.tree.map(lambda a, b: jnp.where(reached, a, b), new, before)  21 us
    and x1, other arithmetic, fold_rows(): columns = jnp.take(hidden_in, logical, axis=1)  15.6 us
    dot_general x2, matrix products, span_terms(): jnp.einsum('g,ghpn->hpn', group_span[length - 1], init_states, precision=...  14.4 us
  transfers between devices with their start and end apart: 7, of which 6 were waited for; matrix products, arithmetic and copies ran while one was open for 14% of the time, Pallas kernels for 0%

commit v1 on v0

v1 whole, which is shorter than its diff:
```python
import functools

import jax
import jax.numpy as jnp
from jax import lax
from jax.experimental import pallas as pl
from jax.experimental.pallas import tpu as pltpu
from jax.sharding import Mesh
from jax.sharding import PartitionSpec as P

N = 128
CONV = 4
PAGE = 128
HALO = 32
TILE = 16
LANES = 128
EPSILON = 1e-05
F32 = jnp.float32
BF16 = jnp.bfloat16
HIGHEST = lax.Precision.HIGHEST
GROUP = ("a", "b", "tp")
SEQ = ("t", "a", "y", "b")
VMEM = pl.BlockSpec(memory_space=pltpu.VMEM)
SMEM = pl.BlockSpec(memory_space=pltpu.SMEM)


def call(body, name, out_shape, ins, scratch=(), limit=40):
    specs = [SMEM if x.dtype == jnp.int32 else VMEM for x in ins]
    return pl.pallas_call(
        body,
        name=name,
        out_shape=out_shape,
        in_specs=specs,
        out_specs=jax.tree.map(lambda _: VMEM, out_shape),
        scratch_shapes=list(scratch),
        compiler_params=pltpu.CompilerParams(vmem_limit_bytes=limit << 20),
    )(*ins)


def shape(dims, dtype):
    return jax.ShapeDtypeStruct(dims, dtype)


def dot(x, y, dims=((1,), (0,)), precision=None):
    return lax.dot_general(x, y, (dims, ((), ())), precision=precision, preferred_element_type=F32)


NT = ((1,), (1,))
TN = ((0,), (0,))


def swap(x, axis):
    return lax.ppermute(x, axis, [(0, 1), (1, 0)])


def stored_block(s, dy, place, info):
    t, y, count = info[3], info[4], info[5]
    a, b, c = place // 4, (place // 2) % 2, place % 2
    source = lax.rem(t - s + count, count)
    seq = ((source * 2 + a) * 2 + (y ^ dy)) * 2 + b
    return seq * 2 + c


def pieces_of(hidden, info):
    own, mine_b, mine_a, mine_d, other_b, other_a, other_d = hidden
    me, c = info[0], info[1]
    half = own.shape[0] // 2
    yield me * 2, lambda: own[:half]
    yield me * 2 + 1, lambda: own[half:]
    for rel, mine, other in ((1, mine_b, other_b), (2, mine_a, other_a), (3, mine_d, other_d)):
        yield (me ^ rel) * 2 + c, lambda mine=mine: mine[...]
        yield (me ^ rel) * 2 + 1 - c, lambda other=other: other[...]


def inner_kernel(count, rows, *refs):
    info, layout = refs[0], refs[1]
    hidden = refs[2:9]
    parts = refs[9 : 9 + count]
    raw_ref, shared_ref, step_ref, weights = refs[9 + count :]
    width = parts[0].shape[1]
    if rows % TILE == 0 and count > 1:
        lane = lax.broadcasted_iota(jnp.int32, (TILE, LANES), 1) // TILE
        for index in range(count):
            part = parts[index]
            for place in range(8):
                block = layout[stored_block(index // 2, index % 2, place, info)]
                at = pl.multiple_of(block * rows, TILE)
                weights[pl.ds(at, rows), :width] = part[place * rows : (place + 1) * rows, :]
                for piece in range(rows // TILE):
                    packed = part[8 * rows : 8 * rows + TILE, piece * LANES : (piece + 1) * LANES]
                    kept = jnp.where(lane == place, packed, jnp.zeros_like(packed))
                    at2 = pl.multiple_of(block * rows + piece * TILE, TILE)
                    weights[pl.ds(at2, TILE), width:] = kept
        w = weights
    else:
        w = parts[0]
    bc = raw_ref.shape[2]
    for index, rows_of in pieces_of(hidden, info):
        result = dot(rows_of(), w[...])
        raw_ref[index] = result[:, :bc].astype(BF16)
        shared_ref[index] = result[:, bc : bc + LANES].astype(BF16)
        step = result[:, bc + LANES :]
        for shift in (64, 32, 16):
            step = step + pltpu.roll(step, shift, 1)
        step_ref[index] = step


def gate_kernel(count, rows, *refs):
    info, layout = refs[0], refs[1]
    hidden = refs[2:9]
    parts = refs[9 : 9 + count]
    gate_ref, weights = refs[9 + count :]
    if rows % TILE == 0 and count > 1:
        for index in range(count):
            for place in range(8):
                block = layout[stored_block(index // 2, index % 2, place, info)]
                at = pl.multiple_of(block * rows, TILE)
                weights[pl.ds(at, rows), :] = parts[index][place * rows : (place + 1) * rows, :]
        w = weights
    else:
        w = parts[0]
    for index, rows_of in pieces_of(hidden, info):
        result = dot(rows_of(), w[...])
        gate_ref[index] = jax.nn.silu(result).astype(BF16)


def chunk_start(i, info, tokens):
    t, y = info[3], info[4]
    per = tokens // PAGE
    q = i // per
    seq = ((t * 2 + q // 2) * 2 + y) * 2 + q % 2
    return seq * tokens + (i % per) * PAGE


def last_start(position, starts):
    best = jnp.int32(0)
    for k in range(starts.shape[0]):
        best = jnp.maximum(best, jnp.where(starts[k] <= position, starts[k], 0))
    return best


def first_positions(first, starts, dims):
    position = first + lax.broadcasted_iota(jnp.int32, dims, 0)
    best = jnp.zeros(dims, jnp.int32)
    for k in range(starts.shape[0]):
        best = jnp.maximum(best, jnp.where(starts[k] <= position, starts[k], 0))
    return best


def conv_silu(window, taps, bias, offset):
    total = bias + taps[0:1, :] * window[TILE : TILE + PAGE]
    for lag in range(1, CONV):
        within = (offset >= lag).astype(F32)
        total = total + taps[lag : lag + 1, :] * window[TILE - lag : TILE - lag + PAGE] * within
    return total / (1.0 + jnp.exp(-total))


def pair_columns(values, pair):
    lane = lax.broadcasted_iota(jnp.int32, (PAGE, LANES), 1)
    left = values[:, 2 * pair : 2 * pair + 1]
    right = values[:, 2 * pair + 1 : 2 * pair + 2]
    return jnp.where(lane < 64, left, right)


def state_kernel(heads, tokens, info, starts, groups, raw, own, other, step, taps, bias, taps2,
                 bias2, dt_bias, decay, init, x_ref, b_ref, c_ref, cum_ref, dt_ref, end_ref,
                 factor_ref, summary_ref, state, factor):
    chunks = x_ref.shape[0]
    per_run = chunks // 2
    per = tokens // PAGE
    pairs = heads // 2
    rate = -jnp.exp(decay[...])
    row = lax.broadcasted_iota(jnp.int32, (PAGE, PAGE), 0)
    col = lax.broadcasted_iota(jnp.int32, (PAGE, PAGE), 1)
    below = (row >= col).astype(F32)

    def one(i, carry):
        @pl.when(i % per_run == 0)
        def _():
            state[...] = jnp.zeros_like(state)
            factor[...] = jnp.ones_like(factor)

        first = chunk_start(i, info, tokens)
        opened = last_start(first + PAGE - 1, starts)
        alive = (opened < first).astype(F32)
        start_of = first_positions(first, starts, (PAGE, 1))
        offset = first + lax.broadcasted_iota(jnp.int32, (PAGE, 1), 0) - start_of
        q = i // per
        at = pl.multiple_of(HALO - TILE + (i % per) * PAGE, TILE)
        window = pl.ds(at, PAGE + TILE)
        x = conv_silu(raw[q, window, :].astype(F32), taps, bias[...], offset)
        is_first = info[1] == 0
        mine, theirs = own[q, window, :].astype(F32), other[q, window, :].astype(F32)
        b_raw = jnp.where(is_first, mine, theirs)
        c_raw = jnp.where(is_first, theirs, mine)
        b = conv_silu(b_raw, taps2[:, :LANES], bias2[:, :LANES], offset).astype(BF16)
        c = conv_silu(c_raw, taps2[:, LANES:], bias2[:, LANES:], offset).astype(BF16)
        raw_step = step[q, pl.ds(pl.multiple_of(HALO + (i % per) * PAGE, TILE), PAGE), :]
        v = raw_step + dt_bias[...]
        dt = jnp.maximum(v, 0.0) + jnp.log1p(jnp.exp(-jnp.abs(v)))
        log_rate = rate * dt
        cum = dot(below, log_rate, precision=HIGHEST)
        last = cum[PAGE - 1 : PAGE, :]
        kept = (row >= opened - first).astype(F32)
        weight = jnp.exp(last - cum) * dt * kept
        cum_t = cum.T
        x_ref[i] = x.astype(BF16)
        b_ref[i] = b
        c_ref[i] = c
        cum_ref[i] = cum
        dt_ref[i] = dt
        whole = jnp.broadcast_to(jnp.exp(cum_t[0:8, PAGE - 1 : PAGE]), (8, LANES)) * alive
        for pair in range(pairs):
            scaled = (x[:, pair * LANES : (pair + 1) * LANES] * pair_columns(weight, pair)).astype(BF16)
            added = dot(scaled, b, TN)
            for k in (0, 1):
                h = 2 * pair + k
                here = slice(h * 64, (h + 1) * 64)
                state[here, :] = state[here, :] * whole[h : h + 1, :] + added[k * 64 : (k + 1) * 64, :]
        for k in range(starts.shape[0]):
            start = starts[k]

            @pl.when((start >= first) & (start == opened))
            def _():
                before = jnp.sum(jnp.where(col == start - first - 1, cum_t, 0.0), axis=1, keepdims=True)
                opening = jnp.exp(cum_t[0:8, PAGE - 1 : PAGE] - before[0:8])
                opening = jnp.broadcast_to(opening, (8, LANES))
                for h in range(heads):
                    here = slice(h * 64, (h + 1) * 64)
                    state[here, :] = state[here, :] + opening[h : h + 1, :] * init[groups[k], here, :]

        factor[...] = factor[...] * whole
        end_ref[i] = state[...]
        factor_ref[i] = factor[...]

        @pl.when(i % per_run == per_run - 1)
        def _():
            summary_ref[i // per_run, : heads * 64, :] = state[...].astype(BF16)
            tail = jnp.concatenate([factor[...], jnp.zeros_like(factor[...])], axis=0)
            summary_ref[i // per_run, heads * 64 :, :] = tail.astype(BF16)

        return carry

    lax.fori_loop(0, chunks, one, 0)


def within_kernel(heads, tokens, info, starts, groups, x_ref, b_ref, c_ref, cum_ref, dt_ref, skip,
                  init, y_ref):
    chunks = x_ref.shape[0]
    pairs = heads // 2
    row = lax.broadcasted_iota(jnp.int32, (PAGE, PAGE), 0)
    col = lax.broadcasted_iota(jnp.int32, (PAGE, PAGE), 1)
    lane = lax.broadcasted_iota(jnp.int32, (PAGE, LANES), 1)

    def one(i, carry):
        first = chunk_start(i, info, tokens)
        start_of = first_positions(first, starts, (PAGE, PAGE))
        bias = jnp.where((row >= col) & (col >= start_of - first), 0.0, -1e30)
        b, c = b_ref[i], c_ref[i]
        cum, dt = cum_ref[i], dt_ref[i]
        cum_t = cum.T
        scores = dot(c, b, NT)
        for pair in range(pairs):
            here = slice(pair * LANES, (pair + 1) * LANES)
            x = x_ref[i, :, here].astype(F32)
            scaled = x * pair_columns(dt, pair)
            mixing = []
            for h in (2 * pair, 2 * pair + 1):
                gap = cum[:, h : h + 1] + bias - cum_t[h : h + 1, :]
                mixing.append((scores * jnp.exp(gap)).astype(BF16))
            both = jnp.concatenate(
                [jnp.where(lane < 64, scaled, 0.0), jnp.where(lane < 64, 0.0, scaled)], axis=0
            ).astype(BF16)
            y = dot(jnp.concatenate(mixing, axis=1), both)
            y_ref[i, :, here] = y + skip[:, here] * x
        for k in range(starts.shape[0]):
            start = starts[k]

            @pl.when((start >= first) & (start < first + PAGE))
            def _():
                before = jnp.sum(jnp.where(row == start - first - 1, cum, 0.0), axis=0, keepdims=True)
                opening = jnp.exp(jnp.minimum(cum - before, 0.0))
                opening = jnp.where(start_of == start, opening, 0.0)
                for pair in range(pairs):
                    here = slice(pair * LANES, (pair + 1) * LANES)
                    read = dot(c, init[groups[k], here, :].astype(BF16), NT)
                    y_ref[i, :, here] = y_ref[i, :, here] + pair_columns(opening, pair) * read

        return carry

    lax.fori_loop(0, chunks, one, 0)


def onto(run, h, before):
    here = slice(h * 64, (h + 1) * 64)
    decay = run[run.shape[0] - 16 + h : run.shape[0] - 16 + h + 1, :].astype(F32)
    return decay * before + run[here, :].astype(F32)


def compose_kernel(heads, info, mine, theirs, block_ref):
    low = info[4] == 0
    runs = []
    for a in range(2):
        m, q = mine[a].astype(F32), theirs[a].astype(F32)
        runs += [jnp.where(low, m, q), jnp.where(low, q, m)]
    total = runs[0]
    for run in runs[1:]:
        parts = []
        for h in range(heads):
            parts.append(onto(run, h, total[h * 64 : (h + 1) * 64, :]))
        tail = total[heads * 64 :, :] * run[heads * 64 :, :]
        total = jnp.concatenate(parts + [tail], axis=0)
    block_ref[...] = total.astype(BF16)


def finish_kernel(heads, tokens, info, starts, mine, theirs, entering, c_ref, cum_ref, end_ref,
                  factor_ref, y_ref, gate, gain, mixed_ref, square_ref, page_ref, starting, state):
    chunks = c_ref.shape[0]
    per = tokens // PAGE
    per_run = chunks // 2
    pairs = heads // 2
    me, y = info[0], info[4]
    for h in range(heads):
        here = slice(h * 64, (h + 1) * 64)
        outside = entering[here, :].astype(F32)
        first = jnp.where(y == 0, outside, onto(theirs[0], h, outside))
        starting[0, here, :] = first
        second = onto(mine[0], h, first)
        third = jnp.where(y == 0, onto(theirs[0], h, second), onto(theirs[1], h, second))
        starting[1, here, :] = third
    ones = jnp.ones((8, LANES), F32)

    def one(i, carry):
        run = i // per_run

        @pl.when(i % per_run == 0)
        def _():
            state[...] = starting[run]

        q = i // per
        first = chunk_start(i, info, tokens)
        alive = (first_positions(first, starts, (PAGE, LANES)) < first).astype(F32)
        decay = jnp.exp(cum_ref[i]) * alive
        read = dot(c_ref[i], state[...].astype(BF16), NT)
        rows = pl.ds(pl.multiple_of(HALO + (i % per) * PAGE, TILE), PAGE)
        squares = jnp.zeros((PAGE, LANES), F32)
        for pair in range(pairs):
            here = slice(pair * LANES, (pair + 1) * LANES)
            value = y_ref[i, :, here] + pair_columns(decay, pair) * read[:, here]
            value = value * gate[q, rows, here].astype(F32)
            mixed_ref[i, :, here] = (value * gain[:, here]).astype(BF16)
            squares = squares + value * value
        square_ref[i] = dot(ones, squares, NT, HIGHEST)
        for h in range(heads):
            here = slice(h * 64, (h + 1) * 64)
            after = end_ref[i, here, :] + factor_ref[i, h : h + 1, :] * starting[run, here, :]
            state[here, :] = after
        page_ref[q ^ me, i % per] = state[...].astype(BF16)
        return carry

    lax.fori_loop(0, chunks, one, 0)


def columns_kernel(count, rows, *refs):
    info = refs[0]
    parts = refs[1 : 1 + count]
    out = refs[1 + count]
    for index in range(count):
        for place in range(4):
            seq = stored_block(index // 2, index % 2, 2 * place, info) // 2
            at = pl.multiple_of(seq * rows, TILE)
            out[pl.ds(at, rows), :] = parts[index][place * rows : (place + 1) * rows, :]


def mix_kernel(keep, info, mixed, columns, out):
    me, c = info[0], info[1]
    half = c if keep else 1 - c
    for rel in range(4):
        out[rel] = dot(mixed[(me ^ rel) * 2 + half], columns[...], NT).astype(BF16)


def page_kernel(info, table, own, from_b, from_a, from_d, out):
    me, seq, per = info[0], info[6], own.shape[0]
    for k in range(per):
        slot = table[k] - seq * per
        for rel, source in enumerate((own, from_b, from_a, from_d)):
            out[slot, me ^ rel] = source[k].astype(F32)


def weight_parts(part, count):
    parts = []
    for s in range(count):
        if s > 0:
            part = lax.ppermute(part, "t", [(i, (i + 1) % count) for i in range(count)])
        parts += [part, swap(part, "y")]
    return parts


def in_order(parts, index):
    stacked = jnp.stack(parts)
    blocks = stacked.reshape((-1, stacked.shape[1] * len(parts) // index.shape[0], stacked.shape[2]))
    return jnp.zeros_like(blocks).at[index].set(blocks).reshape(-1, stacked.shape[2])


def on_device(
    hidden_in,
    gate_proj,
    inner_proj,
    small_proj,
    row_layout,
    conv_inner,
    conv_shared,
    bias_inner,
    bias_shared,
    dt_bias,
    decay_log,
    skip_gain,
    norm_gain,
    out_proj,
    prompt_lengths,
    group_map,
    init_states,
    page_table,
):
    tokens, model = hidden_in.shape
    rows = gate_proj.shape[0]
    half_heads = dt_bias.shape[0]
    heads = half_heads // 4
    inner = conv_inner.shape[1]
    head_dim = inner // half_heads
    width = heads * head_dim
    t_count = lax.axis_size("t")
    t, a, y, b, c = (lax.axis_index(name) for name in ("t", "a", "y", "b", "tp"))
    me = a * 2 + b
    seq = ((t * 2 + a) * 2 + y) * 2 + b
    info = jnp.stack([me, c, 0 * c, t, y, 0 * c + t_count, seq, 0 * c]).astype(jnp.int32)
    starts = (jnp.cumsum(prompt_lengths) - prompt_lengths).astype(jnp.int32)
    count = 2 * t_count

    inner_send = inner_proj.astype(BF16).reshape(rows, 2, 4, width).transpose(2, 1, 0, 3)
    small = small_proj.astype(BF16)
    shared_send = small[:, : 2 * N].reshape(rows, 2, N).transpose(1, 0, 2)
    shared_send = jnp.broadcast_to(shared_send[None], (4, 2, rows, N))
    step_send = small[:, 2 * N :].reshape(rows, 2, 4, heads).transpose(2, 1, 0, 3)
    step_send = jnp.pad(step_send, ((0, 0), (0, 0), (0, 0), (0, LANES - heads)))
    inner_send = jnp.concatenate([inner_send, shared_send, step_send], axis=-1)
    inner_send = inner_send.reshape(8, rows, width + N + LANES)
    inner_got = lax.all_to_all(inner_send, GROUP, 0, 0, tiled=True)
    gate_send = gate_proj.astype(BF16).reshape(rows, 2, 4, width).transpose(2, 1, 0, 3)
    gate_got = lax.all_to_all(gate_send.reshape(8, rows, width), GROUP, 0, 0, tiled=True)
    out_send = out_proj.T.astype(BF16).reshape(out_proj.shape[1], 4, width).transpose(1, 0, 2)
    out_got = lax.all_to_all(out_send, ("a", "b"), 0, 0, tiled=True)

    wide = width + N + LANES
    if rows % TILE == 0:
        packed = inner_got[:, :, width + N : width + N + 16].reshape(8, rows // TILE, TILE, 16)
        packed = packed.transpose(2, 1, 0, 3).reshape(TILE, rows // TILE * LANES)
        packed = jnp.pad(packed, ((0, 0), (0, width + N - packed.shape[1])))
        inner_part = jnp.concatenate([inner_got[:, :, : width + N].reshape(8 * rows, -1), packed])
    else:
        inner_part = inner_got.reshape(8 * rows, wide)
    inner_parts = weight_parts(inner_part, t_count)
    gate_parts = weight_parts(gate_got.reshape(8 * rows, width), t_count)
    out_rows = out_proj.shape[1]
    out_parts = weight_parts(out_got.reshape(4 * out_rows, width), t_count)
    if rows % TILE != 0:
        index = [stored_block(s, dy, p, info) for s in range(t_count) for dy in (0, 1) for p in range(8)]
        index = row_layout[jnp.stack(index)]
        inner_parts = [in_order(inner_parts, index)]
        gate_parts = [in_order(gate_parts, index)]
    if out_rows % TILE != 0:
        index = [
            stored_block(s, dy, 2 * p, info) // 2
            for s in range(t_count)
            for dy in (0, 1)
            for p in range(4)
        ]
        columns = in_order(out_parts, jnp.stack(index))
    else:
        columns = call(
            functools.partial(columns_kernel, count, out_rows),
            "columns",
            shape((model, width), BF16),
            [info, *out_parts],
        )

    size = lax.axis_size(SEQ)
    halo = lax.ppermute(hidden_in[tokens - HALO :], SEQ, [(i, i + 1) for i in range(size - 1)])
    own = jnp.concatenate([halo, hidden_in], axis=0)
    half = own.shape[0] // 2
    mine = lax.dynamic_slice_in_dim(own, c * half, half, 0)
    mine_b, mine_a = swap(mine, "b"), swap(mine, "a")
    cut = -(-half // (2 * TILE)) * TILE
    mine_d = jnp.concatenate([swap(mine_a[:cut], "b"), swap(mine_b[cut:], "a")], axis=0)
    hidden = [own, mine_b, mine_a, mine_d, swap(mine_b, "tp"), swap(mine_a, "tp"), swap(mine_d, "tp")]

    raw, shared, step = call(
        functools.partial(inner_kernel, len(inner_parts), rows),
        "inner_projection",
        (
            shape((8, half, width), BF16),
            shape((8, half, LANES), BF16),
            shape((8, half, LANES), F32),
        ),
        [info, row_layout, *hidden, *inner_parts],
        [pltpu.VMEM((model, wide), BF16)],
    )
    shared_other = swap(shared, "tp")
    gate = call(
        functools.partial(gate_kernel, len(gate_parts), rows),
        "gate_projection",
        shape((8, half, width), BF16),
        [info, row_layout, *hidden, *gate_parts],
        [pltpu.VMEM((model, width), BF16)],
    )

    def whole(x):
        return x.reshape(4, 2 * half, x.shape[2])

    def lanes_of(x):
        mine = lax.dynamic_slice_in_dim(x, me * heads, heads, 0)
        return jnp.pad(mine, (0, LANES - heads))[None]

    taps = lax.dynamic_slice_in_dim(conv_inner, me * width, width, 1)
    bias = lax.dynamic_slice_in_dim(bias_inner, me * width, width, 0)[None]
    gain = lax.dynamic_slice_in_dim(norm_gain, me * width, width, 0)[None]
    skip = jnp.repeat(lax.dynamic_slice_in_dim(skip_gain, me * heads, heads, 0), head_dim)[None]
    init = lax.dynamic_slice_in_dim(init_states, me * heads, heads, 1)
    init = init.reshape(init.shape[0], width, N)
    chunks = 4 * tokens // PAGE
    x, b_in, c_in, cum, dt, ends, factors, summary = call(
        functools.partial(state_kernel, heads, tokens),
        "states",
        (
            shape((chunks, PAGE, width), BF16),
            shape((chunks, PAGE, N), BF16),
            shape((chunks, PAGE, N), BF16),
            shape((chunks, PAGE, LANES), F32),
            shape((chunks, PAGE, LANES), F32),
            shape((chunks, width, N), F32),
            shape((chunks, 8, N), F32),
            shape((2, width + 16, N), BF16),
        ),
        [info, starts, group_map, whole(raw), whole(shared), whole(shared_other), whole(step), taps,
         bias, conv_shared, bias_shared[None], lanes_of(dt_bias), lanes_of(decay_log), init],
        [pltpu.VMEM((width, N), F32), pltpu.VMEM((8, N), F32)],
    )
    theirs = swap(summary, "y")
    block = call(
        functools.partial(compose_kernel, heads),
        "compose",
        shape((width + 16, N), BF16),
        [info, summary, theirs],
    )
    onward = [(i, i + 1) for i in range(t_count - 1)]
    block = lax.ppermute(block, "t", onward)
    entering = block[:width]
    if t_count > 2:
        total = entering.astype(F32).reshape(heads, head_dim, N)
        decay = block[width : width + heads, None, :].astype(F32)
        for _ in range(t_count - 2):
            block = lax.ppermute(block, "t", onward)
            total = total + decay * block[:width].astype(F32).reshape(heads, head_dim, N)
            decay = decay * block[width : width + heads, None, :].astype(F32)
        entering = total.reshape(width, N)
    y_within = call(
        functools.partial(within_kernel, heads, tokens),
        "within_chunks",
        shape((chunks, PAGE, width), F32),
        [info, starts, group_map, x, b_in, c_in, cum, dt, skip, init],
    )
    mixed, squares, pages = call(
        functools.partial(finish_kernel, heads, tokens),
        "finish",
        (
            shape((chunks, PAGE, width), BF16),
            shape((chunks, 8, PAGE), F32),
            shape((4, tokens // PAGE, width, N), BF16),
        ),
        [info, starts, summary, theirs, entering, c_in, cum, ends, factors, y_within, whole(gate), gain],
        [pltpu.VMEM((2, width, N), F32), pltpu.VMEM((width, N), F32)],
    )

    across = [(i, i ^ 3) for i in range(4)]
    got = [pages[0], swap(pages[1], "b"), swap(pages[2], "a"), lax.ppermute(pages[3], ("a", "b"), across)]
    per = tokens // PAGE
    state_pages = call(
        page_kernel, "pages", shape((per, 4, width, N), F32), [info, page_table, *got]
    ).reshape(per, half_heads, head_dim, N)

    sent = call(functools.partial(mix_kernel, False), "mix_send", shape((4, PAGE, model), BF16),
                [info, mixed, columns])
    sent = swap(sent, "tp")
    kept = call(functools.partial(mix_kernel, True), "mix_keep", shape((4, PAGE, model), BF16),
                [info, mixed, columns])
    squares = lax.psum(squares[:, 0, :], GROUP)
    mid = model // 2
    total = kept.astype(F32) + sent.astype(F32)
    left, right = total[..., :mid], total[..., mid:]
    left_in = swap(jnp.stack([left[1], left[3]]).astype(BF16), "b")
    right_in = swap(right[2:4].astype(BF16), "a")
    left = jnp.stack([left[0], left[2]]) + left_in.astype(F32)
    right = right[0:2] + right_in.astype(F32)
    left_in = swap(left[1].astype(BF16), "a")
    right_in = swap(right[1].astype(BF16), "b")
    left = left[0] + left_in.astype(F32)
    right = right[0] + right_in.astype(F32)
    mine_squares = lax.dynamic_index_in_dim(squares, me * 2 + c, 0, keepdims=False)
    scale = lax.rsqrt(mine_squares / (2 * inner) + EPSILON)[:, None]
    mixed_out = (jnp.concatenate([left, right], axis=1) * scale).astype(BF16)
    return (mixed_out, state_pages)


def solution(mesh):
    count = mesh.shape["seq"]
    fine = Mesh(mesh.devices.reshape(count // 8, 2, 2, 2, 2), SEQ + ("tp",))
    placed = (
        P(SEQ, None),
        P(SEQ + ("tp",), None),
        P(SEQ + ("tp",), None),
        P(SEQ + ("tp",), None),
        P(),
        P(None, "tp"),
        P(),
        P("tp"),
        P(),
        P("tp"),
        P("tp"),
        P("tp"),
        P("tp"),
        P("tp", SEQ),
        P(),
        P(),
        P(None, "tp", None, None),
        P(SEQ),
    )
    return jax.shard_map(
        on_device,
        mesh=fine,
        in_specs=placed,
        out_specs=(P(SEQ + ("tp",), None), P(SEQ, "tp", None, None)),
        check_vma=False,
    )
```

time: 524 us -> 218 us (0.42)
  waiting for transfers between devices: 237 us -> 55.3 us
  blocking collectives: 106 us -> 17.3 us
  other arithmetic: 67 us -> 11.1 us
  matrix products: 50.9 us -> 0 us
  starting transfers between devices: 3.19 us -> 50 us
  Pallas kernels: 0 us -> 36.6 us
  between operations: 15 us -> 1.32 us
    all_gather x4 -> x0, waiting for transfers between devices: 235 us -> none  [the longest x1 104 us: entering(): everything = jax.tree.map(lambda part: lax.all_gather(part, axis), array)]
    ppermute x2 -> x28, waiting for transfers between devices: 0.53 us -> 55.3 us  [the longest x22 45.7 us: swap(): return lax.ppermute(x, axis, [(0, 1), (1, 0)])]
    dot_general x15 -> x0, matrix products: 50.9 us -> none  [the longest x2 14.4 us: span_terms(): jnp.einsum('g,ghpn->hpn', group_span[length - 1], init_states, precision=...]
    all_gather x1 -> x0, blocking collectives: 50.2 us -> none  [on_device(): lax.all_gather(small_proj.astype(jnp.bfloat16), ('seq', 'tp'), axis=0, ti...]
    unnamed x1 -> x0, blocking collectives: 43.5 us -> none
    pallas_call x0 -> x10, Pallas kernels: none -> 36.6 us  [call(): pl.pallas_call(body, name=name, out_shape=out_shape, in_specs=specs, out_...]
    ppermute x2 -> x28, starting transfers between devices: 2.98 us -> 37.8 us  [the longest x22 23 us: swap(): return lax.ppermute(x, axis, [(0, 1), (1, 0)])]
    select_n x20 -> x0, other arithmetic: 26.4 us -> none  [the longest x16 21 us: hop(): return jax.tree.map(lambda a, b: jnp.where(reached, a, b), new, before)]
  transfers between devices with their start and end apart: 7 -> 31, of which waited for: 6 -> 11; matrix products, arithmetic and copies ran while one was open for 14% -> 18% of each run, Pallas kernels for 0% -> 14%
where the time goes in v1:
time: 218 us; the launch traced here: 216 us
  waiting for transfers between devices  55.3 us (25%)
  starting transfers between devices  50 us (23%)
  local copies, waits for them, and re-layouts  44 us (20%)
  Pallas kernels  36.6 us (17%)
  blocking collectives  17.3 us (8%)
  other arithmetic  11.1 us (5%)
    ppermute x22, waiting for transfers between devices, swap(): return lax.ppermute(x, axis, [(0, 1), (1, 0)])  45.7 us
    pallas_call x10, Pallas kernels, call(): pl.pallas_call(body, name=name, out_shape=out_shape, in_specs=specs, out_...  36.6 us
    ppermute x22, starting transfers between devices, swap(): return lax.ppermute(x, axis, [(0, 1), (1, 0)])  23 us
    psum x1, blocking collectives, on_device(): squares = lax.psum(squares[:, 0, :], GROUP)  17.3 us
    unnamed x97, local copies, waits for them, and re-layouts  15.3 us
    ppermute x3, waiting for transfers between devices, weight_parts(): part = lax.ppermute(part, 't', [(i, (i + 1) % count) for i in range(count)])  9.52 us
    ppermute x1, starting transfers between devices, on_device(): lax.ppermute(hidden_in[tokens - HALO:], SEQ, [(i, i + 1) for i in range(s...  5.47 us
    ppermute x3, starting transfers between devices, weight_parts(): part = lax.ppermute(part, 't', [(i, (i + 1) % count) for i in range(count)])  5 us
  transfers between devices with their start and end apart: 31, of which 11 were waited for; matrix products, arithmetic and copies ran while one was open for 18% of the time, Pallas kernels for 14%

profile of v1, /device:TPU:0, one launch (start us, length us, event | category | flops | bytes accessed | tf_op | source)
XLA Modules:
  0.0 215.7 jit_solution(4525137607214794861)
XLA Ops:
  0.6 1.7 slice.82
  2.3 5.5 %collective-permute-start = (bf16[32,1536]{1,0:T(8,128)(2,1)}, bf16[32,1536]{1,0:T(8,128)(2,1)}, u32[]{:S(2)}, u32[]{:S(2)}) collective-permute-start(bf16[32,1536]{1,0:T(8,128)(2,1)} %slice.82), channel_id=1, source_target_pairs={{0,2},{2,4},{4,6},{6,8},{8,10},{10,12},{12,14},{14,16},{16,18},{18... | collective-permute-start | bytes 294920 | tf_op jit(solution)/shard_map/ppermute | solution.py:488
  9.6 1.1 convert_element_type.53
  11.6 1.0 copy.44
  14.2 4.1 %all-to-all-start = ((bf16[8,48,640]{2,1,0:T(8,128)(2,1)}), bf16[8,48,640]{2,1,0:T(8,128)(2,1)}, u32[]{:S(2)}, u32[]{:S(2)}) async-start(bf16[8,48,640]{2,1,0:T(8,128)(2,1)} %bitcast.76), calls=%async_computation | async-start | bytes 983040 | tf_op jit(solution)/shard_map/all_to_all | solution.py:448
  18.4 1.0 constant_dynamic-update-slice_fusion.1
  19.4 1.2 constant_dynamic-update-slice_fusion.refs_2_
  22.3 1.9 collective-permute-start.2
  24.2 1.5 collective-permute-start.1
  25.7 10.6 %collective-permute-done.2.refs_4_ = bf16[144,1536]{1,0:T(8,128)(2,1)S(1)} collective-permute-done((bf16[144,1536]{1,0:T(8,128)(2,1)}, bf16[144,1536]{1,0:T(8,128)(2,1)S(1)}, u32[]{:S(2)}, u32[]{:S(2)}) %collective-permute-start.2) | collective-permute-done | bytes 442400 | tf_op jit(solution)/shard_map/ppermute | solution.py:53
  37.7 1.5 collective-permute-start.3
  40.0 4.1 %all-to-all-start.2 = ((bf16[4,96,384]{2,1,0:T(8,128)(2,1)}), bf16[4,96,384]{2,1,0:T(8,128)(2,1)}, u32[]{:S(2)}, u32[]{:S(2)}) async-start(bf16[4,96,384]{2,1,0:T(8,128)(2,1)} %bitcast.66), calls=%async_computation.2 | async-start | bytes 589824 | tf_op jit(solution)/shard_map/all_to_all | solution.py:452
  44.1 1.1 convert_element_type.55
  46.1 1.7 copy.36
  47.8 1.6 slice.106
  49.4 2.0 collective-permute-start.4
  53.8 1.0 slice.109
  55.6 2.0 collective-permute-start.9
  57.6 1.7 constant_dynamic-update-slice_fusion.3
  59.3 4.1 %all-to-all-start.1 = ((bf16[8,48,384]{2,1,0:T(8,128)(2,1)}), bf16[8,48,384]{2,1,0:T(8,128)(2,1)}, u32[]{:S(2)}, u32[]{:S(2)}) async-start(bf16[8,48,384]{2,1,0:T(8,128)(2,1)} %bitcast.80), calls=%async_computation.1 | async-start | bytes 589824 | tf_op jit(solution)/shard_map/all_to_all | solution.py:450
  63.4 1.6 constant_dynamic-update-slice_fusion.2.refs_5_
  65.4 1.5 collective-permute-start.8
  66.9 9.5 %collective-permute-done.9.refs_11_ = bf16[400,512]{1,0:T(8,128)(2,1)} collective-permute-done((bf16[400,512]{1,0:T(8,128)(2,1)S(1)}, bf16[400,512]{1,0:T(8,128)(2,1)}, u32[]{:S(2)}, u32[]{:S(2)}) %collective-permute-start.9) | collective-permute-done | bytes 409632 | tf_op jit(solution)/shard_map/ppermute | solution.py:394
  77.3 1.2 dynamic_slice.31
  78.6 1.3 dynamic_slice.32
  81.2 1.4 reduce-window.9
  83.1 1.3 constant_dynamic-slice_fusion.2.taps
  84.4 1.0 constant_dynamic-slice_fusion.1
  85.4 3.0 %collective-permute-start.15 = (bf16[384,384]{1,0:T(8,128)(2,1)}, bf16[384,384]{1,0:T(8,128)(2,1)}, u32[]{:S(2)}, u32[]{:S(2)}) collective-permute-start(bf16[384,384]{1,0:T(8,128)(2,1)} %bitcast.24.refs_9_), channel_id=1, source_target_pairs={{0,16},{16,0},{1,17},{17,1},{2,18},{18,2},{3,19},{19,3},{4,20},{20... | collective-permute-start | bytes 884744 | tf_op jit(solution)/shard_map/ppermute | solution.py:394
  88.4 1.2 copy-done.4
  89.6 1.0 copy-done.7
  90.6 1.0 copy-done.9
  92.9 5.2 %inner_projection.1 = (bf16[8,144,384]{2,1,0:T(8,128)(2,1)S(1)}, bf16[8,144,128]{2,1,0:T(8,128)(2,1)S(1)}, f32[8,144,128]{2,1,0:T(8,128)S(1)}) custom-call(s32[8]{0:T(128)S(1)} %copy-done.25, s32[32]{0:T(128)S(1)} %copy-done.32, bf16[288,1536]{1,0:T(8,128)(2,1)S(1)} %copy-done.4, bf16[144,1536]{1,0:T(8,128)(2,1)} %collective-permute-done.1.refs_3_, ...), custom_call_target="tpu_custom_call" | custom-call | tf_op jit(solution)/shard_map/inner_projection/pallas_call | solution.py:29
  98.3 1.5 collective-permute-done.11
  99.8 8.8 %states.1 = (bf16[8,128,384]{2,1,0:T(8,128)(2,1)S(1)}, bf16[8,128,128]{2,1,0:T(8,128)(2,1)S(1)}, bf16[8,128,128]{2,1,0:T(8,128)(2,1)S(1)}, f32[8,128,128]{2,1,0:...) custom-call(s32[8]{0:T(128)S(1)} %copy-done.25, ...), custom_call_target="tpu_custom_call" | custom-call | tf_op jit(solution)/shard_map/states/pallas_call | solution.py:29
  109.4 1.1 copy-done.13
  113.2 1.1 collective-permute-start.17
  114.3 1.0 collective-permute-start.19
  115.2 1.1 collective-permute-start.14
  116.3 1.0 collective-permute-start.16
  117.3 2.9 %collective-permute-done.12.theirs = bf16[2,400,128]{2,1,0:T(8,128)(2,1)S(1)} collective-permute-done((bf16[2,400,128]{2,1,0:T(8,128)(2,1)S(1)}, bf16[2,400,128]{2,1,0:T(8,128)(2,1)S(1)}, u32[]{:S(2)}, u32[]{:S(2)}) %collective-permute-start.12) | collective-permute-done | bytes 204832 | tf_op jit(solution)/shard_map/ppermute | solution.py:53
  121.5 3.0 %collective-permute-start.13 = (bf16[400,128]{1,0:T(8,128)(2,1)S(1)}, bf16[400,128]{1,0:T(8,128)(2,1)}, u32[]{:S(2)}, u32[]{:S(2)}) collective-permute-start(bf16[400,128]{1,0:T(8,128)(2,1)S(1)} %compose.1), channel_id=1, source_target_pairs={{0,16},{1,17},{2,18},{3,19},{4,20},{5,21},{6,22},{7,23},{8,24},{9,... | collective-permute-start | bytes 307208 | tf_op jit(solution)/shard_map/ppermute | solution.py:556
  126.6 6.3 %collective-permute-done.19.refs_4_ = bf16[384,384]{1,0:T(8,128)(2,1)} collective-permute-done((bf16[384,384]{1,0:T(8,128)(2,1)}, bf16[384,384]{1,0:T(8,128)(2,1)}, u32[]{:S(2)}, u32[]{:S(2)}) %collective-permute-start.19) | collective-permute-done | bytes 294944 | tf_op jit(solution)/shard_map/ppermute | solution.py:53
  132.9 1.4 columns.1
  134.4 4.9 %collective-permute-done.14.refs_10_ = bf16[384,384]{1,0:T(8,128)(2,1)} collective-permute-done((bf16[384,384]{1,0:T(8,128)(2,1)}, bf16[384,384]{1,0:T(8,128)(2,1)}, u32[]{:S(2)}, u32[]{:S(2)}) %collective-permute-start.14) | collective-permute-done | bytes 294944 | tf_op jit(solution)/shard_map/ppermute | solution.py:53
  139.2 5.5 %collective-permute-done.16.refs_12_ = bf16[384,384]{1,0:T(8,128)(2,1)} collective-permute-done((bf16[384,384]{1,0:T(8,128)(2,1)}, bf16[384,384]{1,0:T(8,128)(2,1)}, u32[]{:S(2)}, u32[]{:S(2)}) %collective-permute-start.16) | collective-permute-done | bytes 294944 | tf_op jit(solution)/shard_map/ppermute | solution.py:53
  144.8 3.9 %gate_projection.1 = bf16[8,144,384]{2,1,0:T(8,128)(2,1)S(1)} custom-call(s32[8]{0:T(128)S(1)} %copy-done.26, s32[32]{0:T(128)S(1)} %copy-done.33, bf16[288,1536]{1,0:T(8,128)(2,1)S(1)} %copy-done.5, bf16[144,1536]{1,0:T(8,128)(2,1)} %collective-permute-done.1.refs_3_, bf16[144,1536]{1,0:T(8,128)(2,1)S(1)} %copy-done.8, bf16[144,1536]{1,0:T(8,128)(2,1)S(1)} %copy-done.10, ...), custom_call_target="tpu_custom_call" | custom-call | tf_op jit(solution)/shard_map/gate_projection/pallas_call | solution.py:29
  148.8 5.2 %within_chunks.1.y_ref = f32[8,128,384]{2,1,0:T(8,128)S(1)} custom-call(s32[8]{0:T(128)S(1)} %copy-done.26, s32[8]{0:T(128)S(1)} %bitcast_subtract_fusion.starts, s32[8]{0:T(128)S(1)} %copy-done.35, bf16[8,128,384]{2,1,0:T(8,128)(2,1)S(1)} %copy-done.20, bf16[8,128,128]{2,1,0:T(8,128)(2,1)S(1)} %copy-done.24, ...), custom_call_target="tpu_custom_call" | custom-call | tf_op jit(solution)/shard_map/within_chunks/pallas_call | solution.py:29
  155.0 4.6 %finish.1 = (bf16[8,128,384]{2,1,0:T(8,128)(2,1)S(1)}, f32[8,8,128]{2,1,0:T(8,128)S(1)}, bf16[4,2,384,128]{3,2,1,0:T(8,128)(2,1)S(1)}) custom-call(s32[8]{0:T(128)S(1)} %copy-done.26, s32[8]{0:T(128)S(1)} %bitcast_subtract_fusion.starts, bf16[2,400,128]{2,1,0:T(8,128)(2,1)S(1)} %copy-done.16, bf16[2,400,128]{2,1,0:T(8,128)(2,1)S(1)} %copy-done.18, ...), custom_call_target="tpu_custom_call" | custom-call | tf_op jit(solution)/shard_map/finish/pallas_call | solution.py:29
  160.3 2.1 mix_send.1
  162.5 2.1 mix_keep.1
  165.5 2.0 collective-permute-start.25
  167.7 1.3 collective-permute-start.27
  169.0 2.2 %fusion.11 = (bf16[4,128,1536]{2,1,0:T(8,128)(2,1)S(1)}, f32[4,128,1536]{2,1,0:T(8,128)}) fusion(bf16[4,128,1536]{2,1,0:T(8,128)(2,1)S(1)} %collective-permute-done.20, bf16[4,128,1536]{2,1,0:T(8,128)(2,1)S(1)} %mix_keep.1), kind=kLoop, calls=%fused_computation.40 | loop fusion | flops 3145728 | bytes 7864320 | tf_op jit(solution)/shard_map/convert.6
  171.2 1.2 copy-done.40
  173.2 2.0 collective-permute-start.21
  176.0 17.3 %psum.7 = f32[8,128]{1,0:T(8,128)S(1)} all-reduce(f32[8,128]{1,0:T(8,128)S(1)} %bitcast.87), channel_id=1, replica_groups=mesh['t'=2,'a'=2,'y'=2,'b'=2,'tp'=2] {'a','b','tp'}, use_global_device_ids=true, to_apply=%region_1.2 | all-reduce | flops 1024 | bytes 8192 | tf_op jit(solution)/shard_map/psum | solution.py:596
  193.4 2.4 %pages.1 = f32[2,4,384,128]{3,2,1,0:T(8,128)} custom-call(s32[8]{0:T(128)S(1)} %copy-done.26, s32[2]{0:T(128)S(1)} %copy-done.38, bf16[2,384,128]{2,1,0:T(8,128)(2,1)S(1)} %get-tuple-element.39.own, bf16[2,384,128]{2,1,0:T(8,128)(2,1)S(1)} %collective-permute-done.25.from_b, bf16[2,384,128]{2,1,0:T(8,128)(2,1)} %collective-permute-done.26.from_a, ...), custom_call_target="tpu_custom_call" | custom-call | tf_op jit(solution)/shard_map/pages/pallas_call | solution.py:29
  195.8 1.0 slice.119
  197.5 1.1 maximum_add_fusion
  198.6 1.5 collective-permute-start.22
  200.2 8.8 %collective-permute-done.23 = bf16[2,128,768]{2,1,0:T(8,128)(2,1)S(1)} collective-permute-done((bf16[2,128,768]{2,1,0:T(8,128)(2,1)S(1)}, bf16[2,128,768]{2,1,0:T(8,128)(2,1)S(1)}, u32[]{:S(2)}, u32[]{:S(2)}) %collective-permute-start.23) | collective-permute-done | bytes 393248 | tf_op jit(solution)/shard_map/ppermute | solution.py:53
  209.1 1.3 collective-permute-start.24
  211.4 3.4 %collective-permute-done.24 = bf16[128,768]{1,0:T(8,128)(2,1)S(1)} collective-permute-done((bf16[128,768]{1,0:T(8,128)(2,1)S(1)}, bf16[128,768]{1,0:T(8,128)(2,1)S(1)}, u32[]{:S(2)}, u32[]{:S(2)}) %collective-permute-start.24) | collective-permute-done | bytes 196640 | tf_op jit(solution)/shard_map/ppermute | solution.py:53
  (166 shorter events, 30.8 us)
Async XLA Ops:
  0.6 83.8 %copy-start = (f32[4,24,64,128]{3,2,1,0:T(8,128)S(1)}, f32[4,24,64,128]{3,2,1,0:T(8,128)}, u32[]{:S(2)}) copy-start(f32[4,24,64,128]{3,2,1,0:T(8,128)} %param.34) | copy-start | bytes 9437188
  2.3 16.1 %collective-permute-start = (bf16[32,1536]{1,0:T(8,128)(2,1)}, bf16[32,1536]{1,0:T(8,128)(2,1)}, u32[]{:S(2)}, u32[]{:S(2)}) collective-permute-start(bf16[32,1536]{1,0:T(8,128)(2,1)} %slice.82), channel_id=1, source_target_pairs={{0,2},{2,4},{4,6},{6,8},{8,10},{10,12},{12,14},{14,16},{16,18},{18... | collective-permute-start | bytes 294920 | tf_op jit(solution)/shard_map/ppermute | solution.py:488
  14.2 25.8 %all-to-all-start = ((bf16[8,48,640]{2,1,0:T(8,128)(2,1)}), bf16[8,48,640]{2,1,0:T(8,128)(2,1)}, u32[]{:S(2)}, u32[]{:S(2)}) async-start(bf16[8,48,640]{2,1,0:T(8,128)(2,1)} %bitcast.76), calls=%async_computation | async-start | bytes 983040 | tf_op jit(solution)/shard_map/all_to_all | solution.py:448
  18.4 20.8 %copy-start.41 = (f32[1536,96]{0,1:T(8,128)S(1)}, f32[1536,96]{0,1:T(8,128)}, u32[]{:S(2)}) copy-start(f32[1536,96]{0,1:T(8,128)} %param.31) | copy-start | bytes 1769476
  22.3 13.9 %collective-permute-start.2 = (bf16[144,1536]{1,0:T(8,128)(2,1)}, bf16[144,1536]{1,0:T(8,128)(2,1)S(1)}, u32[]{:S(2)}, u32[]{:S(2)}) collective-permute-start(bf16[144,1536]{1,0:T(8,128)(2,1)} %constant_dynamic-slice_fusion.3), channel_id=1, source_target_pairs={{0,8},{8,0},{1,9},{9,1},{2,10},{10,2},{3,11},{11,3},{4,12},{12,4},... | collective-permute-start | bytes 1327112 | tf_op jit(solution)/shard_map/ppermute | solution.py:53
  24.2 23.6 %collective-permute-start.1 = (bf16[144,1536]{1,0:T(8,128)(2,1)}, bf16[144,1536]{1,0:T(8,128)(2,1)}, u32[]{:S(2)}, u32[]{:S(2)}) collective-permute-start(bf16[144,1536]{1,0:T(8,128)(2,1)} %constant_dynamic-slice_fusion.3), channel_id=1, source_target_pairs={{0,2},{2,0},{1,3},{3,1},{4,6},{6,4},{5,7},{7,5},{8,10},{10,8},{9,1... | collective-permute-start | bytes 1327112 | tf_op jit(solution)/shard_map/ppermute | solution.py:53
  37.7 19.9 %collective-permute-start.3 = (bf16[80,1536]{1,0:T(8,128)(2,1)}, bf16[80,1536]{1,0:T(8,128)(2,1)}, u32[]{:S(2)}, u32[]{:S(2)}) collective-permute-start(bf16[80,1536]{1,0:T(8,128)(2,1)} %slice.105), channel_id=1, source_target_pairs={{0,2},{2,0},{1,3},{3,1},{4,6},{6,4},{5,7},{7,5},{8,10},{10,8},{9,1... | collective-permute-start | bytes 737288 | tf_op jit(solution)/shard_map/ppermute | solution.py:53
  40.0 19.3 %all-to-all-start.2 = ((bf16[4,96,384]{2,1,0:T(8,128)(2,1)}), bf16[4,96,384]{2,1,0:T(8,128)(2,1)}, u32[]{:S(2)}, u32[]{:S(2)}) async-start(bf16[4,96,384]{2,1,0:T(8,128)(2,1)} %bitcast.66), calls=%async_computation.2 | async-start | bytes 589824 | tf_op jit(solution)/shard_map/all_to_all | solution.py:452
  49.4 14.0 %collective-permute-start.4 = (bf16[64,1536]{1,0:T(8,128)(2,1)}, bf16[64,1536]{1,0:T(8,128)(2,1)}, u32[]{:S(2)}, u32[]{:S(2)}) collective-permute-start(bf16[64,1536]{1,0:T(8,128)(2,1)} %slice.106), channel_id=1, source_target_pairs={{0,8},{8,0},{1,9},{9,1},{2,10},{10,2},{3,11},{11,3},{4,12},{12,4},... | collective-permute-start | bytes 589832 | tf_op jit(solution)/shard_map/ppermute | solution.py:53
  51.4 34.0 %collective-permute-start.5 = (bf16[144,1536]{1,0:T(8,128)(2,1)}, bf16[144,1536]{1,0:T(8,128)(2,1)}, u32[]{:S(2)}, u32[]{:S(2)}) collective-permute-start(bf16[144,1536]{1,0:T(8,128)(2,1)} %collective-permute-done.1.refs_3_), channel_id=1, source_target_pairs={{0,1},{1,0},{2,3},{3,2},{4,5},{5,4},{6,7},{7,6},{8,9},{9,8},{10,11... | collective-permute-start | bytes 1327112 | tf_op jit(solution)/shard_map/ppermute | solution.py:53
  51.4 34.0 %collective-permute-start.6 = (bf16[144,1536]{1,0:T(8,128)(2,1)}, bf16[144,1536]{1,0:T(8,128)(2,1)}, u32[]{:S(2)}, u32[]{:S(2)}) collective-permute-start(bf16[144,1536]{1,0:T(8,128)(2,1)} %copy-done.6), channel_id=1, source_target_pairs={{0,1},{1,0},{2,3},{3,2},{4,5},{5,4},{6,7},{7,6},{8,9},{9,8},{10,11... | collective-permute-start | bytes 1327112 | tf_op jit(solution)/shard_map/ppermute | solution.py:53
  55.6 20.8 %collective-permute-start.9 = (bf16[400,512]{1,0:T(8,128)(2,1)S(1)}, bf16[400,512]{1,0:T(8,128)(2,1)}, u32[]{:S(2)}, u32[]{:S(2)}) collective-permute-start(bf16[400,512]{1,0:T(8,128)(2,1)S(1)} %fusion.4.refs_9_), channel_id=1, source_target_pairs={{0,16},{16,0},{1,17},{17,1},{2,18},{18,2},{3,19},{19,3},{4,20},{20... | collective-permute-start | bytes 1228808 | tf_op jit(solution)/shard_map/ppermute | solution.py:394
  59.3 26.0 %all-to-all-start.1 = ((bf16[8,48,384]{2,1,0:T(8,128)(2,1)}), bf16[8,48,384]{2,1,0:T(8,128)(2,1)}, u32[]{:S(2)}, u32[]{:S(2)}) async-start(bf16[8,48,384]{2,1,0:T(8,128)(2,1)} %bitcast.80), calls=%async_computation.1 | async-start | bytes 589824 | tf_op jit(solution)/shard_map/all_to_all | solution.py:450
  65.0 23.4 %collective-permute-start.7 = (bf16[144,1536]{1,0:T(8,128)(2,1)}, bf16[144,1536]{1,0:T(8,128)(2,1)}, u32[]{:S(2)}, u32[]{:S(2)}) collective-permute-start(bf16[144,1536]{1,0:T(8,128)(2,1)} %constant_dynamic-update-slice_fusion.2.refs_5_), channel_id=1, source_target_pairs={{0,1},{1,0},{2,3},{3,2},{4,5},{5,4},{6,7},{7,6},{8,9},{9,8},{10,11... | collective-permute-start | bytes 1327112 | tf_op jit(solution)/shard_map/ppermute | solution.py:53
  65.4 23.0 %collective-permute-start.8 = (bf16[400,512]{1,0:T(8,128)(2,1)S(1)}, bf16[400,512]{1,0:T(8,128)(2,1)}, u32[]{:S(2)}, u32[]{:S(2)}) collective-permute-start(bf16[400,512]{1,0:T(8,128)(2,1)S(1)} %fusion.4.refs_9_), channel_id=1, source_target_pairs={{0,4},{4,0},{1,5},{5,1},{2,6},{6,2},{3,7},{7,3},{8,12},{12,8},{9,1... | collective-permute-start | bytes 1228808 | tf_op jit(solution)/shard_map/ppermute | solution.py:53
  76.4 12.0 %collective-permute-start.10 = (bf16[400,512]{1,0:T(8,128)(2,1)}, bf16[400,512]{1,0:T(8,128)(2,1)}, u32[]{:S(2)}, u32[]{:S(2)}) collective-permute-start(bf16[400,512]{1,0:T(8,128)(2,1)} %collective-permute-done.9.refs_11_), channel_id=1, source_target_pairs={{0,4},{4,0},{1,5},{5,1},{2,6},{6,2},{3,7},{7,3},{8,12},{12,8},{9,1... | collective-permute-start | bytes 1228808 | tf_op jit(solution)/shard_map/ppermute | solution.py:53
  85.4 28.9 %collective-permute-start.18 = (bf16[384,384]{1,0:T(8,128)(2,1)}, bf16[384,384]{1,0:T(8,128)(2,1)}, u32[]{:S(2)}, u32[]{:S(2)}) collective-permute-start(bf16[384,384]{1,0:T(8,128)(2,1)} %bitcast.28.refs_1_), channel_id=1, source_target_pairs={{0,16},{16,0},{1,17},{17,1},{2,18},{18,2},{3,19},{19,3},{4,20},{20... | collective-permute-start | bytes 884744 | tf_op jit(solution)/shard_map/ppermute | solution.py:394
  85.4 14.4 %copy-start.30 = (f32[1,384]{1,0:T(1,128)S(1)}, f32[1,384]{1,0:T(1,128)}, u32[]{:S(2)}) copy-start(f32[1,384]{1,0:T(1,128)} %broadcast_in_dim.26.bias) | copy-start | bytes 4612
  85.4 14.4 %copy-start.1 = (f32[4,6,64,128]{3,2,1,0:T(8,128)S(1)}, f32[4,6,64,128]{3,2,1,0:T(8,128)}, u32[]{:S(2)}) copy-start(f32[4,6,64,128]{3,2,1,0:T(8,128)} %constant_dynamic-slice_fusion.1) | copy-start | bytes 2359300
  85.4 30.9 %collective-permute-start.15 = (bf16[384,384]{1,0:T(8,128)(2,1)}, bf16[384,384]{1,0:T(8,128)(2,1)}, u32[]{:S(2)}, u32[]{:S(2)}) collective-permute-start(bf16[384,384]{1,0:T(8,128)(2,1)} %bitcast.24.refs_9_), channel_id=1, source_target_pairs={{0,16},{16,0},{1,17},{17,1},{2,18},{18,2},{3,19},{19,3},{4,20},{20... | collective-permute-start | bytes 884744 | tf_op jit(solution)/shard_map/ppermute | solution.py:394
  92.8 5.4 %copy-start.42 = (f32[6]{0:T(128)S(1)}, f32[6]{0:T(128)}, u32[]{:S(2)}) copy-start(f32[6]{0:T(128)} %dynamic_slice.31) | copy-start | bytes 76
  92.8 5.4 %copy-start.43 = (f32[6]{0:T(128)S(1)}, f32[6]{0:T(128)}, u32[]{:S(2)}) copy-start(f32[6]{0:T(128)} %dynamic_slice.32) | copy-start | bytes 76
  92.8 5.4 %copy-start.44 = (s32[8]{0:T(128)S(1)}, s32[8]{0:T(128)}, u32[]{:S(2)}) copy-start(s32[8]{0:T(128)} %param.32) | copy-start | bytes 100
  92.8 5.4 %copy-start.46 = (s32[8,1]{0,1:T(1,128)S(1)}, s32[8,1]{0,1:T(1,128)}, u32[]{:S(2)}) copy-start(s32[8,1]{0,1:T(1,128)} %reduce-window.9) | copy-start | bytes 100
  92.8 6.9 %copy-start.29 = (f32[4,384]{1,0:T(4,128)S(1)}, f32[4,384]{1,0:T(4,128)}, u32[]{:S(2)}) copy-start(f32[4,384]{1,0:T(4,128)} %constant_dynamic-slice_fusion.2.taps) | copy-start | bytes 18436
  92.8 6.9 %copy-start.31 = (f32[4,256]{1,0:T(4,128)S(1)}, f32[4,256]{1,0:T(4,128)}, u32[]{:S(2)}) copy-start(f32[4,256]{1,0:T(4,128)} %taps2.1) | copy-start | bytes 12292
  92.8 6.9 %copy-start.34 = (s32[8]{0:T(128)S(1)}, s32[8]{0:T(128)}, u32[]{:S(2)}) copy-start(s32[8]{0:T(128)} %groups.3) | copy-start | bytes 100
  92.9 6.9 %copy-start.36 = (f32[256]{0:T(256)S(1)}, f32[256]{0:T(256)}, u32[]{:S(2)}) copy-start(f32[256]{0:T(256)} %param.26) | copy-start | bytes 3076
  98.1 1.6 collective-permute-start.11
  99.8 24.8 %copy-start.45 = (f32[24]{0:T(128)S(1)}, f32[24]{0:T(128)}, u32[]{:S(2)}) copy-start(f32[24]{0:T(128)} %param.29) | copy-start | bytes 292
  99.8 33.1 %copy-start.26 = (s32[8]{0:T(128)S(1)}, s32[8]{0:T(128)}, u32[]{:S(2)}) copy-start(s32[8]{0:T(128)} %stack.30.refs_0_.info) | copy-start | bytes 100
  112.2 12.3 %copy-start.23 = (bf16[8,128,128]{2,1,0:T(8,128)(2,1)}, bf16[8,128,128]{2,1,0:T(8,128)(2,1)S(1)}, u32[]{:S(2)}) copy-start(bf16[8,128,128]{2,1,0:T(8,128)(2,1)S(1)} %get-tuple-element.25.b_ref) | copy-start | bytes 786436
  112.2 12.4 %copy-start.27 = (f32[8,8,128]{2,1,0:T(8,128)}, f32[8,8,128]{2,1,0:T(8,128)S(1)}, u32[]{:S(2)}) copy-start(f32[8,8,128]{2,1,0:T(8,128)S(1)} %get-tuple-element.23.factor_ref) | copy-start | bytes 98308
  112.2 32.5 %copy-start.33 = (s32[32]{0:T(128)S(1)}, s32[32]{0:T(128)}, u32[]{:S(2)}) copy-start(s32[32]{0:T(128)} %refs_1_.3) | copy-start | bytes 388
  112.2 7.9 %collective-permute-start.12 = (bf16[2,400,128]{2,1,0:T(8,128)(2,1)S(1)}, bf16[2,400,128]{2,1,0:T(8,128)(2,1)S(1)}, u32[]{:S(2)}, u32[]{:S(2)}) collective-permute-start(bf16[2,400,128]{2,1,0:T(8,128)(2,1)S(1)} %get-tuple-element.19.mine), channel_id=1, source_target_pairs={{0,4},{4,0},{1,5},{5,1},{2,6},{6,2},{3,7},{7,3},{8,12},{12,8},{9,1... | collective-permute-start | bytes 614408 | tf_op jit(solution)/shard_map/ppermute | solution.py:53
  113.2 13.4 %collective-permute-start.17 = (bf16[384,384]{1,0:T(8,128)(2,1)}, bf16[384,384]{1,0:T(8,128)(2,1)}, u32[]{:S(2)}, u32[]{:S(2)}) collective-permute-start(bf16[384,384]{1,0:T(8,128)(2,1)} %bitcast.28.refs_1_), channel_id=1, source_target_pairs={{0,4},{4,0},{1,5},{5,1},{2,6},{6,2},{3,7},{7,3},{8,12},{12,8},{9,1... | collective-permute-start | bytes 884744 | tf_op jit(solution)/shard_map/ppermute | solution.py:53
  114.3 18.6 %collective-permute-start.19 = (bf16[384,384]{1,0:T(8,128)(2,1)}, bf16[384,384]{1,0:T(8,128)(2,1)}, u32[]{:S(2)}, u32[]{:S(2)}) collective-permute-start(bf16[384,384]{1,0:T(8,128)(2,1)} %collective-permute-done.18.refs_3_), channel_id=1, source_target_pairs={{0,4},{4,0},{1,5},{5,1},{2,6},{6,2},{3,7},{7,3},{8,12},{12,8},{9,1... | collective-permute-start | bytes 884744 | tf_op jit(solution)/shard_map/ppermute | solution.py:53
  115.2 24.0 %collective-permute-start.14 = (bf16[384,384]{1,0:T(8,128)(2,1)}, bf16[384,384]{1,0:T(8,128)(2,1)}, u32[]{:S(2)}, u32[]{:S(2)}) collective-permute-start(bf16[384,384]{1,0:T(8,128)(2,1)} %bitcast.24.refs_9_), channel_id=1, source_target_pairs={{0,4},{4,0},{1,5},{5,1},{2,6},{6,2},{3,7},{7,3},{8,12},{12,8},{9,1... | collective-permute-start | bytes 884744 | tf_op jit(solution)/shard_map/ppermute | solution.py:53
  116.3 28.4 %collective-permute-start.16 = (bf16[384,384]{1,0:T(8,128)(2,1)}, bf16[384,384]{1,0:T(8,128)(2,1)}, u32[]{:S(2)}, u32[]{:S(2)}) collective-permute-start(bf16[384,384]{1,0:T(8,128)(2,1)} %collective-permute-done.15.refs_11_), channel_id=1, source_target_pairs={{0,4},{4,0},{1,5},{5,1},{2,6},{6,2},{3,7},{7,3},{8,12},{12,8},{9,1... | collective-permute-start | bytes 884744 | tf_op jit(solution)/shard_map/ppermute | solution.py:53
  121.5 32.5 %collective-permute-start.13 = (bf16[400,128]{1,0:T(8,128)(2,1)S(1)}, bf16[400,128]{1,0:T(8,128)(2,1)}, u32[]{:S(2)}, u32[]{:S(2)}) collective-permute-start(bf16[400,128]{1,0:T(8,128)(2,1)S(1)} %compose.1), channel_id=1, source_target_pairs={{0,16},{1,17},{2,18},{3,19},{4,20},{5,21},{6,22},{7,23},{8,24},{9,... | collective-permute-start | bytes 307208 | tf_op jit(solution)/shard_map/ppermute | solution.py:556
  124.8 20.0 %copy-start.5 = (bf16[288,1536]{1,0:T(8,128)(2,1)S(1)}, bf16[288,1536]{1,0:T(8,128)(2,1)}, u32[]{:S(2)}) copy-start(bf16[288,1536]{1,0:T(8,128)(2,1)} %copy-done.3) | copy-start | bytes 2654212
  124.8 20.0 %copy-start.8 = (bf16[144,1536]{1,0:T(8,128)(2,1)S(1)}, bf16[144,1536]{1,0:T(8,128)(2,1)}, u32[]{:S(2)}) copy-start(bf16[144,1536]{1,0:T(8,128)(2,1)} %copy-done.6) | copy-start | bytes 1327108
  124.8 20.0 %copy-start.10 = (bf16[144,1536]{1,0:T(8,128)(2,1)S(1)}, bf16[144,1536]{1,0:T(8,128)(2,1)}, u32[]{:S(2)}) copy-start(bf16[144,1536]{1,0:T(8,128)(2,1)} %constant_dynamic-update-slice_fusion.2.refs_5_) | copy-start | bytes 1327108
  134.3 14.4 %copy-start.2 = (f32[4,6,64,128]{3,2,1,0:T(8,128)S(1)}, f32[4,6,64,128]{3,2,1,0:T(8,128)}, u32[]{:S(2)}) copy-start(f32[4,6,64,128]{3,2,1,0:T(8,128)} %constant_dynamic-slice_fusion.1) | copy-start | bytes 2359300
  134.3 14.4 %copy-start.12 = (f32[8,128,128]{2,1,0:T(8,128)S(1)}, f32[8,128,128]{2,1,0:T(8,128)}, u32[]{:S(2)}) copy-start(f32[8,128,128]{2,1,0:T(8,128)} %copy-done.11) | copy-start | bytes 1572868
  134.3 14.4 %copy-start.20 = (bf16[8,128,384]{2,1,0:T(8,128)(2,1)S(1)}, bf16[8,128,384]{2,1,0:T(8,128)(2,1)}, u32[]{:S(2)}) copy-start(bf16[8,128,384]{2,1,0:T(8,128)(2,1)} %copy-done.19) | copy-start | bytes 2359300
  134.3 14.4 %copy-start.22 = (f32[8,128,128]{2,1,0:T(8,128)S(1)}, f32[8,128,128]{2,1,0:T(8,128)}, u32[]{:S(2)}) copy-start(f32[8,128,128]{2,1,0:T(8,128)} %copy-done.21) | copy-start | bytes 1572868
  134.3 14.4 %copy-start.24 = (bf16[8,128,128]{2,1,0:T(8,128)(2,1)S(1)}, bf16[8,128,128]{2,1,0:T(8,128)(2,1)}, u32[]{:S(2)}) copy-start(bf16[8,128,128]{2,1,0:T(8,128)(2,1)} %copy-done.23) | copy-start | bytes 786436
  134.4 14.4 %copy-start.35 = (s32[8]{0:T(128)S(1)}, s32[8]{0:T(128)}, u32[]{:S(2)}) copy-start(s32[8]{0:T(128)} %groups.3) | copy-start | bytes 100
  148.7 6.2 %copy-start.14 = (f32[8,384,128]{2,1,0:T(8,128)S(1)}, f32[8,384,128]{2,1,0:T(8,128)}, u32[]{:S(2)}) copy-start(f32[8,384,128]{2,1,0:T(8,128)} %copy-done.13) | copy-start | bytes 4718596
  148.8 6.2 %copy-start.16 = (bf16[2,400,128]{2,1,0:T(8,128)(2,1)S(1)}, bf16[2,400,128]{2,1,0:T(8,128)(2,1)}, u32[]{:S(2)}) copy-start(bf16[2,400,128]{2,1,0:T(8,128)(2,1)} %copy-done.15) | copy-start | bytes 614404
  148.8 6.2 %copy-start.18 = (bf16[2,400,128]{2,1,0:T(8,128)(2,1)S(1)}, bf16[2,400,128]{2,1,0:T(8,128)(2,1)}, u32[]{:S(2)}) copy-start(bf16[2,400,128]{2,1,0:T(8,128)(2,1)} %copy-done.17) | copy-start | bytes 614404
  148.8 6.2 %copy-start.28 = (f32[8,8,128]{2,1,0:T(8,128)S(1)}, f32[8,8,128]{2,1,0:T(8,128)}, u32[]{:S(2)}) copy-start(f32[8,8,128]{2,1,0:T(8,128)} %copy-done.27) | copy-start | bytes 98308
  162.5 6.5 %collective-permute-start.20 = (bf16[4,128,1536]{2,1,0:T(8,128)(2,1)S(1)}, bf16[4,128,1536]{2,1,0:T(8,128)(2,1)S(1)}, u32[]{:S(2)}, u32[]{:S(2)}) collective-permute-start(bf16[4,128,1536]{2,1,0:T(8,128)(2,1)S(1)} %mix_send.1), channel_id=1, source_target_pairs={{0,1},{1,0},{2,3},{3,2},{4,5},{5,4},{6,7},{7,6},{8,9},{9,8},{10,11... | collective-permute-start | bytes 4718600 | tf_op jit(solution)/shard_map/ppermute | solution.py:53
  165.5 27.8 %collective-permute-start.25 = (bf16[2,384,128]{2,1,0:T(8,128)(2,1)}, bf16[2,384,128]{2,1,0:T(8,128)(2,1)S(1)}, u32[]{:S(2)}, u32[]{:S(2)}) collective-permute-start(bf16[2,384,128]{2,1,0:T(8,128)(2,1)} %get-tuple-element.38), channel_id=1, source_target_pairs={{0,2},{2,0},{1,3},{3,1},{4,6},{6,4},{5,7},{7,5},{8,10},{10,8},{9,1... | collective-permute-start | bytes 589832 | tf_op jit(solution)/shard_map/ppermute | solution.py:53
  167.5 25.9 %collective-permute-start.26 = (bf16[2,384,128]{2,1,0:T(8,128)(2,1)}, bf16[2,384,128]{2,1,0:T(8,128)(2,1)}, u32[]{:S(2)}, u32[]{:S(2)}) collective-permute-start(bf16[2,384,128]{2,1,0:T(8,128)(2,1)} %get-tuple-element.37), channel_id=1, source_target_pairs={{0,8},{8,0},{1,9},{9,1},{2,10},{10,2},{3,11},{11,3},{4,12},{12,4},... | collective-permute-start | bytes 589832 | tf_op jit(solution)/shard_map/ppermute | solution.py:53
  167.7 25.7 %collective-permute-start.27 = (bf16[2,384,128]{2,1,0:T(8,128)(2,1)}, bf16[2,384,128]{2,1,0:T(8,128)(2,1)}, u32[]{:S(2)}, u32[]{:S(2)}) collective-permute-start(bf16[2,384,128]{2,1,0:T(8,128)(2,1)} %get-tuple-element.36), channel_id=1, source_target_pairs={{0,10},{2,8},{8,2},{10,0},{1,11},{3,9},{9,3},{11,1},{4,14},{6,12},... | collective-permute-start | bytes 589832 | tf_op jit(solution)/shard_map/ppermute | solution.py:585
  171.2 1.2 copy-start.40
  171.2 22.2 %copy-start.38 = (s32[2]{0:T(128)S(1)}, s32[2]{0:T(128)}, u32[]{:S(2)}) copy-start(s32[2]{0:T(128)} %table.1) | copy-start | bytes 28
  173.2 24.3 %collective-permute-start.21 = (bf16[2,128,768]{2,1,0:T(8,128)(2,1)}, bf16[2,128,768]{2,1,0:T(8,128)(2,1)}, u32[]{:S(2)}, u32[]{:S(2)}) collective-permute-start(bf16[2,128,768]{2,1,0:T(8,128)(2,1)} %pad_maximum_fusion), channel_id=1, source_target_pairs={{0,2},{2,0},{1,3},{3,1},{4,6},{6,4},{5,7},{7,5},{8,10},{10,8},{9,1... | collective-permute-start | bytes 1179656 | tf_op jit(solution)/shard_map/ppermute | solution.py:53
  193.4 4.1 %copy-start.39 = (f32[4,128,1536]{2,1,0:T(8,128)S(1)}, f32[4,128,1536]{2,1,0:T(8,128)}, u32[]{:S(2)}) copy-start(f32[4,128,1536]{2,1,0:T(8,128)} %get-tuple-element.33) | copy-start | bytes 9437188
  196.8 12.1 %collective-permute-start.23 = (bf16[2,128,768]{2,1,0:T(8,128)(2,1)S(1)}, bf16[2,128,768]{2,1,0:T(8,128)(2,1)S(1)}, u32[]{:S(2)}, u32[]{:S(2)}) collective-permute-start(bf16[2,128,768]{2,1,0:T(8,128)(2,1)S(1)} %slice.119), channel_id=1, source_target_pairs={{0,8},{8,0},{1,9},{9,1},{2,10},{10,2},{3,11},{11,3},{4,12},{12,4},... | collective-permute-start | bytes 1179656 | tf_op jit(solution)/shard_map/ppermute | solution.py:53
  198.6 12.7 %collective-permute-start.22 = (bf16[128,768]{1,0:T(8,128)(2,1)S(1)}, bf16[128,768]{1,0:T(8,128)(2,1)S(1)}, u32[]{:S(2)}, u32[]{:S(2)}) collective-permute-start(bf16[128,768]{1,0:T(8,128)(2,1)S(1)} %fusion.7), channel_id=1, source_target_pairs={{0,8},{8,0},{1,9},{9,1},{2,10},{10,2},{3,11},{11,3},{4,12},{12,4},... | collective-permute-start | bytes 589832 | tf_op jit(solution)/shard_map/ppermute | solution.py:53
  209.1 5.7 %collective-permute-start.24 = (bf16[128,768]{1,0:T(8,128)(2,1)S(1)}, bf16[128,768]{1,0:T(8,128)(2,1)S(1)}, u32[]{:S(2)}, u32[]{:S(2)}) collective-permute-start(bf16[128,768]{1,0:T(8,128)(2,1)S(1)} %fusion.8), channel_id=1, source_target_pairs={{0,2},{2,0},{1,3},{3,1},{4,6},{6,4},{5,7},{7,5},{8,10},{10,8},{9,1... | collective-permute-start | bytes 589832 | tf_op jit(solution)/shard_map/ppermute | solution.py:53
  (14 other events, 11.8 us)

commit v2 on v1

v2 whole, which is shorter than its diff:
```python
import functools

import jax
import jax.numpy as jnp
from jax import lax
from jax.experimental import pallas as pl
from jax.experimental.pallas import tpu as pltpu
from jax.sharding import Mesh
from jax.sharding import PartitionSpec as P

N = 128
CONV = 4
PAGE = 128
TILE = 16
LANES = 128
EPSILON = 1e-05
F32 = jnp.float32
BF16 = jnp.bfloat16
HIGHEST = lax.Precision.HIGHEST
GROUP = ("a", "b", "tp")
SEQ = ("t", "a", "y", "b")
VMEM = pl.BlockSpec(memory_space=pltpu.VMEM)
SMEM = pl.BlockSpec(memory_space=pltpu.SMEM)


def call(body, name, out_shape, ins, scratch=(), after=(), us=1.0, limit=40):
    specs = [SMEM if x.dtype == jnp.int32 else VMEM for x in ins]
    specs += [pl.BlockSpec(memory_space=pl.ANY)] * len(after)
    first, last = len(ins), len(ins) + len(after)

    def kernel(*refs):
        body(*refs[:first], *refs[last:])

    return pl.pallas_call(
        kernel,
        name=name,
        out_shape=out_shape,
        in_specs=specs,
        out_specs=jax.tree.map(lambda _: VMEM, out_shape),
        scratch_shapes=list(scratch),
        cost_estimate=pl.CostEstimate(
            flops=int(us * 1e9), bytes_accessed=int(us * 3e6), transcendentals=0
        ),
        compiler_params=pltpu.CompilerParams(vmem_limit_bytes=limit << 20),
    )(*ins, *after)


def shape(dims, dtype):
    return jax.ShapeDtypeStruct(dims, dtype)


def dot(x, y, dims=((1,), (0,)), precision=None):
    return lax.dot_general(x, y, (dims, ((), ())), precision=precision, preferred_element_type=F32)


NT = ((1,), (1,))
TN = ((0,), (0,))


def swap(x, axis):
    return lax.ppermute(x, axis, [(0, 1), (1, 0)])


class Ints:
    def __init__(self, ref, at, size):
        self.ref, self.at, self.size = ref, at, size

    def __getitem__(self, k):
        return self.ref[self.at + k]


def views(ref, sizes):
    out, at = [], 0
    for size in sizes:
        out.append(Ints(ref, at, size))
        at += size
    return out


def stored_block(s, dy, place, info):
    t, y, count = info[3], info[4], info[5]
    a, b, c = place // 4, (place // 2) % 2, place % 2
    source = lax.rem(t - s + count, count)
    seq = ((source * 2 + a) * 2 + (y ^ dy)) * 2 + b
    return seq * 2 + c


def pack_kernel(heads, inner, small, gate, out):
    width = heads * 64
    rows = inner.shape[0]
    lane = lax.broadcasted_iota(jnp.int32, (rows, LANES), 1)
    steps = small[:, 2 * N :]
    steps = jnp.concatenate([steps, jnp.zeros((rows, LANES - steps.shape[1]), F32)], axis=1)
    for place in range(8):
        group, c = place // 2, place % 2
        at = (c * 4 + group) * width
        out[place, :, :width] = inner[:, at : at + width].astype(BF16)
        out[place, :, width : width + N] = small[:, c * N : (c + 1) * N].astype(BF16)
        first = (c * 4 + group) * heads
        moved = pltpu.roll(steps, LANES - first, 1) if first else steps
        out[place, :, width + N : width + N + LANES] = jnp.where(lane < heads, moved, 0.0).astype(BF16)
        out[place, :, width + N + LANES :] = gate[:, at : at + width].astype(BF16)


def repack_kernel(got, whole, low, high, gate):
    rows, width = got.shape[1], whole.shape[1]
    for place in range(8):
        gate[place * rows : (place + 1) * rows, :] = got[place, :, width + LANES :]
    lane = lax.broadcasted_iota(jnp.int32, (TILE, LANES), 1) // TILE
    for place in range(8):
        block = got[place, :, :width]
        whole[place * rows : (place + 1) * rows, :] = block
        half, at = (low, place) if place < 4 else (high, place - 4)
        half[at * rows : (at + 1) * rows, :] = block
    for piece in range(rows // TILE):
        packed = jnp.zeros((TILE, LANES), F32)
        for place in range(8):
            steps = got[place, piece * TILE : (piece + 1) * TILE, width : width + LANES].astype(F32)
            steps = pltpu.roll(steps, place * TILE, 1) if place else steps
            packed = jnp.where(lane == place, steps, packed)
        here = slice(piece * LANES, (piece + 1) * LANES)
        whole[8 * rows :, here] = packed.astype(BF16)
        high[4 * rows :, here] = packed.astype(BF16)
    rest = rows // TILE * LANES
    if rest < width:
        blank = jnp.zeros((TILE, width - rest), BF16)
        whole[8 * rows :, rest:] = blank
        high[4 * rows :, rest:] = blank


def copy_kernel(source, out):
    out[...] = source[...]


def pack_out_kernel(source, out):
    width = out.shape[2]
    for place in range(4):
        out[place] = source[:, place * width : (place + 1) * width].astype(BF16)


def forward_kernel(sizes, ints, mine_b, mine_a, halo0, halo1, over_b, over_a):
    info = views(ints, sizes)[0]
    cut = over_b.shape[0]
    over_b[...] = mine_a[:cut, :]
    over_a[:cut, :] = mine_b[cut:, :]

    @pl.when(info[0] % 2 == 0)
    def _():
        over_a[cut:, :] = halo0[...]

    @pl.when(info[0] % 2 == 1)
    def _():
        over_a[cut:, :] = halo1[...]


def assemble_kernel(sizes, ints, own, mine_b, mine_a, mine_d0, mine_d1, other_b, other_a, other_d0,
                    other_d1, halo0, halo1, out):
    info = views(ints, sizes)[0]
    me, c = info[0], info[1]
    half = own.shape[0] // 2

    def put(q, h, row, source):
        at = TILE + ((q % 2) * 2 + h) * half + row
        out[q // 2, pl.ds(pl.multiple_of(at, TILE), source.shape[0]), :] = source

    put(me, 0, 0, own[:half, :])
    put(me, 1, 0, own[half:, :])
    for h, parts in ((c, (mine_b, mine_a, mine_d0, mine_d1)), (1 - c, (other_b, other_a, other_d0, other_d1))):
        cut = parts[2].shape[0]
        put(me ^ 1, h, 0, parts[0][...])
        put(me ^ 2, h, 0, parts[1][...])
        put(me ^ 3, h, 0, parts[2][...])
        put(me ^ 3, h, cut, parts[3][:cut, :])
    a = me // 2
    out[1 - a, :TILE, :] = mine_d1[cut:, :]

    @pl.when(me % 2 == 0)
    def _():
        out[a, :TILE, :] = halo0[...]

    @pl.when(me % 2 == 1)
    def _():
        out[a, :TILE, :] = halo1[...]


def place_parts(weights, marks, rows, parts, info, layout):
    width = parts[0].shape[1]
    lane = lax.broadcasted_iota(jnp.int32, (TILE, LANES), 1) // TILE
    for (s, dy, first), part in zip(marks, parts):
        count = part.shape[0] // rows
        for k in range(count):
            block = layout[stored_block(s, dy, first + k, info)]
            at = pl.multiple_of(block * rows, TILE)
            weights[pl.ds(at, rows), :width] = part[k * rows : (k + 1) * rows, :]
        base = count * rows
        if part.shape[0] == base:
            continue
        for place in range(8):
            block = layout[stored_block(s, dy, place, info)]
            for piece in range(rows // TILE):
                packed = part[base : base + TILE, piece * LANES : (piece + 1) * LANES]
                kept = jnp.where(lane == place, packed, jnp.zeros_like(packed))
                at = pl.multiple_of(block * rows + piece * TILE, TILE)
                weights[pl.ds(at, TILE), width:] = kept


def inner_kernel(sizes, marks, rows, *refs):
    info, layout = views(refs[0], sizes)[:2]
    hidden = refs[1]
    if marks:
        parts = refs[2 : 2 + len(marks)]
        raw_ref, shared_ref, step_ref, weights = refs[2 + len(marks) :]
        place_parts(weights, marks, rows, parts, info, layout)
    else:
        weights, raw_ref, shared_ref, step_ref = refs[2:6]
    bc = raw_ref.shape[2]
    for run in range(2):
        result = dot(hidden[run], weights[:, bc:])
        shared_ref[run] = result[:, :LANES].astype(BF16)
        step = result[:, LANES:]
        for shift in (64, 32, 16):
            step = step + pltpu.roll(step, shift, 1)
        step_ref[run] = step
        raw_ref[run] = dot(hidden[run], weights[:, :bc]).astype(BF16)


def gate_kernel(sizes, marks, rows, *refs):
    info, layout = views(refs[0], sizes)[:2]
    hidden = refs[1]
    if marks:
        gate_ref, weights = refs[2 + len(marks) :]
        place_parts(weights, marks, rows, refs[2 : 2 + len(marks)], info, layout)
    else:
        weights, gate_ref = refs[2:4]
    for run in range(2):
        gate_ref[run] = jax.nn.silu(dot(hidden[run], weights[...])).astype(BF16)


def starts_of(lengths):
    starts, total = [], jnp.int32(0)
    for k in range(lengths.size):
        starts.append(total)
        total = total + lengths[k]
    return starts


def head_lanes(row, heads, info):
    return pltpu.roll(row, lax.rem(LANES - info[0] * heads, LANES), 1)


def chunk_start(i, info, tokens):
    t, y = info[3], info[4]
    per = tokens // PAGE
    q = i // per
    seq = ((t * 2 + q // 2) * 2 + y) * 2 + q % 2
    return seq * tokens + (i % per) * PAGE


def last_start(position, starts):
    best = jnp.int32(0)
    for k in range(len(starts)):
        best = jnp.maximum(best, jnp.where(starts[k] <= position, starts[k], 0))
    return best


def first_positions(first, starts, dims):
    position = first + lax.broadcasted_iota(jnp.int32, dims, 0)
    best = jnp.zeros(dims, jnp.int32)
    for k in range(len(starts)):
        best = jnp.maximum(best, jnp.where(starts[k] <= position, starts[k], 0))
    return best


def conv_silu(window, taps, bias, offset):
    total = bias + taps[0:1, :] * window[TILE : TILE + PAGE]
    for lag in range(1, CONV):
        within = (offset >= lag).astype(F32)
        total = total + taps[lag : lag + 1, :] * window[TILE - lag : TILE - lag + PAGE] * within
    return total / (1.0 + jnp.exp(-total))


def pair_columns(values, pair):
    lane = lax.broadcasted_iota(jnp.int32, (PAGE, LANES), 1)
    left = values[:, 2 * pair : 2 * pair + 1]
    right = values[:, 2 * pair + 1 : 2 * pair + 2]
    return jnp.where(lane < 64, left, right)


def state_kernel(heads, tokens, sizes, ints, raw, own, other, step, params, init, x_ref, b_ref, c_ref,
                 cum_ref, dt_ref, end_ref, factor_ref, summary_ref, state, factor):
    info, _, lengths, groups = views(ints, sizes)[:4]
    starts = starts_of(lengths)
    width = heads * 64
    here = pl.ds(pl.multiple_of(info[0] * width, LANES), width)
    taps, bias = params[0:4, here], params[4:5, here]
    taps2, bias2 = params[8:12, : 2 * N], params[12:13, : 2 * N]
    per_head = head_lanes(params[8:16, 2 * N : 2 * N + LANES], heads, info)
    dt_bias, rate = per_head[0:1], -jnp.exp(per_head[1:2])
    chunks = x_ref.shape[0]
    per_run = chunks // 2
    pairs = heads // 2
    row = lax.broadcasted_iota(jnp.int32, (PAGE, PAGE), 0)
    col = lax.broadcasted_iota(jnp.int32, (PAGE, PAGE), 1)
    below = (row >= col).astype(F32)

    def one(i, carry):
        @pl.when(i % per_run == 0)
        def _():
            state[...] = jnp.zeros_like(state)
            factor[...] = jnp.ones_like(factor)

        first = chunk_start(i, info, tokens)
        opened = last_start(first + PAGE - 1, starts)
        alive = (opened < first).astype(F32)
        start_of = first_positions(first, starts, (PAGE, 1))
        offset = first + lax.broadcasted_iota(jnp.int32, (PAGE, 1), 0) - start_of
        q = i // per_run
        at = pl.multiple_of((i % per_run) * PAGE, TILE)
        window = pl.ds(at, PAGE + TILE)
        x = conv_silu(raw[q, window, :].astype(F32), taps, bias, offset)
        is_first = info[1] == 0
        mine, theirs = own[q, window, :].astype(F32), other[q, window, :].astype(F32)
        b_raw = jnp.where(is_first, mine, theirs)
        c_raw = jnp.where(is_first, theirs, mine)
        b = conv_silu(b_raw, taps2[:, :LANES], bias2[:, :LANES], offset).astype(BF16)
        c = conv_silu(c_raw, taps2[:, LANES:], bias2[:, LANES:], offset).astype(BF16)
        raw_step = step[q, pl.ds(pl.multiple_of(at + TILE, TILE), PAGE), :]
        v = raw_step + dt_bias
        dt = jnp.maximum(v, 0.0) + jnp.log1p(jnp.exp(-jnp.abs(v)))
        log_rate = rate * dt
        cum = dot(below, log_rate, precision=HIGHEST)
        last = cum[PAGE - 1 : PAGE, :]
        kept = (row >= opened - first).astype(F32)
        weight = jnp.exp(last - cum) * dt * kept
        cum_t = cum.T
        x_ref[i] = x.astype(BF16)
        b_ref[i] = b
        c_ref[i] = c
        cum_ref[i] = cum
        dt_ref[i] = dt
        whole = jnp.broadcast_to(jnp.exp(cum_t[0:8, PAGE - 1 : PAGE]), (8, LANES)) * alive
        for pair in range(pairs):
            scaled = (x[:, pair * LANES : (pair + 1) * LANES] * pair_columns(weight, pair)).astype(BF16)
            added = dot(scaled, b, TN)
            for k in (0, 1):
                h = 2 * pair + k
                here = slice(h * 64, (h + 1) * 64)
                state[here, :] = state[here, :] * whole[h : h + 1, :] + added[k * 64 : (k + 1) * 64, :]
        for k in range(len(starts)):
            start = starts[k]

            @pl.when((start >= first) & (start == opened))
            def _():
                before = jnp.sum(jnp.where(col == start - first - 1, cum_t, 0.0), axis=1, keepdims=True)
                opening = jnp.exp(cum_t[0:8, PAGE - 1 : PAGE] - before[0:8])
                opening = jnp.broadcast_to(opening, (8, LANES))
                for h in range(heads):
                    here = slice(h * 64, (h + 1) * 64)
                    state[here, :] = state[here, :] + opening[h : h + 1, :] * init[groups[k], here, :]

        factor[...] = factor[...] * whole
        end_ref[i] = state[...]
        factor_ref[i] = factor[...]

        @pl.when(i % per_run == per_run - 1)
        def _():
            summary_ref[i // per_run, : heads * 64, :] = state[...].astype(BF16)
            tail = jnp.concatenate([factor[...], jnp.zeros_like(factor[...])], axis=0)
            summary_ref[i // per_run, heads * 64 :, :] = tail.astype(BF16)

        return carry

    lax.fori_loop(0, chunks, one, 0)


def within_kernel(heads, tokens, sizes, ints, x_ref, b_ref, c_ref, cum_ref, dt_ref, params, init, y_ref):
    info, _, lengths, groups = views(ints, sizes)[:4]
    starts = starts_of(lengths)
    skip = head_lanes(params[8:16, 2 * N : 2 * N + LANES], heads, info)[2:3]
    skip = jnp.broadcast_to(skip, (PAGE, LANES))
    chunks = x_ref.shape[0]
    pairs = heads // 2
    row = lax.broadcasted_iota(jnp.int32, (PAGE, PAGE), 0)
    col = lax.broadcasted_iota(jnp.int32, (PAGE, PAGE), 1)
    lane = lax.broadcasted_iota(jnp.int32, (PAGE, LANES), 1)

    def one(i, carry):
        first = chunk_start(i, info, tokens)
        start_of = first_positions(first, starts, (PAGE, PAGE))
        bias = jnp.where((row >= col) & (col >= start_of - first), 0.0, -1e30)
        b, c = b_ref[i], c_ref[i]
        cum, dt = cum_ref[i], dt_ref[i]
        cum_t = cum.T
        scores = dot(c, b, NT)
        for pair in range(pairs):
            here = slice(pair * LANES, (pair + 1) * LANES)
            x = x_ref[i, :, here].astype(F32)
            scaled = x * pair_columns(dt, pair)
            mixing = []
            for h in (2 * pair, 2 * pair + 1):
                gap = cum[:, h : h + 1] + bias - cum_t[h : h + 1, :]
                mixing.append((scores * jnp.exp(gap)).astype(BF16))
            both = jnp.concatenate(
                [jnp.where(lane < 64, scaled, 0.0), jnp.where(lane < 64, 0.0, scaled)], axis=0
            ).astype(BF16)
            y = dot(jnp.concatenate(mixing, axis=1), both)
            y_ref[i, :, here] = y + pair_columns(skip, pair) * x
        for k in range(len(starts)):
            start = starts[k]

            @pl.when((start >= first) & (start < first + PAGE))
            def _():
                before = jnp.sum(jnp.where(row == start - first - 1, cum, 0.0), axis=0, keepdims=True)
                opening = jnp.exp(jnp.minimum(cum - before, 0.0))
                opening = jnp.where(start_of == start, opening, 0.0)
                for pair in range(pairs):
                    here = slice(pair * LANES, (pair + 1) * LANES)
                    read = dot(c, init[groups[k], here, :].astype(BF16), NT)
                    y_ref[i, :, here] = y_ref[i, :, here] + pair_columns(opening, pair) * read

        return carry

    lax.fori_loop(0, chunks, one, 0)


def onto(run, h, before):
    here = slice(h * 64, (h + 1) * 64)
    decay = run[run.shape[0] - 16 + h : run.shape[0] - 16 + h + 1, :].astype(F32)
    return decay * before + run[here, :].astype(F32)


def compose_kernel(heads, sizes, ints, mine, theirs, block_ref):
    info = views(ints, sizes)[0]
    low = info[4] == 0
    runs = []
    for a in range(2):
        m, q = mine[a].astype(F32), theirs[a].astype(F32)
        runs += [jnp.where(low, m, q), jnp.where(low, q, m)]
    total = runs[0]
    for run in runs[1:]:
        parts = []
        for h in range(heads):
            parts.append(onto(run, h, total[h * 64 : (h + 1) * 64, :]))
        tail = total[heads * 64 :, :] * run[heads * 64 :, :]
        total = jnp.concatenate(parts + [tail], axis=0)
    block_ref[...] = total.astype(BF16)


def finish_kernel(heads, tokens, sizes, ints, mine, theirs, entering, c_ref, cum_ref, end_ref,
                  factor_ref, y_ref, gate, params, mixed_ref, square_ref, page0, page1, page2, page3,
                  starting, state):
    info, _, lengths = views(ints, sizes)[:3]
    starts = starts_of(lengths)
    width = heads * 64
    gain = params[5:6, pl.ds(pl.multiple_of(info[0] * width, LANES), width)]
    pages = (page0, page1, page2, page3)
    chunks = c_ref.shape[0]
    per = tokens // PAGE
    per_run = chunks // 2
    pairs = heads // 2
    me, y = info[0], info[4]
    for h in range(heads):
        here = slice(h * 64, (h + 1) * 64)
        outside = entering[here, :].astype(F32)
        first = jnp.where(y == 0, outside, onto(theirs[0], h, outside))
        starting[0, here, :] = first
        second = onto(mine[0], h, first)
        third = jnp.where(y == 0, onto(theirs[0], h, second), onto(theirs[1], h, second))
        starting[1, here, :] = third
    ones = jnp.ones((8, LANES), F32)

    def one(i, carry):
        run = i // per_run

        @pl.when(i % per_run == 0)
        def _():
            state[...] = starting[run]

        q = i // per
        first = chunk_start(i, info, tokens)
        alive = (first_positions(first, starts, (PAGE, LANES)) < first).astype(F32)
        decay = jnp.exp(cum_ref[i]) * alive
        read = dot(c_ref[i], state[...].astype(BF16), NT)
        rows = pl.ds(pl.multiple_of(TILE + (i % per_run) * PAGE, TILE), PAGE)
        squares = jnp.zeros((PAGE, LANES), F32)
        for pair in range(pairs):
            here = slice(pair * LANES, (pair + 1) * LANES)
            value = y_ref[i, :, here] + pair_columns(decay, pair) * read[:, here]
            value = value * gate[run, rows, here].astype(F32)
            mixed_ref[i, :, here] = (value * gain[:, here]).astype(BF16)
            squares = squares + value * value
        square_ref[i] = dot(ones, squares, NT, HIGHEST)
        for h in range(heads):
            here = slice(h * 64, (h + 1) * 64)
            after = end_ref[i, here, :] + factor_ref[i, h : h + 1, :] * starting[run, here, :]
            state[here, :] = after
        for rel in range(4):

            @pl.when(q ^ me == rel)
            def _():
                pages[rel][i % per] = state[...].astype(BF16)

        return carry

    lax.fori_loop(0, chunks, one, 0)


def columns_kernel(sizes, count, rows, *refs):
    info = views(refs[0], sizes)[0]
    parts = refs[1 : 1 + count]
    out = refs[1 + count]
    for index in range(count):
        for place in range(4):
            seq = stored_block(index // 2, index % 2, 2 * place, info) // 2
            at = pl.multiple_of(seq * rows, TILE)
            out[pl.ds(at, rows), :] = parts[index][place * rows : (place + 1) * rows, :]


def mix_kernel(sizes, keep, ints, mixed, squares, columns, out):
    info = views(ints, sizes)[0]
    me, c = info[0], info[1]
    half = c if keep else 1 - c
    for rel in range(4):
        i = (me ^ rel) * 2 + half
        out[rel, :PAGE, :] = dot(mixed[i], columns[...], NT).astype(BF16)
        both = jnp.concatenate([squares[i], squares[i]], axis=0)
        out[rel, PAGE:, :LANES] = both.astype(BF16)
        out[rel, PAGE:, LANES:] = jnp.zeros((TILE, out.shape[2] - LANES), BF16)


def add_cores_kernel(kept, got, send_b, send_a, keep_b, keep_a):
    mid = send_b.shape[2]
    for k in (0, 1):
        total = kept[2 * k + 1, :, :mid].astype(F32) + got[2 * k + 1, :, :mid].astype(F32)
        send_b[k] = total.astype(BF16)
        keep_b[k] = kept[2 * k, :, :mid].astype(F32) + got[2 * k, :, :mid].astype(F32)
        total = kept[k + 2, :PAGE, mid:].astype(F32) + got[k + 2, :PAGE, mid:].astype(F32)
        send_a[k] = total.astype(BF16)
        keep_a[k] = kept[k, :PAGE, mid:].astype(F32) + got[k, :PAGE, mid:].astype(F32)


def add_second_kernel(keep_b, got_b, keep_a, got_a, send_a, send_b, left, right):
    send_a[...] = (keep_b[1] + got_b[1].astype(F32)).astype(BF16)
    left[...] = keep_b[0] + got_b[0].astype(F32)
    send_b[...] = (keep_a[1] + got_a[1].astype(F32)).astype(BF16)
    right[...] = keep_a[0] + got_a[0].astype(F32)


def add_last_kernel(channels, left, got_left, right, got_right, out):
    mid = left.shape[1]
    squares = left[PAGE : PAGE + 1, :LANES] + got_left[PAGE:, :LANES].astype(F32)[0:1]
    row = lax.broadcasted_iota(jnp.int32, (PAGE, PAGE), 0)
    col = lax.broadcasted_iota(jnp.int32, (PAGE, PAGE), 1)
    squares = jnp.sum(jnp.where(row == col, squares, 0.0), axis=1, keepdims=True)
    scale = lax.rsqrt(squares / channels + EPSILON)
    out[:, :mid] = ((left[:PAGE] + got_left[:PAGE, :].astype(F32)) * scale).astype(BF16)
    out[:, mid:] = ((right[...] + got_right[...].astype(F32)) * scale).astype(BF16)


def page_kernel(sizes, ints, own, from_b, from_a, from_d, out):
    info, _, _, _, table = views(ints, sizes)
    me, seq, per = info[0], info[6], own.shape[0]
    for k in range(per):
        slot = table[k] - seq * per
        for rel, source in enumerate((own, from_b, from_a, from_d)):
            out[slot, me ^ rel] = source[k].astype(F32)


def round_t(x, count):
    return lax.ppermute(x, "t", [(i, (i + 1) % count) for i in range(count)])


def weight_parts(part, count):
    parts = []
    for s in range(count):
        part = round_t(part, count) if s > 0 else part
        parts += [part, swap(part, "y")]
    return parts


def in_order(parts, index):
    stacked = jnp.stack(parts)
    blocks = stacked.reshape((-1, stacked.shape[1] * len(parts) // index.shape[0], stacked.shape[2]))
    return jnp.zeros_like(blocks).at[index].set(blocks).reshape(-1, stacked.shape[2])


def on_device(
    hidden_in,
    gate_proj,
    inner_proj,
    small_proj,
    row_layout,
    conv_inner,
    conv_shared,
    bias_inner,
    bias_shared,
    dt_bias,
    decay_log,
    skip_gain,
    norm_gain,
    out_proj,
    prompt_lengths,
    group_map,
    init_states,
    page_table,
):
    tokens, model = hidden_in.shape
    rows = gate_proj.shape[0]
    half_heads = dt_bias.shape[0]
    heads = half_heads // 4
    inner = conv_inner.shape[1]
    head_dim = inner // half_heads
    width = heads * head_dim
    t_count = lax.axis_size("t")
    t, a, y, b, c = (lax.axis_index(name) for name in ("t", "a", "y", "b", "tp"))
    me = a * 2 + b
    seq = ((t * 2 + a) * 2 + y) * 2 + b
    info = jnp.stack([me, c, 0 * c, t, y, 0 * c + t_count, seq, 0 * c]).astype(jnp.int32)
    pieces = [info, row_layout, prompt_lengths, group_map, page_table]
    sizes = tuple(piece.shape[0] for piece in pieces)
    ints = jnp.concatenate(pieces)
    per_head = jnp.pad(jnp.stack([dt_bias, decay_log, skip_gain]), ((0, 5), (0, LANES - half_heads)))
    top = jnp.concatenate([conv_inner, bias_inner[None], norm_gain[None]])
    low = jnp.concatenate([conv_shared, bias_shared[None]])
    low = jnp.concatenate([jnp.pad(low, ((0, 3), (0, 0))), per_head], axis=1)
    params = jnp.concatenate(
        [jnp.pad(top, ((0, 2), (0, 0))), jnp.pad(low, ((0, 0), (0, inner - low.shape[1])))]
    )
    count = 2 * t_count

    wide = width + N + LANES
    aligned = rows % TILE == 0
    inner_send = call(
        functools.partial(pack_kernel, heads),
        "pack_rows",
        shape((8, rows, wide + width), BF16),
        [inner_proj, small_proj, gate_proj],
    )
    inner_got = lax.all_to_all(inner_send, GROUP, 0, 0, tiled=True)

    size = lax.axis_size(SEQ)
    half = tokens // 2
    mine = lax.dynamic_slice_in_dim(hidden_in, c * half, half, 0)
    mine_b, mine_a = swap(mine, "b"), swap(mine, "a")
    tail = hidden_in[tokens - TILE :]
    halo0 = lax.ppermute(tail, SEQ, [(i, i + 1) for i in range(1, size - 1, 2)])
    halo1 = lax.ppermute(tail, SEQ, [(i, i + 2) for i in range(1, size - 2, 2)])

    if aligned:
        part, low, high, gate_part = call(
            repack_kernel,
            "repack_inner",
            (
                shape((8 * rows + TILE, width + N), BF16),
                shape((4 * rows, width + N), BF16),
                shape((4 * rows + TILE, width + N), BF16),
                shape((8 * rows, width), BF16),
            ),
            [inner_got],
        )
        marks, inner_parts = [(0, 0, 0), (0, 1, 0)], [part, swap(part, "y")]
        for s in range(1, t_count):
            low, high = round_t(low, t_count), round_t(high, t_count)
            marks += [(s, 0, 0), (s, 0, 4), (s, 1, 0), (s, 1, 4)]
            inner_parts += [low, high, swap(low, "y"), swap(high, "y")]
        ready = [part]
    else:
        marks = None
        index = [stored_block(s, dy, p, info) for s in range(t_count) for dy in (0, 1) for p in range(8)]
        index = row_layout[jnp.stack(index)]
        inner_got = inner_got.reshape(8 * rows, wide + width)
        inner_parts = [in_order(weight_parts(inner_got[:, :wide], t_count), index)]
        gate_part = inner_got[:, wide:]
        ready = high = None

    over_b, over_a = call(
        functools.partial(forward_kernel, sizes),
        "forward_rows",
        (shape((half // 2, model), BF16), shape((half // 2 + TILE, model), BF16)),
        [ints, mine_b, mine_a, halo0, halo1],
        after=ready or (),
    )
    mine_d0, mine_d1 = swap(over_b, "b"), swap(over_a, "a")
    rows_in = [mine_b, mine_a, mine_d0, mine_d1]
    hidden = call(
        functools.partial(assemble_kernel, sizes),
        "assemble_rows",
        shape((2, TILE + 2 * tokens, model), BF16),
        [ints, hidden_in, *rows_in, *[swap(x, "tp") for x in rows_in], halo0, halo1],
        us=2,
    )
    if aligned:
        gate_part = call(copy_kernel, "gate_part", shape(gate_part.shape, BF16), [gate_part], after=[high])
    gate_parts = weight_parts(gate_part, t_count)
    out_send = call(
        pack_out_kernel,
        "pack_out",
        shape((4, out_proj.shape[1], width), BF16),
        [out_proj.T],
        after=[high] if aligned else (),
    )
    out_got = lax.all_to_all(out_send, ("a", "b"), 0, 0, tiled=True)
    out_rows = out_proj.shape[1]
    out_got = out_got.reshape(4 * out_rows, width)
    if out_rows % TILE == 0:
        out_got = call(
            copy_kernel, "out_part", shape(out_got.shape, BF16), [out_got], after=[gate_parts[-2]]
        )
    out_parts = weight_parts(out_got, t_count)
    if not aligned:
        gate_parts = [in_order(gate_parts, index)]
    if out_rows % TILE == 0:
        columns = call(
            functools.partial(columns_kernel, sizes, count, out_rows),
            "columns",
            shape((model, width), BF16),
            [ints, *out_parts],
        )
    else:
        index = [
            stored_block(s, dy, 2 * p, info) // 2
            for s in range(t_count)
            for dy in (0, 1)
            for p in range(4)
        ]
        columns = in_order(out_parts, jnp.stack(index))

    long = TILE + 2 * tokens
    raw, shared, step = call(
        functools.partial(inner_kernel, sizes, marks, rows),
        "inner_projection",
        (
            shape((2, long, width), BF16),
            shape((2, long, LANES), BF16),
            shape((2, long, LANES), F32),
        ),
        [ints, hidden, *inner_parts],
        [pltpu.VMEM((model, wide), BF16)] if marks else [], us=4.3
    )
    shared_other = swap(shared, "tp")
    init = lax.dynamic_slice_in_dim(init_states, me * heads, heads, 1)
    init = init.reshape(init.shape[0], width, N)
    chunks = 4 * tokens // PAGE
    x, b_in, c_in, cum, dt, ends, factors, summary = call(
        functools.partial(state_kernel, heads, tokens, sizes),
        "states",
        (
            shape((chunks, PAGE, width), BF16),
            shape((chunks, PAGE, N), BF16),
            shape((chunks, PAGE, N), BF16),
            shape((chunks, PAGE, LANES), F32),
            shape((chunks, PAGE, LANES), F32),
            shape((chunks, width, N), F32),
            shape((chunks, 8, N), F32),
            shape((2, width + 16, N), BF16),
        ),
        [ints, raw, shared, shared_other, step, params, init],
        [pltpu.VMEM((width, N), F32), pltpu.VMEM((8, N), F32)], us=9.3
    )
    theirs = swap(summary, "y")
    block = call(
        functools.partial(compose_kernel, heads, sizes),
        "compose",
        shape((width + 16, N), BF16),
        [ints, summary, theirs],
    )
    onward = [(i, i + 1) for i in range(t_count - 1)]
    gate_marks = [(s, dy, 0) for s in range(t_count) for dy in (0, 1)] if aligned else None
    gate = call(
        functools.partial(gate_kernel, sizes, gate_marks, rows),
        "gate_projection",
        shape((2, long, width), BF16),
        [ints, hidden, *gate_parts],
        [pltpu.VMEM((model, width), BF16)] if aligned else [],
        after=[block], us=3
    )
    block = lax.ppermute(block, "t", onward)
    entering = block
    if t_count > 2:
        total = block[:width].astype(F32).reshape(heads, head_dim, N)
        decay = block[width : width + heads, None, :].astype(F32)
        for _ in range(t_count - 2):
            block = lax.ppermute(block, "t", onward)
            total = total + decay * block[:width].astype(F32).reshape(heads, head_dim, N)
            decay = decay * block[width : width + heads, None, :].astype(F32)
        entering = total.reshape(width, N)
    y_within = call(
        functools.partial(within_kernel, heads, tokens, sizes),
        "within_chunks",
        shape((chunks, PAGE, width), F32),
        [ints, x, b_in, c_in, cum, dt, params, init], us=5.4
    )
    mixed, squares, *pages = call(
        functools.partial(finish_kernel, heads, tokens, sizes),
        "finish",
        (
            shape((chunks, PAGE, width), BF16),
            shape((chunks, 8, PAGE), F32),
            *[shape((tokens // PAGE, width, N), BF16)] * 4,
        ),
        [ints, summary, theirs, entering, c_in, cum, ends, factors, y_within, gate, params],
        [pltpu.VMEM((2, width, N), F32), pltpu.VMEM((width, N), F32)], us=4.8
    )

    across = [(i, i ^ 3) for i in range(4)]
    got = [pages[0], swap(pages[1], "b"), swap(pages[2], "a"), lax.ppermute(pages[3], ("a", "b"), across)]
    per = tokens // PAGE
    state_pages = call(
        functools.partial(page_kernel, sizes), "pages", shape((per, 4, width, N), F32), [ints, *got], us=1.8
    ).reshape(per, half_heads, head_dim, N)

    dims = shape((4, PAGE + TILE, model), BF16)
    sent = call(functools.partial(mix_kernel, sizes, False), "mix_send", dims, [ints, mixed, squares, columns], us=2.1)
    got = swap(sent, "tp")
    kept = call(functools.partial(mix_kernel, sizes, True), "mix_keep", dims, [ints, mixed, squares, columns], us=2.1)
    mid = model // 2
    send_b, send_a, keep_b, keep_a = call(
        add_cores_kernel,
        "add_cores",
        (
            shape((2, PAGE + TILE, mid), BF16),
            shape((2, PAGE, mid), BF16),
            shape((2, PAGE + TILE, mid), F32),
            shape((2, PAGE, mid), F32),
        ),
        [kept, got],
    )
    got_b, got_a = swap(send_b, "b"), swap(send_a, "a")
    send_a, send_b, left, right = call(
        add_second_kernel,
        "add_second",
        (
            shape((PAGE + TILE, mid), BF16),
            shape((PAGE, mid), BF16),
            shape((PAGE + TILE, mid), F32),
            shape((PAGE, mid), F32),
        ),
        [keep_b, got_b, keep_a, got_a],
    )
    got_left, got_right = swap(send_a, "a"), swap(send_b, "b")
    mixed_out = call(
        functools.partial(add_last_kernel, float(2 * inner)),
        "add_last",
        shape((PAGE, model), BF16),
        [left, got_left, right, got_right],
    )
    return (mixed_out, state_pages)


def solution(mesh):
    count = mesh.shape["seq"]
    fine = Mesh(mesh.devices.reshape(count // 8, 2, 2, 2, 2), SEQ + ("tp",))
    placed = (
        P(SEQ, None),
        P(SEQ + ("tp",), None),
        P(SEQ + ("tp",), None),
        P(SEQ + ("tp",), None),
        P(),
        P(None, "tp"),
        P(),
        P("tp"),
        P(),
        P("tp"),
        P("tp"),
        P("tp"),
        P("tp"),
        P("tp", SEQ),
        P(),
        P(),
        P(None, "tp", None, None),
        P(SEQ),
    )
    return jax.shard_map(
        on_device,
        mesh=fine,
        in_specs=placed,
        out_specs=(P(SEQ + ("tp",), None), P(SEQ, "tp", None, None)),
        check_vma=False,
    )
```

time: 218 us -> 154 us (0.71)
  local copies, waits for them, and re-layouts: 44 us -> 14.8 us
  waiting for transfers between devices: 55.3 us -> 36.6 us
  blocking collectives: 17.3 us -> 0 us
  other arithmetic: 11.1 us -> 0.69 us
  starting transfers between devices: 50 us -> 58.9 us
  Pallas kernels: 36.6 us -> 41.3 us
    psum x1 -> x0, blocking collectives: 17.3 us -> none  [on_device(): squares = lax.psum(squares[:, 0, :], GROUP)]
    ppermute x22 -> x24, waiting for transfers between devices: 45.7 us -> 33.1 us  [swap(): return lax.ppermute(x, axis, [(0, 1), (1, 0)])]
    ppermute x4 -> x6, waiting for transfers between devices: 9.52 us -> 2.03 us  [the longest x4 2.02 us: round_t(): return lax.ppermute(x, 't', [(i, (i + 1) % count) for i in range(count)])]
    slice x13 -> x1, local copies, waits for them, and re-layouts: 8.78 us -> 1.41 us  [on_device(): tail = hidden_in[tokens - TILE:]]
    all_to_all x1, starting transfers between devices: 4.09 us -> 10.2 us  [on_device(): out_got = lax.all_to_all(out_send, ('a', 'b'), 0, 0, tiled=True)]
    unnamed x97 -> x70, local copies, waits for them, and re-layouts: 15.3 us -> 9.88 us
    pallas_call x10 -> x20, Pallas kernels: 36.6 us -> 41.3 us  [call(): pl.pallas_call(kernel, name=name, out_shape=out_shape, in_specs=specs, ou...]
    dynamic_slice x7 -> x1, local copies, waits for them, and re-layouts: 6.35 us -> 1.77 us  [on_device(): mine = lax.dynamic_slice_in_dim(hidden_in, c * half, half, 0)]
  transfers between devices with their start and end apart: 31 -> 34, of which waited for: 11 -> 13; matrix products, arithmetic and copies ran while one was open for 18% -> 4% of each run, Pallas kernels for 14% -> 24%
where the time goes in v2:
time: 154 us; the launch traced here: 153 us
  starting transfers between devices  58.9 us (38%)
  Pallas kernels  41.3 us (27%)
  waiting for transfers between devices  36.6 us (24%)
  local copies, waits for them, and re-layouts  14.8 us (10%)
    pallas_call x20, Pallas kernels, call(): pl.pallas_call(kernel, name=name, out_shape=out_shape, in_specs=specs, ou...  41.3 us
    ppermute x24, waiting for transfers between devices, swap(): return lax.ppermute(x, axis, [(0, 1), (1, 0)])  33.1 us
    ppermute x24, starting transfers between devices, swap(): return lax.ppermute(x, axis, [(0, 1), (1, 0)])  21.9 us
    ppermute x4, starting transfers between devices, round_t(): return lax.ppermute(x, 't', [(i, (i + 1) % count) for i in range(count)])  10.6 us
    all_to_all x1, starting transfers between devices, on_device(): out_got = lax.all_to_all(out_send, ('a', 'b'), 0, 0, tiled=True)  10.2 us
    unnamed x70, local copies, waits for them, and re-layouts  9.88 us
    all_to_all x1, starting transfers between devices, on_device(): inner_got = lax.all_to_all(inner_send, GROUP, 0, 0, tiled=True)  5.36 us
    ppermute x1, starting transfers between devices, on_device(): block = lax.ppermute(block, 't', onward)  5.24 us
  transfers between devices with their start and end apart: 34, of which 13 were waited for; matrix products, arithmetic and copies ran while one was open for 4% of the time, Pallas kernels for 24%

profile of v2, /device:TPU:0, one launch (start us, length us, event | category | flops | bytes accessed | tf_op | source)
XLA Modules:
  0.0 153.3 jit_solution(6193800166733984478)
XLA Ops:
  0.7 1.2 copy-done.5
  1.9 1.1 copy-done.6
  2.9 0.9 copy-done.13
  3.9 0.9 copy-done.1
  4.8 5.4 %all-to-all-start = ((bf16[8,48,1024]{2,1,0:T(8,128)(2,1)}), bf16[8,48,1024]{2,1,0:T(8,128)(2,1)}, u32[]{:S(2)}, u32[]{:S(2)}) async-start(bf16[8,48,1024]{2,1,0:T(8,128)(2,1)} %copy-done.1), calls=%async_computation | async-start | bytes 1572864 | tf_op jit(solution)/shard_map/all_to_all | solution.py:639
  10.2 1.8 %constant_dynamic-slice_fusion.1 = bf16[128,1536]{1,0:T(8,128)(2,1)} fusion(bf16[256,1536]{1,0:T(8,128)(2,1)} %refs_1_.3, s32[]{:T(128)S(6)} %select_n.6), kind=kLoop, calls=%fused_computation.13 | loop fusion | bytes 786436 | tf_op jit(solution)/shard_map/dynamic_slice | solution.py:643
  11.9 2.0 %collective-permute-start = (bf16[128,1536]{1,0:T(8,128)(2,1)}, bf16[128,1536]{1,0:T(8,128)(2,1)S(1)}, u32[]{:S(2)}, u32[]{:S(2)}) collective-permute-start(bf16[128,1536]{1,0:T(8,128)(2,1)} %constant_dynamic-slice_fusion.1), channel_id=1, source_target_pairs={{0,2},{2,0},{1,3},{3,1},{4,6},{6,4},{5,7},{7,5},{8,10},{10,8},{9,1... | collective-permute-start | bytes 1179656 | tf_op jit(solution)/shard_map/ppermute | solution.py:61
  14.0 1.5 collective-permute-start.1
  15.4 1.4 slice.3
  16.8 1.3 collective-permute-start.2
  18.1 1.3 collective-permute-start.3
  19.4 0.7 concatenate.15.refs_0_
  20.1 10.6 %collective-permute-done.refs_1_.refs_2_ = bf16[128,1536]{1,0:T(8,128)(2,1)S(1)} collective-permute-done((bf16[128,1536]{1,0:T(8,128)(2,1)}, bf16[128,1536]{1,0:T(8,128)(2,1)S(1)}, u32[]{:S(2)}, u32[]{:S(2)}) %collective-permute-start) | collective-permute-done | bytes 393248 | tf_op jit(solution)/shard_map/ppermute | solution.py:61
  30.7 2.2 %repack_inner.1 = (bf16[400,512]{1,0:T(8,128)(2,1)}, bf16[192,512]{1,0:T(8,128)(2,1)}, bf16[208,512]{1,0:T(8,128)(2,1)S(1)}, bf16[384,384]{1,0:T(8,128)(2,1)S(1)}) custom-call(bf16[8,48,1024]{2,1,0:T(8,128)(2,1)} %all-to-all-done.refs_0_), custom_call_target="tpu_custom_call" | custom-call | flops 1000000000 | bytes 3000000 | tf_op jit(solution)/shard_map/repack_inner/pallas_call | solution.py:34
  32.9 0.7 copy-done.16
  33.7 1.1 forward_rows.1
  34.9 1.5 %collective-permute-start.5 = (bf16[80,1536]{1,0:T(8,128)(2,1)S(1)}, bf16[80,1536]{1,0:T(8,128)(2,1)}, u32[]{:S(2)}, u32[]{:S(2)}) collective-permute-start(bf16[80,1536]{1,0:T(8,128)(2,1)S(1)} %get-tuple-element.35), channel_id=1, source_target_pairs={{0,8},{8,0},{1,9},{9,1},{2,10},{10,2},{3,11},{11,3},{4,12},{12,4},... | collective-permute-start | bytes 737288 | tf_op jit(solution)/shard_map/ppermute | solution.py:61
  36.5 0.7 collective-permute-start.4
  37.2 2.6 %collective-permute-start.12 = (bf16[208,512]{1,0:T(8,128)(2,1)S(1)}, bf16[208,512]{1,0:T(8,128)(2,1)S(1)}, u32[]{:S(2)}, u32[]{:S(2)}) collective-permute-start(bf16[208,512]{1,0:T(8,128)(2,1)S(1)} %get-tuple-element.37), channel_id=1, source_target_pairs={{0,16},{16,0},{1,17},{17,1},{2,18},{18,2},{3,19},{19,3},{4,20},{20... | collective-permute-start | bytes 638984 | tf_op jit(solution)/shard_map/ppermute | solution.py:570
  39.9 1.4 collective-permute-start.10
  41.3 2.2 %collective-permute-done.4.refs_4_ = bf16[64,1536]{1,0:T(8,128)(2,1)} collective-permute-done((bf16[64,1536]{1,0:T(8,128)(2,1)S(1)}, bf16[64,1536]{1,0:T(8,128)(2,1)}, u32[]{:S(2)}, u32[]{:S(2)}) %collective-permute-start.4) | collective-permute-done | bytes 196640 | tf_op jit(solution)/shard_map/ppermute | solution.py:61
  43.5 2.9 %collective-permute-start.11 = (bf16[192,512]{1,0:T(8,128)(2,1)}, bf16[192,512]{1,0:T(8,128)(2,1)}, u32[]{:S(2)}, u32[]{:S(2)}) collective-permute-start(bf16[192,512]{1,0:T(8,128)(2,1)} %get-tuple-element.36), channel_id=1, source_target_pairs={{0,16},{16,0},{1,17},{17,1},{2,18},{18,2},{3,19},{19,3},{4,20},{20... | collective-permute-start | bytes 589832 | tf_op jit(solution)/shard_map/ppermute | solution.py:570
  46.4 0.9 collective-permute-done.12.refs_5_.refs_1_
  48.6 0.7 copy-done.3
  49.3 0.7 copy-done.10
  50.1 10.2 %all-to-all-start.1 = ((bf16[4,96,384]{2,1,0:T(8,128)(2,1)}), bf16[4,96,384]{2,1,0:T(8,128)(2,1)S(1)}, u32[]{:S(2)}, u32[]{:S(2)}) async-start(bf16[4,96,384]{2,1,0:T(8,128)(2,1)} %copy-done.3), calls=%async_computation.1 | async-start | bytes 589824 | tf_op jit(solution)/shard_map/all_to_all | solution.py:702
  60.3 1.6 %collective-permute-start.13 = (bf16[192,512]{1,0:T(8,128)(2,1)}, bf16[192,512]{1,0:T(8,128)(2,1)S(1)}, u32[]{:S(2)}, u32[]{:S(2)}) collective-permute-start(bf16[192,512]{1,0:T(8,128)(2,1)} %collective-permute-done.11.refs_4_), channel_id=1, source_target_pairs={{0,4},{4,0},{1,5},{5,1},{2,6},{6,2},{3,7},{7,3},{8,12},{12,8},{9,1... | collective-permute-start | bytes 589832 | tf_op jit(solution)/shard_map/ppermute | solution.py:61
  62.3 1.0 copy-done.11
  63.3 1.0 copy-done.17
  64.2 0.7 gate_part.1.refs_2_
  65.0 2.9 %collective-permute-start.19 = (bf16[384,384]{1,0:T(8,128)(2,1)}, bf16[384,384]{1,0:T(8,128)(2,1)}, u32[]{:S(2)}, u32[]{:S(2)}) collective-permute-start(bf16[384,384]{1,0:T(8,128)(2,1)} %gate_part.1.refs_2_), channel_id=1, source_target_pairs={{0,16},{16,0},{1,17},{17,1},{2,18},{18,2},{3,19},{19,3},{4,20},{20... | collective-permute-start | bytes 884744 | tf_op jit(solution)/shard_map/ppermute | solution.py:570
  68.0 1.8 %assemble_rows.1.refs_1_ = bf16[2,528,1536]{2,1,0:T(8,128)(2,1)S(1)} custom-call(s32[58]{0:T(128)S(1)} %concatenate.15.refs_0_, bf16[256,1536]{1,0:T(8,128)(2,1)S(1)} %copy-done.4, bf16[128,1536]{1,0:T(8,128)(2,1)S(1)} %copy-done.9, bf16[128,1536]{1,0:T(8,128)(2,1)} %collective-permute-done.1.refs_2_.refs_3_, ...), custom_call_target="tpu_custom_call" | custom-call | flops 2000000000 | bytes 6000000 | tf_op jit(solution)/shard_map/assemble_rows/pallas_call | solution.py:34
  69.8 1.8 %collective-permute-done.14.refs_7_ = bf16[208,512]{1,0:T(8,128)(2,1)S(1)} collective-permute-done((bf16[208,512]{1,0:T(8,128)(2,1)}, bf16[208,512]{1,0:T(8,128)(2,1)S(1)}, u32[]{:S(2)}, u32[]{:S(2)}) %collective-permute-start.14) | collective-permute-done | bytes 213024 | tf_op jit(solution)/shard_map/ppermute | solution.py:61
  71.6 4.1 %inner_projection.1 = (bf16[2,528,384]{2,1,0:T(8,128)(2,1)S(1)}, bf16[2,528,128]{2,1,0:T(8,128)(2,1)}, f32[2,528,128]{2,1,0:T(8,128)S(1)}) custom-call(s32[58]{0:T(128)S(1)} %concatenate.15.refs_0_, bf16[2,528,1536]{2,1,0:T(8,128)(2,1)S(1)} %assemble_rows.1.refs_1_, bf16[400,512]{1,0:T(8,128)(2,1)} %get-tuple-element.33.refs_5_.refs_2_, ...), custom_call_target="tpu_custom_call" | custom-call | flops 4300000256 | bytes 12900000 | tf_op jit(solution)/shard_map/inner_projection/pallas_call | solution.py:34
  75.8 0.9 copy-done.18
  76.6 0.8 copy-done.20
  77.5 1.0 constant_dynamic-slice_fusion
  78.5 1.6 %collective-permute-start.18 = (bf16[384,384]{1,0:T(8,128)(2,1)}, bf16[384,384]{1,0:T(8,128)(2,1)}, u32[]{:S(2)}, u32[]{:S(2)}) collective-permute-start(bf16[384,384]{1,0:T(8,128)(2,1)} %gate_part.1.refs_2_), channel_id=1, source_target_pairs={{0,4},{4,0},{1,5},{5,1},{2,6},{6,2},{3,7},{7,3},{8,12},{12,8},{9,1... | collective-permute-start | bytes 884744 | tf_op jit(solution)/shard_map/ppermute | solution.py:61
  80.1 1.1 collective-permute-done.19.refs_4_.refs_1_
  81.2 1.7 %collective-permute-start.20 = (bf16[384,384]{1,0:T(8,128)(2,1)}, bf16[384,384]{1,0:T(8,128)(2,1)}, u32[]{:S(2)}, u32[]{:S(2)}) collective-permute-start(bf16[384,384]{1,0:T(8,128)(2,1)} %collective-permute-done.19.refs_4_.refs_1_), channel_id=1, source_target_pairs={{0,4},{4,0},{1,5},{5,1},{2,6},{6,2},{3,7},{7,3},{8,12},{12,8},{9,1... | collective-permute-start | bytes 884744 | tf_op jit(solution)/shard_map/ppermute | solution.py:61
  83.3 2.2 %collective-permute-start.22 = (bf16[384,384]{1,0:T(8,128)(2,1)S(1)}, bf16[384,384]{1,0:T(8,128)(2,1)S(1)}, u32[]{:S(2)}, u32[]{:S(2)}) collective-permute-start(bf16[384,384]{1,0:T(8,128)(2,1)S(1)} %out_part.1.refs_1_), channel_id=1, source_target_pairs={{0,16},{16,0},{1,17},{17,1},{2,18},{18,2},{3,19},{19,3},{4,20},{20... | collective-permute-start | bytes 884744 | tf_op jit(solution)/shard_map/ppermute | solution.py:570
  85.5 9.1 %states.1 = (bf16[8,128,384]{2,1,0:T(8,128)(2,1)S(1)}, bf16[8,128,128]{2,1,0:T(8,128)(2,1)S(1)}, bf16[8,128,128]{2,1,0:T(8,128)(2,1)S(1)}, f32[8,128,128]{2,1,0:...) custom-call(s32[58]{0:T(128)S(1)} %concatenate.15.refs_0_, ...), custom_call_target="tpu_custom_call" | custom-call | flops 9299999744 | bytes 27900000 | tf_op jit(solution)/shard_map/states/pallas_call | solution.py:34
  94.8 5.2 %within_chunks.1.refs_8_ = f32[8,128,384]{2,1,0:T(8,128)S(1)} custom-call(s32[58]{0:T(128)S(1)} %concatenate.15.refs_0_, bf16[8,128,384]{2,1,0:T(8,128)(2,1)S(1)} %get-tuple-element.46.refs_1_, bf16[8,128,128]{2,1,0:T(8,128)(2,1)S(1)} %get-tuple-element.47.refs_2_, bf16[8,128,128]{2,1,0:T(8,128)(2,1)S(1)} %get-tuple-element.42.refs_3_.refs_4_, ...), custom_call_target="tpu_custom_call" | custom-call | flops 5400000000 | bytes 16200000 | tf_op jit(solution)/shard_map/within_chunks/pallas_call | solution.py:34
  100.0 1.8 %collective-permute-start.23 = (bf16[384,384]{1,0:T(8,128)(2,1)S(1)}, bf16[384,384]{1,0:T(8,128)(2,1)S(1)}, u32[]{:S(2)}, u32[]{:S(2)}) collective-permute-start(bf16[384,384]{1,0:T(8,128)(2,1)S(1)} %collective-permute-done.22.refs_3_), channel_id=1, source_target_pairs={{0,4},{4,0},{1,5},{5,1},{2,6},{6,2},{3,7},{7,3},{8,12},{12,8},{9,1... | collective-permute-start | bytes 884744 | tf_op jit(solution)/shard_map/ppermute | solution.py:61
  101.8 3.7 %collective-permute-done.16.refs_2_ = bf16[2,400,128]{2,1,0:T(8,128)(2,1)S(1)} collective-permute-done((bf16[2,400,128]{2,1,0:T(8,128)(2,1)S(1)}, bf16[2,400,128]{2,1,0:T(8,128)(2,1)S(1)}, u32[]{:S(2)}, u32[]{:S(2)}) %collective-permute-start.16) | collective-permute-done | bytes 204832 | tf_op jit(solution)/shard_map/ppermute | solution.py:61
  106.2 5.2 %collective-permute-start.17 = (bf16[400,128]{1,0:T(8,128)(2,1)S(1)}, bf16[400,128]{1,0:T(8,128)(2,1)S(1)}, u32[]{:S(2)}, u32[]{:S(2)}) collective-permute-start(bf16[400,128]{1,0:T(8,128)(2,1)S(1)} %compose.1.refs_6_), channel_id=1, source_target_pairs={{0,16},{1,17},{2,18},{3,19},{4,20},{5,21},{6,22},{7,23},{8,24},{9,... | collective-permute-start | bytes 307208 | tf_op jit(solution)/shard_map/ppermute | solution.py:777
  111.4 3.2 %gate_projection.1.refs_9_ = bf16[2,528,384]{2,1,0:T(8,128)(2,1)S(1)} custom-call(s32[58]{0:T(128)S(1)} %concatenate.15.refs_0_, bf16[2,528,1536]{2,1,0:T(8,128)(2,1)S(1)} %copy-done.15, bf16[384,384]{1,0:T(8,128)(2,1)} %gate_part.1.refs_2_, bf16[384,384]{1,0:T(8,128)(2,1)} %collective-permute-done.18.refs_3_, ...), custom_call_target="tpu_custom_call" | custom-call | flops 3000000000 | bytes 9000000 | tf_op jit(solution)/shard_map/gate_projection/pallas_call | solution.py:34
  114.7 4.8 %finish.1 = (bf16[8,128,384]{2,1,0:T(8,128)(2,1)S(1)}, f32[8,8,128]{2,1,0:T(8,128)S(1)}, bf16[2,384,128]{2,1,0:T(8,128)(2,1)S(1)}, bf16[2,384,128]{2,1,0:T(8,128...) custom-call(s32[58]{0:T(128)S(1)} %concatenate.15.refs_0_, ...), custom_call_target="tpu_custom_call" | custom-call | flops 4800000000 | bytes 14400000 | tf_op jit(solution)/shard_map/finish/pallas_call | solution.py:34
  119.6 0.7 columns.1.refs_3_
  120.3 2.1 %mix_send.1 = bf16[4,144,1536]{2,1,0:T(8,128)(2,1)S(1)} custom-call(s32[58]{0:T(128)S(1)} %concatenate.15.refs_0_, bf16[8,128,384]{2,1,0:T(8,128)(2,1)S(1)} %get-tuple-element.50.refs_1_, f32[8,8,128]{2,1,0:T(8,128)S(1)} %get-tuple-element.51.refs_2_, bf16[1536,384]{1,0:T(8,128)(2,1)S(1)} %columns.1.refs_3_), custom_call_target="tpu_custom_call" | custom-call | flops 2100000000 | bytes 6300000 | tf_op jit(solution)/shard_map/mix_send/pallas_call | solution.py:34
  122.5 2.1 %mix_keep.1.refs_0_ = bf16[4,144,1536]{2,1,0:T(8,128)(2,1)S(1)} custom-call(s32[58]{0:T(128)S(1)} %concatenate.15.refs_0_, bf16[8,128,384]{2,1,0:T(8,128)(2,1)S(1)} %get-tuple-element.50.refs_1_, f32[8,8,128]{2,1,0:T(8,128)S(1)} %get-tuple-element.51.refs_2_, bf16[1536,384]{1,0:T(8,128)(2,1)S(1)} %columns.1.refs_3_), custom_call_target="tpu_custom_call" | custom-call | flops 2100000000 | bytes 6300000 | tf_op jit(solution)/shard_map/mix_keep/pallas_call | solution.py:34
  124.6 1.5 collective-permute-done.24.refs_1_
  126.5 1.8 %collective-permute-start.25 = (bf16[2,144,768]{2,1,0:T(8,128)(2,1)S(1)}, bf16[2,144,768]{2,1,0:T(8,128)(2,1)S(1)}, u32[]{:S(2)}, u32[]{:S(2)}) collective-permute-start(bf16[2,144,768]{2,1,0:T(8,128)(2,1)S(1)} %get-tuple-element.53), channel_id=1, source_target_pairs={{0,2},{2,0},{1,3},{3,1},{4,6},{6,4},{5,7},{7,5},{8,10},{10,8},{9,1... | collective-permute-start | bytes 1327112 | tf_op jit(solution)/shard_map/ppermute | solution.py:61
  128.3 1.8 %collective-permute-start.26 = (bf16[2,128,768]{2,1,0:T(8,128)(2,1)S(1)}, bf16[2,128,768]{2,1,0:T(8,128)(2,1)S(1)}, u32[]{:S(2)}, u32[]{:S(2)}) collective-permute-start(bf16[2,128,768]{2,1,0:T(8,128)(2,1)S(1)} %get-tuple-element.55), channel_id=1, source_target_pairs={{0,8},{8,0},{1,9},{9,1},{2,10},{10,2},{3,11},{11,3},{4,12},{12,4},... | collective-permute-start | bytes 1179656 | tf_op jit(solution)/shard_map/ppermute | solution.py:61
  130.6 3.0 %collective-permute-start.31 = (bf16[2,384,128]{2,1,0:T(8,128)(2,1)S(1)}, bf16[2,384,128]{2,1,0:T(8,128)(2,1)S(1)}, u32[]{:S(2)}, u32[]{:S(2)}) collective-permute-start(bf16[2,384,128]{2,1,0:T(8,128)(2,1)S(1)} %get-tuple-element.63), channel_id=1, source_target_pairs={{0,10},{2,8},{8,2},{10,0},{1,11},{3,9},{9,3},{11,1},{4,14},{6,12},... | collective-permute-start | bytes 589832 | tf_op jit(solution)/shard_map/ppermute | solution.py:806
  133.6 6.7 %collective-permute-done.26.refs_3_ = bf16[2,128,768]{2,1,0:T(8,128)(2,1)S(1)} collective-permute-done((bf16[2,128,768]{2,1,0:T(8,128)(2,1)S(1)}, bf16[2,128,768]{2,1,0:T(8,128)(2,1)S(1)}, u32[]{:S(2)}, u32[]{:S(2)}) %collective-permute-start.26) | collective-permute-done | bytes 393248 | tf_op jit(solution)/shard_map/ppermute | solution.py:61
  140.5 1.8 %collective-permute-start.27 = (bf16[144,768]{1,0:T(8,128)(2,1)S(1)}, bf16[144,768]{1,0:T(8,128)(2,1)S(1)}, u32[]{:S(2)}, u32[]{:S(2)}) collective-permute-start(bf16[144,768]{1,0:T(8,128)(2,1)S(1)} %get-tuple-element.57), channel_id=1, source_target_pairs={{0,8},{8,0},{1,9},{9,1},{2,10},{10,2},{3,11},{11,3},{4,12},{12,4},... | collective-permute-start | bytes 663560 | tf_op jit(solution)/shard_map/ppermute | solution.py:61
  142.3 1.0 collective-permute-start.28
  143.3 3.8 %collective-permute-done.29.refs_2_ = bf16[2,384,128]{2,1,0:T(8,128)(2,1)S(1)} collective-permute-done((bf16[2,384,128]{2,1,0:T(8,128)(2,1)S(1)}, bf16[2,384,128]{2,1,0:T(8,128)(2,1)S(1)}, u32[]{:S(2)}, u32[]{:S(2)}) %collective-permute-start.29) | collective-permute-done | bytes 196640 | tf_op jit(solution)/shard_map/ppermute | solution.py:61
  147.1 1.4 collective-permute-done.31.refs_4_
  148.5 1.8 %pages.1 = f32[2,4,384,128]{3,2,1,0:T(8,128)} custom-call(s32[58]{0:T(128)S(1)} %concatenate.15.refs_0_, bf16[2,384,128]{2,1,0:T(8,128)(2,1)S(1)} %get-tuple-element.60.refs_1_, bf16[2,384,128]{2,1,0:T(8,128)(2,1)S(1)} %collective-permute-done.29.refs_2_, bf16[2,384,128]{2,1,0:T(8,128)(2,1)S(1)} %collective-permute-done.30.refs_3_, ...), custom_call_target="tpu_custom_call" | custom-call | flops 1800000000 | bytes 5400000 | tf_op jit(solution)/shard_map/pages/pallas_call | solution.py:34
  150.3 1.1 collective-permute-done.28.refs_3_
  151.4 1.0 collective-permute-done.27.refs_1_
  152.5 0.9 add_last.1
  (104 shorter events, 4.5 us)
Async XLA Ops:
  0.6 76.9 %copy-start = (f32[4,24,64,128]{3,2,1,0:T(8,128)S(1)}, f32[4,24,64,128]{3,2,1,0:T(8,128)}, u32[]{:S(2)}) copy-start(f32[4,24,64,128]{3,2,1,0:T(8,128)} %param.34) | copy-start | bytes 9437188
  0.6 1.2 copy-start.5
  1.9 1.1 copy-start.6
  2.9 0.9 copy-start.13
  4.8 14.6 %copy-start.29 = (s32[32]{0:T(128)S(1)}, s32[32]{0:T(128)}, u32[]{:S(2)}) copy-start(s32[32]{0:T(128)} %param.22) | copy-start | bytes 388
  4.8 14.6 %copy-start.30 = (s32[8]{0:T(128)S(1)}, s32[8]{0:T(128)}, u32[]{:S(2)}) copy-start(s32[8]{0:T(128)} %param.32) | copy-start | bytes 100
  4.8 14.6 %copy-start.31 = (s32[8]{0:T(128)S(1)}, s32[8]{0:T(128)}, u32[]{:S(2)}) copy-start(s32[8]{0:T(128)} %param.33) | copy-start | bytes 100
  4.8 25.9 %all-to-all-start = ((bf16[8,48,1024]{2,1,0:T(8,128)(2,1)}), bf16[8,48,1024]{2,1,0:T(8,128)(2,1)}, u32[]{:S(2)}, u32[]{:S(2)}) async-start(bf16[8,48,1024]{2,1,0:T(8,128)(2,1)} %copy-done.1), calls=%async_computation | async-start | bytes 1572864 | tf_op jit(solution)/shard_map/all_to_all | solution.py:639
  11.9 18.8 %collective-permute-start = (bf16[128,1536]{1,0:T(8,128)(2,1)}, bf16[128,1536]{1,0:T(8,128)(2,1)S(1)}, u32[]{:S(2)}, u32[]{:S(2)}) collective-permute-start(bf16[128,1536]{1,0:T(8,128)(2,1)} %constant_dynamic-slice_fusion.1), channel_id=1, source_target_pairs={{0,2},{2,0},{1,3},{3,1},{4,6},{6,4},{5,7},{7,5},{8,10},{10,8},{9,1... | collective-permute-start | bytes 1179656 | tf_op jit(solution)/shard_map/ppermute | solution.py:61
  14.0 19.6 %collective-permute-start.1 = (bf16[128,1536]{1,0:T(8,128)(2,1)}, bf16[128,1536]{1,0:T(8,128)(2,1)}, u32[]{:S(2)}, u32[]{:S(2)}) collective-permute-start(bf16[128,1536]{1,0:T(8,128)(2,1)} %constant_dynamic-slice_fusion.1), channel_id=1, source_target_pairs={{0,8},{8,0},{1,9},{9,1},{2,10},{10,2},{3,11},{11,3},{4,12},{12,4},... | collective-permute-start | bytes 1179656 | tf_op jit(solution)/shard_map/ppermute | solution.py:61
  16.8 16.8 %collective-permute-start.2 = (bf16[16,1536]{1,0:T(8,128)(2,1)}, bf16[16,1536]{1,0:T(8,128)(2,1)}, u32[]{:S(2)}, u32[]{:S(2)}) collective-permute-start(bf16[16,1536]{1,0:T(8,128)(2,1)} %slice.3), channel_id=1, source_target_pairs={{2,4},{6,8},{10,12},{14,16},{18,20},{22,24},{26,28},{3,5},{7,9},{1... | collective-permute-start | bytes 147464 | tf_op jit(solution)/shard_map/ppermute | solution.py:646
  18.1 15.5 %collective-permute-start.3 = (bf16[16,1536]{1,0:T(8,128)(2,1)}, bf16[16,1536]{1,0:T(8,128)(2,1)}, u32[]{:S(2)}, u32[]{:S(2)}) collective-permute-start(bf16[16,1536]{1,0:T(8,128)(2,1)} %slice.3), channel_id=1, source_target_pairs={{2,6},{6,10},{10,14},{14,18},{18,22},{22,26},{26,30},{3,7},{7,11},... | collective-permute-start | bytes 147464 | tf_op jit(solution)/shard_map/ppermute | solution.py:647
  30.7 2.9 %copy-start.8 = (bf16[128,1536]{1,0:T(8,128)(2,1)}, bf16[128,1536]{1,0:T(8,128)(2,1)S(1)}, u32[]{:S(2)}) copy-start(bf16[128,1536]{1,0:T(8,128)(2,1)S(1)} %collective-permute-done.refs_1_.refs_2_) | copy-start | bytes 1179652
  30.7 9.2 %collective-permute-start.6 = (bf16[128,1536]{1,0:T(8,128)(2,1)S(1)}, bf16[128,1536]{1,0:T(8,128)(2,1)}, u32[]{:S(2)}, u32[]{:S(2)}) collective-permute-start(bf16[128,1536]{1,0:T(8,128)(2,1)S(1)} %collective-permute-done.refs_1_.refs_2_), channel_id=1, source_target_pairs={{0,1},{1,0},{2,3},{3,2},{4,5},{5,4},{6,7},{7,6},{8,9},{9,8},{10,11... | collective-permute-start | bytes 1179656 | tf_op jit(solution)/shard_map/ppermute | solution.py:61
  33.6 2.8 %copy-start.25 = (f32[1536]{0:T(1024)S(1)}, f32[1536]{0:T(1024)}, u32[]{:S(2)}) copy-start(f32[1536]{0:T(1024)} %param.30) | copy-start | bytes 18436
  33.6 2.8 %copy-start.26 = (f32[1536]{0:T(1024)S(1)}, f32[1536]{0:T(1024)}, u32[]{:S(2)}) copy-start(f32[1536]{0:T(1024)} %param.25) | copy-start | bytes 18436
  33.6 6.1 %copy-start.27 = (f32[4,256]{1,0:T(4,128)S(1)}, f32[4,256]{1,0:T(4,128)}, u32[]{:S(2)}) copy-start(f32[4,256]{1,0:T(4,128)} %param.24) | copy-start | bytes 12292
  33.7 6.1 %copy-start.28 = (f32[256]{0:T(256)S(1)}, f32[256]{0:T(256)}, u32[]{:S(2)}) copy-start(f32[256]{0:T(256)} %param.26) | copy-start | bytes 3076
  33.7 6.2 %copy-start.32 = (f32[24]{0:T(128)S(1)}, f32[24]{0:T(128)}, u32[]{:S(2)}) copy-start(f32[24]{0:T(128)} %param.29) | copy-start | bytes 292
  33.7 6.2 %copy-start.33 = (f32[24]{0:T(128)S(1)}, f32[24]{0:T(128)}, u32[]{:S(2)}) copy-start(f32[24]{0:T(128)} %param.28) | copy-start | bytes 292
  33.7 6.2 %copy-start.34 = (f32[24]{0:T(128)S(1)}, f32[24]{0:T(128)}, u32[]{:S(2)}) copy-start(f32[24]{0:T(128)} %param.27) | copy-start | bytes 292
  33.7 14.2 %copy-start.24 = (f32[4,1536]{1,0:T(4,128)S(1)}, f32[4,1536]{1,0:T(4,128)}, u32[]{:S(2)}) copy-start(f32[4,1536]{1,0:T(4,128)} %param.23) | copy-start | bytes 73732
  33.7 14.9 %copy-start.7 = (f32[1536,96]{0,1:T(8,128)S(1)}, f32[1536,96]{0,1:T(8,128)}, u32[]{:S(2)}) copy-start(f32[1536,96]{0,1:T(8,128)} %param.31) | copy-start | bytes 1769476
  34.9 13.1 %collective-permute-start.5 = (bf16[80,1536]{1,0:T(8,128)(2,1)S(1)}, bf16[80,1536]{1,0:T(8,128)(2,1)}, u32[]{:S(2)}, u32[]{:S(2)}) collective-permute-start(bf16[80,1536]{1,0:T(8,128)(2,1)S(1)} %get-tuple-element.35), channel_id=1, source_target_pairs={{0,8},{8,0},{1,9},{9,1},{2,10},{10,2},{3,11},{11,3},{4,12},{12,4},... | collective-permute-start | bytes 737288 | tf_op jit(solution)/shard_map/ppermute | solution.py:61
  36.5 7.0 %collective-permute-start.4 = (bf16[64,1536]{1,0:T(8,128)(2,1)S(1)}, bf16[64,1536]{1,0:T(8,128)(2,1)}, u32[]{:S(2)}, u32[]{:S(2)}) collective-permute-start(bf16[64,1536]{1,0:T(8,128)(2,1)S(1)} %get-tuple-element.34), channel_id=1, source_target_pairs={{0,2},{2,0},{1,3},{3,1},{4,6},{6,4},{5,7},{7,5},{8,10},{10,8},{9,1... | collective-permute-start | bytes 589832 | tf_op jit(solution)/shard_map/ppermute | solution.py:61
  37.2 10.1 %collective-permute-start.12 = (bf16[208,512]{1,0:T(8,128)(2,1)S(1)}, bf16[208,512]{1,0:T(8,128)(2,1)S(1)}, u32[]{:S(2)}, u32[]{:S(2)}) collective-permute-start(bf16[208,512]{1,0:T(8,128)(2,1)S(1)} %get-tuple-element.37), channel_id=1, source_target_pairs={{0,16},{16,0},{1,17},{17,1},{2,18},{18,2},{3,19},{19,3},{4,20},{20... | collective-permute-start | bytes 638984 | tf_op jit(solution)/shard_map/ppermute | solution.py:570
  39.8 22.1 %collective-permute-start.7 = (bf16[128,1536]{1,0:T(8,128)(2,1)}, bf16[128,1536]{1,0:T(8,128)(2,1)}, u32[]{:S(2)}, u32[]{:S(2)}) collective-permute-start(bf16[128,1536]{1,0:T(8,128)(2,1)} %collective-permute-done.1.refs_2_.refs_3_), channel_id=1, source_target_pairs={{0,1},{1,0},{2,3},{3,2},{4,5},{5,4},{6,7},{7,6},{8,9},{9,8},{10,11... | collective-permute-start | bytes 1179656 | tf_op jit(solution)/shard_map/ppermute | solution.py:61
  39.9 29.9 %collective-permute-start.10 = (bf16[400,512]{1,0:T(8,128)(2,1)}, bf16[400,512]{1,0:T(8,128)(2,1)}, u32[]{:S(2)}, u32[]{:S(2)}) collective-permute-start(bf16[400,512]{1,0:T(8,128)(2,1)} %get-tuple-element.33.refs_5_.refs_2_), channel_id=1, source_target_pairs={{0,4},{4,0},{1,5},{5,1},{2,6},{6,2},{3,7},{7,3},{8,12},{12,8},{9,1... | collective-permute-start | bytes 1228808 | tf_op jit(solution)/shard_map/ppermute | solution.py:61
  43.5 16.8 %collective-permute-start.11 = (bf16[192,512]{1,0:T(8,128)(2,1)}, bf16[192,512]{1,0:T(8,128)(2,1)}, u32[]{:S(2)}, u32[]{:S(2)}) collective-permute-start(bf16[192,512]{1,0:T(8,128)(2,1)} %get-tuple-element.36), channel_id=1, source_target_pairs={{0,16},{16,0},{1,17},{17,1},{2,18},{18,2},{3,19},{19,3},{4,20},{20... | collective-permute-start | bytes 589832 | tf_op jit(solution)/shard_map/ppermute | solution.py:570
  47.3 17.7 %collective-permute-start.8 = (bf16[64,1536]{1,0:T(8,128)(2,1)}, bf16[64,1536]{1,0:T(8,128)(2,1)}, u32[]{:S(2)}, u32[]{:S(2)}) collective-permute-start(bf16[64,1536]{1,0:T(8,128)(2,1)} %collective-permute-done.4.refs_4_), channel_id=1, source_target_pairs={{0,1},{1,0},{2,3},{3,2},{4,5},{5,4},{6,7},{7,6},{8,9},{9,8},{10,11... | collective-permute-start | bytes 589832 | tf_op jit(solution)/shard_map/ppermute | solution.py:61
  47.9 20.0 %collective-permute-start.9 = (bf16[80,1536]{1,0:T(8,128)(2,1)}, bf16[80,1536]{1,0:T(8,128)(2,1)}, u32[]{:S(2)}, u32[]{:S(2)}) collective-permute-start(bf16[80,1536]{1,0:T(8,128)(2,1)} %collective-permute-done.5.refs_5_), channel_id=1, source_target_pairs={{0,1},{1,0},{2,3},{3,2},{4,5},{5,4},{6,7},{7,6},{8,9},{9,8},{10,11... | collective-permute-start | bytes 737288 | tf_op jit(solution)/shard_map/ppermute | solution.py:61
  50.1 32.8 %all-to-all-start.1 = ((bf16[4,96,384]{2,1,0:T(8,128)(2,1)}), bf16[4,96,384]{2,1,0:T(8,128)(2,1)S(1)}, u32[]{:S(2)}, u32[]{:S(2)}) async-start(bf16[4,96,384]{2,1,0:T(8,128)(2,1)} %copy-done.3), calls=%async_computation.1 | async-start | bytes 589824 | tf_op jit(solution)/shard_map/all_to_all | solution.py:702
  60.3 9.5 %collective-permute-start.13 = (bf16[192,512]{1,0:T(8,128)(2,1)}, bf16[192,512]{1,0:T(8,128)(2,1)S(1)}, u32[]{:S(2)}, u32[]{:S(2)}) collective-permute-start(bf16[192,512]{1,0:T(8,128)(2,1)} %collective-permute-done.11.refs_4_), channel_id=1, source_target_pairs={{0,4},{4,0},{1,5},{5,1},{2,6},{6,2},{3,7},{7,3},{8,12},{12,8},{9,1... | collective-permute-start | bytes 589832 | tf_op jit(solution)/shard_map/ppermute | solution.py:61
  61.9 9.7 %collective-permute-start.14 = (bf16[208,512]{1,0:T(8,128)(2,1)}, bf16[208,512]{1,0:T(8,128)(2,1)S(1)}, u32[]{:S(2)}, u32[]{:S(2)}) collective-permute-start(bf16[208,512]{1,0:T(8,128)(2,1)} %copy-done.10), channel_id=1, source_target_pairs={{0,4},{4,0},{1,5},{5,1},{2,6},{6,2},{3,7},{7,3},{8,12},{12,8},{9,1... | collective-permute-start | bytes 638984 | tf_op jit(solution)/shard_map/ppermute | solution.py:61
  62.3 1.0 copy-start.11
  63.3 1.0 copy-start.17
  64.2 3.7 %copy-start.4 = (bf16[256,1536]{1,0:T(8,128)(2,1)S(1)}, bf16[256,1536]{1,0:T(8,128)(2,1)}, u32[]{:S(2)}) copy-start(bf16[256,1536]{1,0:T(8,128)(2,1)} %refs_1_.3) | copy-start | bytes 2359300
  64.2 3.7 %copy-start.9 = (bf16[128,1536]{1,0:T(8,128)(2,1)S(1)}, bf16[128,1536]{1,0:T(8,128)(2,1)}, u32[]{:S(2)}) copy-start(bf16[128,1536]{1,0:T(8,128)(2,1)} %copy-done.8) | copy-start | bytes 1179652
  65.0 6.6 %copy-start.12 = (bf16[208,512]{1,0:T(8,128)(2,1)S(1)}, bf16[208,512]{1,0:T(8,128)(2,1)}, u32[]{:S(2)}) copy-start(bf16[208,512]{1,0:T(8,128)(2,1)} %copy-done.10) | copy-start | bytes 638980
  65.0 16.2 %collective-permute-start.19 = (bf16[384,384]{1,0:T(8,128)(2,1)}, bf16[384,384]{1,0:T(8,128)(2,1)}, u32[]{:S(2)}, u32[]{:S(2)}) collective-permute-start(bf16[384,384]{1,0:T(8,128)(2,1)} %gate_part.1.refs_2_), channel_id=1, source_target_pairs={{0,16},{16,0},{1,17},{17,1},{2,18},{18,2},{3,19},{19,3},{4,20},{20... | collective-permute-start | bytes 884744 | tf_op jit(solution)/shard_map/ppermute | solution.py:570
  69.8 6.0 %copy-start.14 = (bf16[2,528,1536]{2,1,0:T(8,128)(2,1)}, bf16[2,528,1536]{2,1,0:T(8,128)(2,1)S(1)}, u32[]{:S(2)}) copy-start(bf16[2,528,1536]{2,1,0:T(8,128)(2,1)S(1)} %assemble_rows.1.refs_1_) | copy-start | bytes 9732100
  69.8 7.7 %copy-start.22 = (f32[8,1536]{1,0:T(8,128)S(1)}, f32[8,1536]{1,0:T(8,128)}, u32[]{:S(2)}) copy-start(f32[8,1536]{1,0:T(8,128)} %get-tuple-element.64) | copy-start | bytes 147460
  69.8 7.7 %copy-start.23 = (f32[8,1536]{1,0:T(8,128)S(1)}, f32[8,1536]{1,0:T(8,128)}, u32[]{:S(2)}) copy-start(f32[8,1536]{1,0:T(8,128)} %get-tuple-element.65) | copy-start | bytes 147460
  75.8 0.9 copy-start.18
  77.5 8.1 %collective-permute-start.15 = (bf16[2,528,128]{2,1,0:T(8,128)(2,1)}, bf16[2,528,128]{2,1,0:T(8,128)(2,1)}, u32[]{:S(2)}, u32[]{:S(2)}) collective-permute-start(bf16[2,528,128]{2,1,0:T(8,128)(2,1)} %get-tuple-element.39.refs_2_), channel_id=1, source_target_pairs={{0,1},{1,0},{2,3},{3,2},{4,5},{5,4},{6,7},{7,6},{8,9},{9,8},{10,11... | collective-permute-start | bytes 811016 | tf_op jit(solution)/shard_map/ppermute | solution.py:61
  78.5 32.9 %collective-permute-start.18 = (bf16[384,384]{1,0:T(8,128)(2,1)}, bf16[384,384]{1,0:T(8,128)(2,1)}, u32[]{:S(2)}, u32[]{:S(2)}) collective-permute-start(bf16[384,384]{1,0:T(8,128)(2,1)} %gate_part.1.refs_2_), channel_id=1, source_target_pairs={{0,4},{4,0},{1,5},{5,1},{2,6},{6,2},{3,7},{7,3},{8,12},{12,8},{9,1... | collective-permute-start | bytes 884744 | tf_op jit(solution)/shard_map/ppermute | solution.py:61
  81.2 30.2 %collective-permute-start.20 = (bf16[384,384]{1,0:T(8,128)(2,1)}, bf16[384,384]{1,0:T(8,128)(2,1)}, u32[]{:S(2)}, u32[]{:S(2)}) collective-permute-start(bf16[384,384]{1,0:T(8,128)(2,1)} %collective-permute-done.19.refs_4_.refs_1_), channel_id=1, source_target_pairs={{0,4},{4,0},{1,5},{5,1},{2,6},{6,2},{3,7},{7,3},{8,12},{12,8},{9,1... | collective-permute-start | bytes 884744 | tf_op jit(solution)/shard_map/ppermute | solution.py:61
  82.9 2.7 %copy-start.2 = (f32[4,6,64,128]{3,2,1,0:T(8,128)S(1)}, f32[4,6,64,128]{3,2,1,0:T(8,128)}, u32[]{:S(2)}) copy-start(f32[4,6,64,128]{3,2,1,0:T(8,128)} %constant_dynamic-slice_fusion) | copy-start | bytes 2359300
  82.9 2.7 %copy-start.19 = (bf16[2,528,384]{2,1,0:T(8,128)(2,1)S(1)}, bf16[2,528,384]{2,1,0:T(8,128)(2,1)}, u32[]{:S(2)}) copy-start(bf16[2,528,384]{2,1,0:T(8,128)(2,1)} %copy-done.18) | copy-start | bytes 2433028
  82.9 2.7 %copy-start.21 = (f32[2,528,128]{2,1,0:T(8,128)S(1)}, f32[2,528,128]{2,1,0:T(8,128)}, u32[]{:S(2)}) copy-start(f32[2,528,128]{2,1,0:T(8,128)} %copy-done.20) | copy-start | bytes 1622020
  82.9 36.6 %collective-permute-start.21 = (bf16[384,384]{1,0:T(8,128)(2,1)S(1)}, bf16[384,384]{1,0:T(8,128)(2,1)S(1)}, u32[]{:S(2)}, u32[]{:S(2)}) collective-permute-start(bf16[384,384]{1,0:T(8,128)(2,1)S(1)} %out_part.1.refs_1_), channel_id=1, source_target_pairs={{0,4},{4,0},{1,5},{5,1},{2,6},{6,2},{3,7},{7,3},{8,12},{12,8},{9,1... | collective-permute-start | bytes 884744 | tf_op jit(solution)/shard_map/ppermute | solution.py:61
  83.3 16.7 %collective-permute-start.22 = (bf16[384,384]{1,0:T(8,128)(2,1)S(1)}, bf16[384,384]{1,0:T(8,128)(2,1)S(1)}, u32[]{:S(2)}, u32[]{:S(2)}) collective-permute-start(bf16[384,384]{1,0:T(8,128)(2,1)S(1)} %out_part.1.refs_1_), channel_id=1, source_target_pairs={{0,16},{16,0},{1,17},{17,1},{2,18},{18,2},{3,19},{19,3},{4,20},{20... | collective-permute-start | bytes 884744 | tf_op jit(solution)/shard_map/ppermute | solution.py:570
  94.7 10.9 %collective-permute-start.16 = (bf16[2,400,128]{2,1,0:T(8,128)(2,1)S(1)}, bf16[2,400,128]{2,1,0:T(8,128)(2,1)S(1)}, u32[]{:S(2)}, u32[]{:S(2)}) collective-permute-start(bf16[2,400,128]{2,1,0:T(8,128)(2,1)S(1)} %get-tuple-element.41.refs_1_), channel_id=1, source_target_pairs={{0,4},{4,0},{1,5},{5,1},{2,6},{6,2},{3,7},{7,3},{8,12},{12,8},{9,1... | collective-permute-start | bytes 614408 | tf_op jit(solution)/shard_map/ppermute | solution.py:61
  100.0 11.4 %copy-start.15 = (bf16[2,528,1536]{2,1,0:T(8,128)(2,1)S(1)}, bf16[2,528,1536]{2,1,0:T(8,128)(2,1)}, u32[]{:S(2)}) copy-start(bf16[2,528,1536]{2,1,0:T(8,128)(2,1)} %copy-done.14) | copy-start | bytes 9732100
  100.0 19.5 %collective-permute-start.23 = (bf16[384,384]{1,0:T(8,128)(2,1)S(1)}, bf16[384,384]{1,0:T(8,128)(2,1)S(1)}, u32[]{:S(2)}, u32[]{:S(2)}) collective-permute-start(bf16[384,384]{1,0:T(8,128)(2,1)S(1)} %collective-permute-done.22.refs_3_), channel_id=1, source_target_pairs={{0,4},{4,0},{1,5},{5,1},{2,6},{6,2},{3,7},{7,3},{8,12},{12,8},{9,1... | collective-permute-start | bytes 884744 | tf_op jit(solution)/shard_map/ppermute | solution.py:61
  106.2 8.5 %collective-permute-start.17 = (bf16[400,128]{1,0:T(8,128)(2,1)S(1)}, bf16[400,128]{1,0:T(8,128)(2,1)S(1)}, u32[]{:S(2)}, u32[]{:S(2)}) collective-permute-start(bf16[400,128]{1,0:T(8,128)(2,1)S(1)} %compose.1.refs_6_), channel_id=1, source_target_pairs={{0,16},{1,17},{2,18},{3,19},{4,20},{5,21},{6,22},{7,23},{8,24},{9,... | collective-permute-start | bytes 307208 | tf_op jit(solution)/shard_map/ppermute | solution.py:777
  122.4 3.8 %collective-permute-start.24 = (bf16[4,144,1536]{2,1,0:T(8,128)(2,1)S(1)}, bf16[4,144,1536]{2,1,0:T(8,128)(2,1)S(1)}, u32[]{:S(2)}, u32[]{:S(2)}) collective-permute-start(bf16[4,144,1536]{2,1,0:T(8,128)(2,1)S(1)} %mix_send.1), channel_id=1, source_target_pairs={{0,1},{1,0},{2,3},{3,2},{4,5},{5,4},{6,7},{7,6},{8,9},{9,8},{10,11... | collective-permute-start | bytes 5308424 | tf_op jit(solution)/shard_map/ppermute | solution.py:61
  126.5 13.8 %collective-permute-start.25 = (bf16[2,144,768]{2,1,0:T(8,128)(2,1)S(1)}, bf16[2,144,768]{2,1,0:T(8,128)(2,1)S(1)}, u32[]{:S(2)}, u32[]{:S(2)}) collective-permute-start(bf16[2,144,768]{2,1,0:T(8,128)(2,1)S(1)} %get-tuple-element.53), channel_id=1, source_target_pairs={{0,2},{2,0},{1,3},{3,1},{4,6},{6,4},{5,7},{7,5},{8,10},{10,8},{9,1... | collective-permute-start | bytes 1327112 | tf_op jit(solution)/shard_map/ppermute | solution.py:61
  128.3 12.0 %collective-permute-start.26 = (bf16[2,128,768]{2,1,0:T(8,128)(2,1)S(1)}, bf16[2,128,768]{2,1,0:T(8,128)(2,1)S(1)}, u32[]{:S(2)}, u32[]{:S(2)}) collective-permute-start(bf16[2,128,768]{2,1,0:T(8,128)(2,1)S(1)} %get-tuple-element.55), channel_id=1, source_target_pairs={{0,8},{8,0},{1,9},{9,1},{2,10},{10,2},{3,11},{11,3},{4,12},{12,4},... | collective-permute-start | bytes 1179656 | tf_op jit(solution)/shard_map/ppermute | solution.py:61
  130.1 17.0 %collective-permute-start.29 = (bf16[2,384,128]{2,1,0:T(8,128)(2,1)S(1)}, bf16[2,384,128]{2,1,0:T(8,128)(2,1)S(1)}, u32[]{:S(2)}, u32[]{:S(2)}) collective-permute-start(bf16[2,384,128]{2,1,0:T(8,128)(2,1)S(1)} %get-tuple-element.61), channel_id=1, source_target_pairs={{0,2},{2,0},{1,3},{3,1},{4,6},{6,4},{5,7},{7,5},{8,10},{10,8},{9,1... | collective-permute-start | bytes 589832 | tf_op jit(solution)/shard_map/ppermute | solution.py:61
  130.4 16.7 %collective-permute-start.30 = (bf16[2,384,128]{2,1,0:T(8,128)(2,1)S(1)}, bf16[2,384,128]{2,1,0:T(8,128)(2,1)S(1)}, u32[]{:S(2)}, u32[]{:S(2)}) collective-permute-start(bf16[2,384,128]{2,1,0:T(8,128)(2,1)S(1)} %get-tuple-element.62), channel_id=1, source_target_pairs={{0,8},{8,0},{1,9},{9,1},{2,10},{10,2},{3,11},{11,3},{4,12},{12,4},... | collective-permute-start | bytes 589832 | tf_op jit(solution)/shard_map/ppermute | solution.py:61
  130.6 17.9 %collective-permute-start.31 = (bf16[2,384,128]{2,1,0:T(8,128)(2,1)S(1)}, bf16[2,384,128]{2,1,0:T(8,128)(2,1)S(1)}, u32[]{:S(2)}, u32[]{:S(2)}) collective-permute-start(bf16[2,384,128]{2,1,0:T(8,128)(2,1)S(1)} %get-tuple-element.63), channel_id=1, source_target_pairs={{0,10},{2,8},{8,2},{10,0},{1,11},{3,9},{9,3},{11,1},{4,14},{6,12},... | collective-permute-start | bytes 589832 | tf_op jit(solution)/shard_map/ppermute | solution.py:806
  140.5 12.0 %collective-permute-start.27 = (bf16[144,768]{1,0:T(8,128)(2,1)S(1)}, bf16[144,768]{1,0:T(8,128)(2,1)S(1)}, u32[]{:S(2)}, u32[]{:S(2)}) collective-permute-start(bf16[144,768]{1,0:T(8,128)(2,1)S(1)} %get-tuple-element.57), channel_id=1, source_target_pairs={{0,8},{8,0},{1,9},{9,1},{2,10},{10,2},{3,11},{11,3},{4,12},{12,4},... | collective-permute-start | bytes 663560 | tf_op jit(solution)/shard_map/ppermute | solution.py:61
  142.3 9.1 %collective-permute-start.28 = (bf16[128,768]{1,0:T(8,128)(2,1)S(1)}, bf16[128,768]{1,0:T(8,128)(2,1)S(1)}, u32[]{:S(2)}, u32[]{:S(2)}) collective-permute-start(bf16[128,768]{1,0:T(8,128)(2,1)S(1)} %get-tuple-element.59), channel_id=1, source_target_pairs={{0,2},{2,0},{1,3},{3,1},{4,6},{6,4},{5,7},{7,5},{8,10},{10,8},{9,1... | collective-permute-start | bytes 589832 | tf_op jit(solution)/shard_map/ppermute | solution.py:61
  (5 other events, 3.8 us)

commit v3 on v2

--- a/solution.py
+++ b/solution.py
@@ -21,11 +21,13 @@
 SEQ = ("t", "a", "y", "b")
 VMEM = pl.BlockSpec(memory_space=pltpu.VMEM)
 SMEM = pl.BlockSpec(memory_space=pltpu.SMEM)
-
-
-def call(body, name, out_shape, ins, scratch=(), after=(), us=1.0, limit=40):
-    specs = [SMEM if x.dtype == jnp.int32 else VMEM for x in ins]
-    specs += [pl.BlockSpec(memory_space=pl.ANY)] * len(after)
+ANY = pl.BlockSpec(memory_space=pl.ANY)
+
+
+def call(body, name, out_shape, ins, scratch=(), after=(), us=1.0, limit=16,
+         fetch=False):
+    specs = [SMEM if x.dtype == jnp.int32 else (ANY if fetch else VMEM) for x in ins]
+    specs += [ANY] * len(after)
     first, last = len(ins), len(ins) + len(after)
 
     def kernel(*refs):
@@ -85,32 +87,59 @@
     return seq * 2 + c
 
 
-def pack_kernel(heads, inner, small, gate, out):
+def pack_kernel(heads, inner_hbm, small_hbm, gate_hbm, out, inner, small, gate, arrived):
+    copies = [
+        pltpu.make_async_copy(source, target, arrived.at[k])
+        for k, (source, target) in enumerate(((inner_hbm, inner), (small_hbm, small), (gate_hbm, gate)))
+    ]
+    for copy in copies:
+        copy.start()
     width = heads * 64
     rows = inner.shape[0]
+    places = [(place, place % 2, place // 2) for place in range(8)]
+    copies[0].wait()
+    for place, c, group in places:
+        at = (c * 4 + group) * width
+        out[place, :, :width] = inner[:, at : at + width].astype(BF16)
+    copies[1].wait()
     lane = lax.broadcasted_iota(jnp.int32, (rows, LANES), 1)
     steps = small[:, 2 * N :]
     steps = jnp.concatenate([steps, jnp.zeros((rows, LANES - steps.shape[1]), F32)], axis=1)
-    for place in range(8):
-        group, c = place // 2, place % 2
-        at = (c * 4 + group) * width
-        out[place, :, :width] = inner[:, at : at + width].astype(BF16)
+    for place, c, group in places:
         out[place, :, width : width + N] = small[:, c * N : (c + 1) * N].astype(BF16)
         first = (c * 4 + group) * heads
         moved = pltpu.roll(steps, LANES - first, 1) if first else steps
         out[place, :, width + N : width + N + LANES] = jnp.where(lane < heads, moved, 0.0).astype(BF16)
+    copies[2].wait()
+    for place, c, group in places:
+        at = (c * 4 + group) * width
         out[place, :, width + N + LANES :] = gate[:, at : at + width].astype(BF16)
+
+
+def rows_kernel(sizes, ints, hidden, mine, tail, arrived):
+    c = views(ints, sizes)[0][1]
+    half = mine.shape[0]
+    at = pl.multiple_of(c * half, TILE)
+    copies = (
+        pltpu.make_async_copy(hidden.at[pl.ds(at, half), :], mine, arrived.at[0]),
+        pltpu.make_async_copy(hidden.at[pl.ds(hidden.shape[0] - TILE, TILE), :], tail, arrived.at[1]),
+    )
+    for copy in copies:
+        copy.start()
+    for copy in copies:
+        copy.wait()
 
 
 def repack_kernel(got, whole, low, high, gate):
     rows, width = got.shape[1], whole.shape[1]
+    cut = low.shape[0] // rows
     for place in range(8):
         gate[place * rows : (place + 1) * rows, :] = got[place, :, width + LANES :]
     lane = lax.broadcasted_iota(jnp.int32, (TILE, LANES), 1) // TILE
     for place in range(8):
         block = got[place, :, :width]
         whole[place * rows : (place + 1) * rows, :] = block
-        half, at = (low, place) if place < 4 else (high, place - 4)
+        half, at = (low, place) if place < cut else (high, place - cut)
         half[at * rows : (at + 1) * rows, :] = block
     for piece in range(rows // TILE):
         packed = jnp.zeros((TILE, LANES), F32)
@@ -120,22 +149,31 @@
             packed = jnp.where(lane == place, steps, packed)
         here = slice(piece * LANES, (piece + 1) * LANES)
         whole[8 * rows :, here] = packed.astype(BF16)
-        high[4 * rows :, here] = packed.astype(BF16)
+        high[(8 - cut) * rows :, here] = packed.astype(BF16)
     rest = rows // TILE * LANES
     if rest < width:
         blank = jnp.zeros((TILE, width - rest), BF16)
         whole[8 * rows :, rest:] = blank
-        high[4 * rows :, rest:] = blank
+        high[(8 - cut) * rows :, rest:] = blank
 
 
 def copy_kernel(source, out):
     out[...] = source[...]
 
 
-def pack_out_kernel(source, out):
-    width = out.shape[2]
-    for place in range(4):
-        out[place] = source[:, place * width : (place + 1) * width].astype(BF16)
+def pack_out_kernel(sizes, ints, source, *outs):
+    me = views(ints, sizes)[0][0]
+    width = outs[0].shape[1]
+    for rel, out in enumerate(outs):
+        at = pl.multiple_of((me ^ rel) * width, LANES)
+        out[...] = source[:, pl.ds(at, width)].astype(BF16)
+
+
+def join_kernel(*refs):
+    out, at = refs[-1], 0
+    for source in refs[:-1]:
+        out[at : at + source.shape[0], :] = source[...]
+        at += source.shape[0]
 
 
 def forward_kernel(sizes, ints, mine_b, mine_a, halo0, halo1, over_b, over_a):
@@ -204,15 +242,12 @@
                 weights[pl.ds(at, TILE), width:] = kept
 
 
-def inner_kernel(sizes, marks, rows, *refs):
+def weights_kernel(sizes, marks, rows, *refs):
     info, layout = views(refs[0], sizes)[:2]
-    hidden = refs[1]
-    if marks:
-        parts = refs[2 : 2 + len(marks)]
-        raw_ref, shared_ref, step_ref, weights = refs[2 + len(marks) :]
-        place_parts(weights, marks, rows, parts, info, layout)
-    else:
-        weights, raw_ref, shared_ref, step_ref = refs[2:6]
+    place_parts(refs[1 + len(marks)], marks, rows, refs[1 : 1 + len(marks)], info, layout)
+
+
+def inner_kernel(hidden, weights, raw_ref, shared_ref, step_ref):
     bc = raw_ref.shape[2]
     for run in range(2):
         result = dot(hidden[run], weights[:, bc:])
@@ -224,14 +259,7 @@
         raw_ref[run] = dot(hidden[run], weights[:, :bc]).astype(BF16)
 
 
-def gate_kernel(sizes, marks, rows, *refs):
-    info, layout = views(refs[0], sizes)[:2]
-    hidden = refs[1]
-    if marks:
-        gate_ref, weights = refs[2 + len(marks) :]
-        place_parts(weights, marks, rows, refs[2 : 2 + len(marks)], info, layout)
-    else:
-        weights, gate_ref = refs[2:4]
+def gate_kernel(hidden, weights, gate_ref):
     for run in range(2):
         gate_ref[run] = jax.nn.silu(dot(hidden[run], weights[...])).astype(BF16)
 
@@ -287,7 +315,7 @@
 
 
 def state_kernel(heads, tokens, sizes, ints, raw, own, other, step, params, init, x_ref, b_ref, c_ref,
-                 cum_ref, dt_ref, end_ref, factor_ref, summary_ref, state, factor):
+                 cum_ref, dt_ref, end_ref, factor_ref, summary_ref):
     info, _, lengths, groups = views(ints, sizes)[:4]
     starts = starts_of(lengths)
     width = heads * 64
@@ -304,11 +332,6 @@
     below = (row >= col).astype(F32)
 
     def one(i, carry):
-        @pl.when(i % per_run == 0)
-        def _():
-            state[...] = jnp.zeros_like(state)
-            factor[...] = jnp.ones_like(factor)
-
         first = chunk_start(i, info, tokens)
         opened = last_start(first + PAGE - 1, starts)
         alive = (opened < first).astype(F32)
@@ -338,39 +361,41 @@
         c_ref[i] = c
         cum_ref[i] = cum
         dt_ref[i] = dt
-        whole = jnp.broadcast_to(jnp.exp(cum_t[0:8, PAGE - 1 : PAGE]), (8, LANES)) * alive
+        last_t = cum_t[0:8, PAGE - 1 : PAGE]
+        factor_ref[i] = jnp.broadcast_to(jnp.exp(last_t), (8, LANES)) * alive
         for pair in range(pairs):
-            scaled = (x[:, pair * LANES : (pair + 1) * LANES] * pair_columns(weight, pair)).astype(BF16)
-            added = dot(scaled, b, TN)
-            for k in (0, 1):
-                h = 2 * pair + k
+            here = slice(pair * LANES, (pair + 1) * LANES)
+            scaled = (x[:, here] * pair_columns(weight, pair)).astype(BF16)
+            end_ref[i, here, :] = dot(scaled, b, TN)
+
+        @pl.when(opened >= first)
+        def _():
+            for k in range(len(starts)):
+
+                @pl.when(starts[k] == opened)
+                def _():
+                    at_start = col == opened - first - 1
+                    before = jnp.sum(jnp.where(at_start, cum_t, 0.0), axis=1, keepdims=True)
+                    opening = jnp.broadcast_to(jnp.exp(last_t - before[0:8]), (8, LANES))
+                    for h in range(heads):
+                        here = slice(h * 64, (h + 1) * 64)
+                        entered = opening[h : h + 1, :] * init[groups[k], here, :]
+                        end_ref[i, here, :] = end_ref[i, here, :] + entered
+
+        return carry
+
+    lax.fori_loop(0, chunks, one, 0, unroll=2)
+    for run in range(2):
+        factor = factor_ref[run * per_run]
+        for i in range(run * per_run + 1, (run + 1) * per_run):
+            for h in range(heads):
                 here = slice(h * 64, (h + 1) * 64)
-                state[here, :] = state[here, :] * whole[h : h + 1, :] + added[k * 64 : (k + 1) * 64, :]
-        for k in range(len(starts)):
-            start = starts[k]
-
-            @pl.when((start >= first) & (start == opened))
-            def _():
-                before = jnp.sum(jnp.where(col == start - first - 1, cum_t, 0.0), axis=1, keepdims=True)
-                opening = jnp.exp(cum_t[0:8, PAGE - 1 : PAGE] - before[0:8])
-                opening = jnp.broadcast_to(opening, (8, LANES))
-                for h in range(heads):
-                    here = slice(h * 64, (h + 1) * 64)
-                    state[here, :] = state[here, :] + opening[h : h + 1, :] * init[groups[k], here, :]
-
-        factor[...] = factor[...] * whole
-        end_ref[i] = state[...]
-        factor_ref[i] = factor[...]
-
-        @pl.when(i % per_run == per_run - 1)
-        def _():
-            summary_ref[i // per_run, : heads * 64, :] = state[...].astype(BF16)
-            tail = jnp.concatenate([factor[...], jnp.zeros_like(factor[...])], axis=0)
-            summary_ref[i // per_run, heads * 64 :, :] = tail.astype(BF16)
-
-        return carry
-
-    lax.fori_loop(0, chunks, one, 0)
+                end_ref[i, here, :] = end_ref[i, here, :] + factor_ref[i, h : h + 1, :] * end_ref[i - 1, here, :]
+            factor = factor * factor_ref[i]
+            factor_ref[i] = factor
+        summary_ref[run, : heads * 64, :] = end_ref[(run + 1) * per_run - 1].astype(BF16)
+        tail = jnp.concatenate([factor, jnp.zeros_like(factor)], axis=0)
+        summary_ref[run, heads * 64 :, :] = tail.astype(BF16)
 
 
 def within_kernel(heads, tokens, sizes, ints, x_ref, b_ref, c_ref, cum_ref, dt_ref, params, init, y_ref):
@@ -405,22 +430,25 @@
             ).astype(BF16)
             y = dot(jnp.concatenate(mixing, axis=1), both)
             y_ref[i, :, here] = y + pair_columns(skip, pair) * x
-        for k in range(len(starts)):
-            start = starts[k]
-
-            @pl.when((start >= first) & (start < first + PAGE))
-            def _():
-                before = jnp.sum(jnp.where(row == start - first - 1, cum, 0.0), axis=0, keepdims=True)
-                opening = jnp.exp(jnp.minimum(cum - before, 0.0))
-                opening = jnp.where(start_of == start, opening, 0.0)
-                for pair in range(pairs):
-                    here = slice(pair * LANES, (pair + 1) * LANES)
-                    read = dot(c, init[groups[k], here, :].astype(BF16), NT)
-                    y_ref[i, :, here] = y_ref[i, :, here] + pair_columns(opening, pair) * read
+        @pl.when(last_start(first + PAGE - 1, starts) >= first)
+        def _():
+            for k in range(len(starts)):
+                start = starts[k]
+
+                @pl.when((start >= first) & (start < first + PAGE))
+                def _():
+                    at_start = row == start - first - 1
+                    before = jnp.sum(jnp.where(at_start, cum, 0.0), axis=0, keepdims=True)
+                    opening = jnp.exp(jnp.minimum(cum - before, 0.0))
+                    opening = jnp.where(start_of == start, opening, 0.0)
+                    for pair in range(pairs):
+                        here = slice(pair * LANES, (pair + 1) * LANES)
+                        read = dot(c, init[groups[k], here, :].astype(BF16), NT)
+                        y_ref[i, :, here] = y_ref[i, :, here] + pair_columns(opening, pair) * read
 
         return carry
 
-    lax.fori_loop(0, chunks, one, 0)
+    lax.fori_loop(0, chunks, one, 0, unroll=2)
 
 
 def onto(run, h, before):
@@ -446,19 +474,12 @@
     block_ref[...] = total.astype(BF16)
 
 
-def finish_kernel(heads, tokens, sizes, ints, mine, theirs, entering, c_ref, cum_ref, end_ref,
-                  factor_ref, y_ref, gate, params, mixed_ref, square_ref, page0, page1, page2, page3,
-                  starting, state):
-    info, _, lengths = views(ints, sizes)[:3]
-    starts = starts_of(lengths)
-    width = heads * 64
-    gain = params[5:6, pl.ds(pl.multiple_of(info[0] * width, LANES), width)]
-    pages = (page0, page1, page2, page3)
-    chunks = c_ref.shape[0]
+def enter_kernel(heads, tokens, sizes, ints, mine, theirs, entering, end_ref, factor_ref, states,
+                 page0, page1, page2, page3, starting):
+    info = views(ints, sizes)[0]
+    me, y = info[0], info[4]
     per = tokens // PAGE
-    per_run = chunks // 2
-    pairs = heads // 2
-    me, y = info[0], info[4]
+    per_run = states.shape[0] // 2
     for h in range(heads):
         here = slice(h * 64, (h + 1) * 64)
         outside = entering[here, :].astype(F32)
@@ -467,20 +488,39 @@
         second = onto(mine[0], h, first)
         third = jnp.where(y == 0, onto(theirs[0], h, second), onto(theirs[1], h, second))
         starting[1, here, :] = third
+    states[0] = starting[0].astype(BF16)
+    states[per_run] = starting[1].astype(BF16)
+    for rel, page in enumerate((page0, page1, page2, page3)):
+        for k in range(per):
+            i = (me ^ rel) * per + k
+            run = i // per_run
+            for h in range(heads):
+                here = slice(h * 64, (h + 1) * 64)
+                after = end_ref[i, here, :] + factor_ref[i, h : h + 1, :] * starting[run, here, :]
+                page[k, here, :] = after.astype(BF16)
+
+            @pl.when(i % per_run < per_run - 1)
+            def _():
+                states[i + 1] = page[k]
+
+
+def finish_kernel(heads, tokens, sizes, ints, states, c_ref, cum_ref, y_ref, gate, params, mixed_ref,
+                  square_ref):
+    info, _, lengths = views(ints, sizes)[:3]
+    starts = starts_of(lengths)
+    width = heads * 64
+    gain = params[5:6, pl.ds(pl.multiple_of(info[0] * width, LANES), width)]
+    chunks = c_ref.shape[0]
+    per_run = chunks // 2
+    pairs = heads // 2
     ones = jnp.ones((8, LANES), F32)
 
     def one(i, carry):
         run = i // per_run
-
-        @pl.when(i % per_run == 0)
-        def _():
-            state[...] = starting[run]
-
-        q = i // per
         first = chunk_start(i, info, tokens)
         alive = (first_positions(first, starts, (PAGE, LANES)) < first).astype(F32)
         decay = jnp.exp(cum_ref[i]) * alive
-        read = dot(c_ref[i], state[...].astype(BF16), NT)
+        read = dot(c_ref[i], states[i], NT)
         rows = pl.ds(pl.multiple_of(TILE + (i % per_run) * PAGE, TILE), PAGE)
         squares = jnp.zeros((PAGE, LANES), F32)
         for pair in range(pairs):
@@ -490,30 +530,19 @@
             mixed_ref[i, :, here] = (value * gain[:, here]).astype(BF16)
             squares = squares + value * value
         square_ref[i] = dot(ones, squares, NT, HIGHEST)
-        for h in range(heads):
-            here = slice(h * 64, (h + 1) * 64)
-            after = end_ref[i, here, :] + factor_ref[i, h : h + 1, :] * starting[run, here, :]
-            state[here, :] = after
+        return carry
+
+    lax.fori_loop(0, chunks, one, 0, unroll=2)
+
+
+def columns_kernel(sizes, count, rows, ints, *refs):
+    info = views(ints, sizes)[0]
+    parts, out = refs[:count], refs[count]
+    for index, part in enumerate(parts):
         for rel in range(4):
-
-            @pl.when(q ^ me == rel)
-            def _():
-                pages[rel][i % per] = state[...].astype(BF16)
-
-        return carry
-
-    lax.fori_loop(0, chunks, one, 0)
-
-
-def columns_kernel(sizes, count, rows, *refs):
-    info = views(refs[0], sizes)[0]
-    parts = refs[1 : 1 + count]
-    out = refs[1 + count]
-    for index in range(count):
-        for place in range(4):
-            seq = stored_block(index // 2, index % 2, 2 * place, info) // 2
+            seq = stored_block(index // 2, index % 2, 2 * (info[0] ^ rel), info) // 2
             at = pl.multiple_of(seq * rows, TILE)
-            out[pl.ds(at, rows), :] = parts[index][place * rows : (place + 1) * rows, :]
+            out[pl.ds(at, rows), :] = part[rel * rows : (rel + 1) * rows, :]
 
 
 def mix_kernel(sizes, keep, ints, mixed, squares, columns, out):
@@ -630,21 +659,31 @@
 
     wide = width + N + LANES
     aligned = rows % TILE == 0
+    size = lax.axis_size(SEQ)
+    half = tokens // 2
+    mine, tail = call(
+        functools.partial(rows_kernel, sizes),
+        "own_rows",
+        (shape((half, model), BF16), shape((TILE, model), BF16)),
+        [ints, hidden_in],
+        [pltpu.SemaphoreType.DMA((2,))],
+        fetch=True,
+    )
+    mine_b, mine_a = swap(mine, "b"), swap(mine, "a")
     inner_send = call(
         functools.partial(pack_kernel, heads),
         "pack_rows",
         shape((8, rows, wide + width), BF16),
         [inner_proj, small_proj, gate_proj],
+        [
+            *[pltpu.VMEM(x.shape, F32) for x in (inner_proj, small_proj, gate_proj)],
+            pltpu.SemaphoreType.DMA((3,)),
+        ],
+        after=[mine],
+        us=2,
+        fetch=True,
     )
     inner_got = lax.all_to_all(inner_send, GROUP, 0, 0, tiled=True)
-
-    size = lax.axis_size(SEQ)
-    half = tokens // 2
-    mine = lax.dynamic_slice_in_dim(hidden_in, c * half, half, 0)
-    mine_b, mine_a = swap(mine, "b"), swap(mine, "a")
-    tail = hidden_in[tokens - TILE :]
-    halo0 = lax.ppermute(tail, SEQ, [(i, i + 1) for i in range(1, size - 1, 2)])
-    halo1 = lax.ppermute(tail, SEQ, [(i, i + 2) for i in range(1, size - 2, 2)])
 
     if aligned:
         part, low, high, gate_part = call(
@@ -653,7 +692,7 @@
             (
                 shape((8 * rows + TILE, width + N), BF16),
                 shape((4 * rows, width + N), BF16),
-                shape((4 * rows + TILE, width + N), BF16),
+                shape(((8 - 4) * rows + TILE, width + N), BF16),
                 shape((8 * rows, width), BF16),
             ),
             [inner_got],
@@ -669,73 +708,69 @@
         index = [stored_block(s, dy, p, info) for s in range(t_count) for dy in (0, 1) for p in range(8)]
         index = row_layout[jnp.stack(index)]
         inner_got = inner_got.reshape(8 * rows, wide + width)
-        inner_parts = [in_order(weight_parts(inner_got[:, :wide], t_count), index)]
+        inner_weights = in_order(weight_parts(inner_got[:, :wide], t_count), index)
         gate_part = inner_got[:, wide:]
         ready = high = None
+
+    halo0 = lax.ppermute(tail, SEQ, [(i, i + 1) for i in range(1, size - 1, 2)])
+    halo1 = lax.ppermute(tail, SEQ, [(i, i + 2) for i in range(1, size - 2, 2)])
 
     over_b, over_a = call(
         functools.partial(forward_kernel, sizes),
         "forward_rows",
         (shape((half // 2, model), BF16), shape((half // 2 + TILE, model), BF16)),
         [ints, mine_b, mine_a, halo0, halo1],
-        after=ready or (),
+        after=ready or [],
     )
     mine_d0, mine_d1 = swap(over_b, "b"), swap(over_a, "a")
     rows_in = [mine_b, mine_a, mine_d0, mine_d1]
+    if aligned:
+        gate_part = call(copy_kernel, "gate_part", shape(gate_part.shape, BF16), [gate_part], after=[high])
+    gate_parts = weight_parts(gate_part, t_count)
+    across = [(i, i ^ 3) for i in range(4)]
+    out_rows = out_proj.shape[1]
+    out_send = call(
+        functools.partial(pack_out_kernel, sizes),
+        "pack_out",
+        [shape((out_rows, width), BF16)] * 4,
+        [ints, out_proj.T],
+        after=inner_parts[1:2] if aligned else [],
+    )
+    out_got = [
+        out_send[0],
+        swap(out_send[1], "b"),
+        swap(out_send[2], "a"),
+        lax.ppermute(out_send[3], ("a", "b"), across),
+    ]
+    out_part = call(join_kernel, "out_part", shape((4 * out_rows, width), BF16), out_got)
+    out_parts = weight_parts(out_part, t_count)
     hidden = call(
         functools.partial(assemble_kernel, sizes),
         "assemble_rows",
         shape((2, TILE + 2 * tokens, model), BF16),
         [ints, hidden_in, *rows_in, *[swap(x, "tp") for x in rows_in], halo0, halo1],
+        after=[],
         us=2,
     )
     if aligned:
-        gate_part = call(copy_kernel, "gate_part", shape(gate_part.shape, BF16), [gate_part], after=[high])
-    gate_parts = weight_parts(gate_part, t_count)
-    out_send = call(
-        pack_out_kernel,
-        "pack_out",
-        shape((4, out_proj.shape[1], width), BF16),
-        [out_proj.T],
-        after=[high] if aligned else (),
-    )
-    out_got = lax.all_to_all(out_send, ("a", "b"), 0, 0, tiled=True)
-    out_rows = out_proj.shape[1]
-    out_got = out_got.reshape(4 * out_rows, width)
-    if out_rows % TILE == 0:
-        out_got = call(
-            copy_kernel, "out_part", shape(out_got.shape, BF16), [out_got], after=[gate_parts[-2]]
+        inner_weights = call(
+            functools.partial(weights_kernel, sizes, marks, rows),
+            "inner_weights",
+            shape((model, wide), BF16),
+            [ints, *inner_parts],
+            us=15,
         )
-    out_parts = weight_parts(out_got, t_count)
-    if not aligned:
-        gate_parts = [in_order(gate_parts, index)]
-    if out_rows % TILE == 0:
-        columns = call(
-            functools.partial(columns_kernel, sizes, count, out_rows),
-            "columns",
-            shape((model, width), BF16),
-            [ints, *out_parts],
-        )
-    else:
-        index = [
-            stored_block(s, dy, 2 * p, info) // 2
-            for s in range(t_count)
-            for dy in (0, 1)
-            for p in range(4)
-        ]
-        columns = in_order(out_parts, jnp.stack(index))
-
     long = TILE + 2 * tokens
     raw, shared, step = call(
-        functools.partial(inner_kernel, sizes, marks, rows),
+        inner_kernel,
         "inner_projection",
         (
             shape((2, long, width), BF16),
             shape((2, long, LANES), BF16),
             shape((2, long, LANES), F32),
         ),
-        [ints, hidden, *inner_parts],
-        [pltpu.VMEM((model, wide), BF16)] if marks else [], us=4.3
+        [hidden, inner_weights],
+        us=3.5,
     )
     shared_other = swap(shared, "tp")
     init = lax.dynamic_slice_in_dim(init_states, me * heads, heads, 1)
@@ -755,8 +790,38 @@
             shape((2, width + 16, N), BF16),
         ),
         [ints, raw, shared, shared_other, step, params, init],
-        [pltpu.VMEM((width, N), F32), pltpu.VMEM((8, N), F32)], us=9.3
-    )
+        after=gate_parts[2:3],
+        us=7,
+    )
+    if aligned:
+        gate_marks = [(s, dy, 0) for s in range(t_count) for dy in (0, 1)]
+        gate_weights = call(
+            functools.partial(weights_kernel, sizes, gate_marks, rows),
+            "gate_weights",
+            shape((model, width), BF16),
+            [ints, *gate_parts],
+            after=[summary],
+            us=1,
+        )
+    else:
+        gate_weights = in_order(gate_parts, index)
+    if out_rows % TILE == 0:
+        columns = call(
+            functools.partial(columns_kernel, sizes, count, out_rows),
+            "columns",
+            shape((model, width), BF16),
+            [ints, *out_parts],
+            after=[summary],
+            us=1,
+        )
+    else:
+        index = [
+            stored_block(s, dy, 2 * (me ^ rel), info) // 2
+            for s in range(t_count)
+            for dy in (0, 1)
+            for rel in range(4)
+        ]
+        columns = in_order(out_parts, jnp.stack(index))
     theirs = swap(summary, "y")
     block = call(
         functools.partial(compose_kernel, heads, sizes),
@@ -764,16 +829,8 @@
         shape((width + 16, N), BF16),
         [ints, summary, theirs],
     )
+    composed = block
     onward = [(i, i + 1) for i in range(t_count - 1)]
-    gate_marks = [(s, dy, 0) for s in range(t_count) for dy in (0, 1)] if aligned else None
-    gate = call(
-        functools.partial(gate_kernel, sizes, gate_marks, rows),
-        "gate_projection",
-        shape((2, long, width), BF16),
-        [ints, hidden, *gate_parts],
-        [pltpu.VMEM((model, width), BF16)] if aligned else [],
-        after=[block], us=3
-    )
     block = lax.ppermute(block, "t", onward)
     entering = block
     if t_count > 2:
@@ -788,31 +845,42 @@
         functools.partial(within_kernel, heads, tokens, sizes),
         "within_chunks",
         shape((chunks, PAGE, width), F32),
-        [ints, x, b_in, c_in, cum, dt, params, init], us=5.4
-    )
-    mixed, squares, *pages = call(
+        [ints, x, b_in, c_in, cum, dt, params, init],
+        after=[composed, out_parts[2]],
+        us=5,
+    )
+    states, *pages = call(
+        functools.partial(enter_kernel, heads, tokens, sizes),
+        "entering_states",
+        (shape((chunks, width, N), BF16), *[shape((tokens // PAGE, width, N), BF16)] * 4),
+        [ints, summary, theirs, entering, ends, factors],
+        [pltpu.VMEM((2, width, N), F32)],
+    )
+    got_pages = [pages[0], swap(pages[1], "b"), swap(pages[2], "a"), lax.ppermute(pages[3], ("a", "b"), across)]
+    gate = call(
+        gate_kernel,
+        "gate_projection",
+        shape((2, long, width), BF16),
+        [hidden, gate_weights],
+        after=[states],
+        us=2.5,
+    )
+    mixed, squares = call(
         functools.partial(finish_kernel, heads, tokens, sizes),
         "finish",
-        (
-            shape((chunks, PAGE, width), BF16),
-            shape((chunks, 8, PAGE), F32),
-            *[shape((tokens // PAGE, width, N), BF16)] * 4,
-        ),
-        [ints, summary, theirs, entering, c_in, cum, ends, factors, y_within, gate, params],
-        [pltpu.VMEM((2, width, N), F32), pltpu.VMEM((width, N), F32)], us=4.8
-    )
-
-    across = [(i, i ^ 3) for i in range(4)]
-    got = [pages[0], swap(pages[1], "b"), swap(pages[2], "a"), lax.ppermute(pages[3], ("a", "b"), across)]
-    per = tokens // PAGE
-    state_pages = call(
-        functools.partial(page_kernel, sizes), "pages", shape((per, 4, width, N), F32), [ints, *got], us=1.8
-    ).reshape(per, half_heads, head_dim, N)
+        (shape((chunks, PAGE, width), BF16), shape((chunks, 8, PAGE), F32)),
+        [ints, states, c_in, cum, y_within, gate, params],
+        after=got_pages[1:2],
+        us=4,
+    )
 
     dims = shape((4, PAGE + TILE, model), BF16)
-    sent = call(functools.partial(mix_kernel, sizes, False), "mix_send", dims, [ints, mixed, squares, columns], us=2.1)
+    sent = call(functools.partial(mix_kernel, sizes, False), "mix_send", dims, [ints, mixed, squares, columns],
+                after=got_pages[2:4], us=2.1)
+    mix_sent = sent
     got = swap(sent, "tp")
-    kept = call(functools.partial(mix_kernel, sizes, True), "mix_keep", dims, [ints, mixed, squares, columns], us=2.1)
+    kept = call(functools.partial(mix_kernel, sizes, True), "mix_keep", dims, [ints, mixed, squares, columns],
+                after=[mix_sent], us=2.1)
     mid = model // 2
     send_b, send_a, keep_b, keep_a = call(
         add_cores_kernel,
@@ -825,6 +893,11 @@
         ),
         [kept, got],
     )
+    per = tokens // PAGE
+    state_pages = call(
+        functools.partial(page_kernel, sizes), "pages", shape((per, 4, width, N), F32), [ints, *got_pages], after=[send_b], us=1.8
+    )
+
     got_b, got_a = swap(send_b, "b"), swap(send_a, "a")
     send_a, send_b, left, right = call(
         add_second_kernel,
@@ -844,7 +917,7 @@
         shape((PAGE, model), BF16),
         [left, got_left, right, got_right],
     )
-    return (mixed_out, state_pages)
+    return (mixed_out, state_pages.reshape(per, half_heads, head_dim, N))
 
 
 def solution(mesh):

time: 154 us -> 142 us (0.922)
  local copies, waits for them, and re-layouts: 14.8 us -> 7.26 us
  waiting for transfers between devices: 36.6 us -> 31 us
    ppermute x24 -> x26, starting transfers between devices: 21.9 us -> 35.9 us  [swap(): return lax.ppermute(x, axis, [(0, 1), (1, 0)])]
    ppermute x24 -> x26, waiting for transfers between devices: 33.1 us -> 21.5 us  [swap(): return lax.ppermute(x, axis, [(0, 1), (1, 0)])]
    all_to_all x1 -> x0, starting transfers between devices: 10.2 us -> none  [on_device(): out_got = lax.all_to_all(out_send, ('a', 'b'), 0, 0, tiled=True)]
    unnamed x70 -> x32, local copies, waits for them, and re-layouts: 9.88 us -> 4.38 us
    ppermute x4, starting transfers between devices: 10.6 us -> 6.34 us  [round_t(): return lax.ppermute(x, 't', [(i, (i + 1) % count) for i in range(count)])]
    ppermute x0 -> x1, waiting for transfers between devices: none -> 3.79 us  [on_device(): lax.ppermute(out_send[3], ('a', 'b'), across)]
    all_to_all x1, waiting for transfers between devices: 0.01 us -> 2.9 us  [on_device(): inner_got = lax.all_to_all(inner_send, GROUP, 0, 0, tiled=True)]
    broadcast_in_dim x2, local copies, waits for them, and re-layouts: 0.01 us -> 1.89 us  [on_device(): top = jnp.concatenate([conv_inner, bias_inner[None], norm_gain[None]])]
  transfers between devices with their start and end apart: 34 -> 36, of which waited for: 13 -> 14; matrix products, arithmetic and copies ran while one was open for 4% -> 2% of each run, Pallas kernels for 24% -> 27%
where the time goes in v3:
time: 142 us
  starting transfers between devices  58.5 us (41%)
  Pallas kernels  42.7 us (30%)
  waiting for transfers between devices  31 us (22%)
  local copies, waits for them, and re-layouts  7.26 us (5%)
  other arithmetic  1.42 us (1%)
    pallas_call x24, Pallas kernels, call(): pl.pallas_call(kernel, name=name, out_shape=out_shape, in_specs=specs, ou...  42.7 us
    ppermute x26, starting transfers between devices, swap(): return lax.ppermute(x, axis, [(0, 1), (1, 0)])  35.9 us
    ppermute x26, waiting for transfers between devices, swap(): return lax.ppermute(x, axis, [(0, 1), (1, 0)])  21.5 us
    ppermute x4, starting transfers between devices, round_t(): return lax.ppermute(x, 't', [(i, (i + 1) % count) for i in range(count)])  6.34 us
    all_to_all x1, starting transfers between devices, on_device(): inner_got = lax.all_to_all(inner_send, GROUP, 0, 0, tiled=True)  5.23 us
    unnamed x32, local copies, waits for them, and re-layouts  4.38 us
    ppermute x1, starting transfers between devices, on_device(): block = lax.ppermute(block, 't', onward)  3.99 us
    ppermute x1, waiting for transfers between devices, on_device(): lax.ppermute(out_send[3], ('a', 'b'), across)  3.79 us
  transfers between devices with their start and end apart: 36, of which 14 were waited for; matrix products, arithmetic and copies ran while one was open for 2% of the time, Pallas kernels for 27%

profile of v3, /device:TPU:0, one launch (start us, length us, event | category | flops | bytes accessed | tf_op | source)
XLA Modules:
  0.0 142.0 jit_solution(226588484671380766)
XLA Ops:
  0.7 0.9 concatenate.15.refs_0_
  1.6 1.2 copy-done.2
  2.8 0.8 own_rows.1
  3.6 0.6 copy-done.8
  4.8 0.9 copy-done.1
  5.7 5.2 %all-to-all-start = ((bf16[8,48,1024]{2,1,0:T(8,128)(2,1)}), bf16[8,48,1024]{2,1,0:T(8,128)(2,1)}, u32[]{:S(2)}, u32[]{:S(2)}) async-start(bf16[8,48,1024]{2,1,0:T(8,128)(2,1)} %copy-done.1), calls=%async_computation | async-start | bytes 1572864 | tf_op jit(solution)/shard_map/all_to_all | solution.py:686
  10.9 2.0 %collective-permute-start = (bf16[128,1536]{1,0:T(8,128)(2,1)S(1)}, bf16[128,1536]{1,0:T(8,128)(2,1)}, u32[]{:S(2)}, u32[]{:S(2)}) collective-permute-start(bf16[128,1536]{1,0:T(8,128)(2,1)S(1)} %get-tuple-element.40.refs_3_), channel_id=1, source_target_pairs={{0,2},{2,0},{1,3},{3,1},{4,6},{6,4},{5,7},{7,5},{8,10},{10,8},{9,1... | collective-permute-start | bytes 1179656 | tf_op jit(solution)/shard_map/ppermute | solution.py:63
  12.9 1.5 %collective-permute-start.1 = (bf16[128,1536]{1,0:T(8,128)(2,1)S(1)}, bf16[128,1536]{1,0:T(8,128)(2,1)}, u32[]{:S(2)}, u32[]{:S(2)}) collective-permute-start(bf16[128,1536]{1,0:T(8,128)(2,1)S(1)} %get-tuple-element.40.refs_3_), channel_id=1, source_target_pairs={{0,8},{8,0},{1,9},{9,1},{2,10},{10,2},{3,11},{11,3},{4,12},{12,4},... | collective-permute-start | bytes 1179656 | tf_op jit(solution)/shard_map/ppermute | solution.py:63
  14.4 1.3 collective-permute-start.2
  15.7 1.3 collective-permute-start.3
  17.0 0.6 broadcast_in_dim.10
  17.6 1.3 broadcast_in_dim.9
  18.9 0.7 select_maximum_fusion.3
  19.6 0.7 select_maximum_fusion.4
  20.3 2.9 %all-to-all-done.refs_0_ = bf16[8,48,1024]{2,1,0:T(8,128)(2,1)} async-done(((bf16[8,48,1024]{2,1,0:T(8,128)(2,1)}), bf16[8,48,1024]{2,1,0:T(8,128)(2,1)}, u32[]{:S(2)}, u32[]{:S(2)}) %all-to-all-start) | async-done | bytes 786464 | tf_op jit(solution)/shard_map/all_to_all | solution.py:686
  23.2 2.0 %repack_inner.1 = (bf16[400,512]{1,0:T(8,128)(2,1)}, bf16[192,512]{1,0:T(8,128)(2,1)S(1)}, bf16[208,512]{1,0:T(8,128)(2,1)S(1)}, bf16[384,384]{1,0:T(8,128)(2,1)S(1)}) custom-call(bf16[8,48,1024]{2,1,0:T(8,128)(2,1)} %all-to-all-done.refs_0_), custom_call_target="tpu_custom_call" | custom-call | flops 1000000000 | bytes 3000000 | tf_op jit(solution)/shard_map/repack_inner/pallas_call | solution.py:36
  25.2 0.7 copy-done.9
  25.9 2.9 %collective-permute-start.11 = (bf16[192,512]{1,0:T(8,128)(2,1)S(1)}, bf16[192,512]{1,0:T(8,128)(2,1)}, u32[]{:S(2)}, u32[]{:S(2)}) collective-permute-start(bf16[192,512]{1,0:T(8,128)(2,1)S(1)} %get-tuple-element.45), channel_id=1, source_target_pairs={{0,16},{16,0},{1,17},{17,1},{2,18},{18,2},{3,19},{19,3},{4,20},{20... | collective-permute-start | bytes 589832 | tf_op jit(solution)/shard_map/ppermute | solution.py:599
  28.9 7.7 %collective-permute-start.10 = (bf16[400,512]{1,0:T(8,128)(2,1)}, bf16[400,512]{1,0:T(8,128)(2,1)}, u32[]{:S(2)}, u32[]{:S(2)}) collective-permute-start(bf16[400,512]{1,0:T(8,128)(2,1)} %get-tuple-element.42.refs_5_.refs_1_), channel_id=1, source_target_pairs={{0,4},{4,0},{1,5},{5,1},{2,6},{6,2},{3,7},{7,3},{8,12},{12,8},{9,1... | collective-permute-start | bytes 1228808 | tf_op jit(solution)/shard_map/ppermute | solution.py:63
  36.6 1.9 %forward_rows.1 = (bf16[64,1536]{1,0:T(8,128)(2,1)}, bf16[80,1536]{1,0:T(8,128)(2,1)}) custom-call(s32[58]{0:T(128)S(1)} %concatenate.15.refs_0_, bf16[128,1536]{1,0:T(8,128)(2,1)} %collective-permute-done.refs_1_.refs_2_, bf16[128,1536]{1,0:T(8,128)(2,1)} %collective-permute-done.1.refs_2_.refs_3_, ...), custom_call_target="tpu_custom_call" | custom-call | flops 1000000000 | bytes 3000000 | tf_op jit(solution)/shard_map/forward_rows/pallas_call | solution.py:36
  38.6 3.8 %collective-permute-start.4 = (bf16[64,1536]{1,0:T(8,128)(2,1)}, bf16[64,1536]{1,0:T(8,128)(2,1)}, u32[]{:S(2)}, u32[]{:S(2)}) collective-permute-start(bf16[64,1536]{1,0:T(8,128)(2,1)} %get-tuple-element.43), channel_id=1, source_target_pairs={{0,2},{2,0},{1,3},{3,1},{4,6},{6,4},{5,7},{7,5},{8,10},{10,8},{9,1... | collective-permute-start | bytes 589832 | tf_op jit(solution)/shard_map/ppermute | solution.py:63
  42.4 1.4 collective-permute-start.5
  43.8 2.0 %collective-permute-start.13 = (bf16[192,512]{1,0:T(8,128)(2,1)}, bf16[192,512]{1,0:T(8,128)(2,1)}, u32[]{:S(2)}, u32[]{:S(2)}) collective-permute-start(bf16[192,512]{1,0:T(8,128)(2,1)} %collective-permute-done.11.refs_3_), channel_id=1, source_target_pairs={{0,4},{4,0},{1,5},{5,1},{2,6},{6,2},{3,7},{7,3},{8,12},{12,8},{9,1... | collective-permute-start | bytes 589832 | tf_op jit(solution)/shard_map/ppermute | solution.py:63
  46.2 2.4 %collective-permute-start.14 = (bf16[208,512]{1,0:T(8,128)(2,1)}, bf16[208,512]{1,0:T(8,128)(2,1)}, u32[]{:S(2)}, u32[]{:S(2)}) collective-permute-start(bf16[208,512]{1,0:T(8,128)(2,1)} %collective-permute-done.12.refs_4_.refs_1_), channel_id=1, source_target_pairs={{0,4},{4,0},{1,5},{5,1},{2,6},{6,2},{3,7},{7,3},{8,12},{12,8},{9,1... | collective-permute-start | bytes 638984 | tf_op jit(solution)/shard_map/ppermute | solution.py:63
  48.6 1.0 copy-done.10
  50.5 2.7 %collective-permute-start.16 = (bf16[384,384]{1,0:T(8,128)(2,1)S(1)}, bf16[384,384]{1,0:T(8,128)(2,1)S(1)}, u32[]{:S(2)}, u32[]{:S(2)}) collective-permute-start(bf16[384,384]{1,0:T(8,128)(2,1)S(1)} %gate_part.1.refs_1_), channel_id=1, source_target_pairs={{0,16},{16,0},{1,17},{17,1},{2,18},{18,2},{3,19},{19,3},{4,20},{20... | collective-permute-start | bytes 884744 | tf_op jit(solution)/shard_map/ppermute | solution.py:599
  53.1 1.6 %collective-permute-done.14.refs_6_ = bf16[208,512]{1,0:T(8,128)(2,1)} collective-permute-done((bf16[208,512]{1,0:T(8,128)(2,1)}, bf16[208,512]{1,0:T(8,128)(2,1)}, u32[]{:S(2)}, u32[]{:S(2)}) %collective-permute-start.14) | collective-permute-done | bytes 213024 | tf_op jit(solution)/shard_map/ppermute | solution.py:63
  54.7 1.7 %inner_weights.1.refs_1_ = bf16[1536,640]{1,0:T(8,128)(2,1)S(1)} custom-call(s32[58]{0:T(128)S(1)} %concatenate.15.refs_0_, bf16[400,512]{1,0:T(8,128)(2,1)} %get-tuple-element.42.refs_5_.refs_1_, bf16[400,512]{1,0:T(8,128)(2,1)} %collective-permute-done.10.refs_2_, bf16[192,512]{1,0:T(8,128)(2,1)} %collective-permute-done.11.refs_3_, ...), custom_call_target="tpu_custom_call" | custom-call | flops 15000000512 | bytes 45000000 | tf_op jit(solution)/shard_map/inner_weights/pallas_call | solution.py:36
  56.5 1.4 %assemble_rows.1.refs_0_ = bf16[2,528,1536]{2,1,0:T(8,128)(2,1)S(1)} custom-call(s32[58]{0:T(128)S(1)} %concatenate.15.refs_0_, bf16[256,1536]{1,0:T(8,128)(2,1)S(1)} %copy-done.3, bf16[128,1536]{1,0:T(8,128)(2,1)} %collective-permute-done.refs_1_.refs_2_, bf16[128,1536]{1,0:T(8,128)(2,1)} %collective-permute-done.1.refs_2_.refs_3_, ...), custom_call_target="tpu_custom_call" | custom-call | flops 2000000000 | bytes 6000000 | tf_op jit(solution)/shard_map/assemble_rows/pallas_call | solution.py:36
  57.9 2.7 %inner_projection.1 = (bf16[2,528,384]{2,1,0:T(8,128)(2,1)S(1)}, bf16[2,528,128]{2,1,0:T(8,128)(2,1)S(1)}, f32[2,528,128]{2,1,0:T(8,128)S(1)}) custom-call(bf16[2,528,1536]{2,1,0:T(8,128)(2,1)S(1)} %assemble_rows.1.refs_0_, bf16[1536,640]{1,0:T(8,128)(2,1)S(1)} %inner_weights.1.refs_1_), custom_call_target="tpu_custom_call" | custom-call | flops 3500000000 | bytes 10500000 | tf_op jit(solution)/shard_map/inner_projection/pallas_call | solution.py:36
  60.6 0.6 collective-permute-start.15
  61.2 0.6 pack_out.1
  61.7 3.4 %collective-permute-start.19 = (bf16[96,384]{1,0:T(8,128)(2,1)S(1)}, bf16[96,384]{1,0:T(8,128)(2,1)S(1)}, u32[]{:S(2)}, u32[]{:S(2)}) collective-permute-start(bf16[96,384]{1,0:T(8,128)(2,1)S(1)} %get-tuple-element.61), channel_id=1, source_target_pairs={{0,2},{2,0},{1,3},{3,1},{4,6},{6,4},{5,7},{7,5},{8,10},{10,8},{9,1... | collective-permute-start | bytes 221192 | tf_op jit(solution)/shard_map/ppermute | solution.py:63
  65.2 3.2 %collective-permute-start.20 = (bf16[96,384]{1,0:T(8,128)(2,1)S(1)}, bf16[96,384]{1,0:T(8,128)(2,1)S(1)}, u32[]{:S(2)}, u32[]{:S(2)}) collective-permute-start(bf16[96,384]{1,0:T(8,128)(2,1)S(1)} %get-tuple-element.62), channel_id=1, source_target_pairs={{0,8},{8,0},{1,9},{9,1},{2,10},{10,2},{3,11},{11,3},{4,12},{12,4},... | collective-permute-start | bytes 221192 | tf_op jit(solution)/shard_map/ppermute | solution.py:63
  68.3 1.4 collective-permute-start.21
  70.1 0.7 collective-permute-done.20.refs_2_
  70.8 3.8 %collective-permute-done.21.refs_3_ = bf16[96,384]{1,0:T(8,128)(2,1)S(1)} collective-permute-done((bf16[96,384]{1,0:T(8,128)(2,1)S(1)}, bf16[96,384]{1,0:T(8,128)(2,1)S(1)}, u32[]{:S(2)}, u32[]{:S(2)}) %collective-permute-start.21) | collective-permute-done | bytes 73760 | tf_op jit(solution)/shard_map/ppermute | solution.py:743
  74.7 0.7 collective-permute-start.22
  75.4 0.6 collective-permute-start.24
  76.0 9.0 %states.1 = (bf16[8,128,384]{2,1,0:T(8,128)(2,1)S(1)}, bf16[8,128,128]{2,1,0:T(8,128)(2,1)S(1)}, bf16[8,128,128]{2,1,0:T(8,128)(2,1)S(1)}, f32[8,128,128]{2,1,0:...) custom-call(s32[58]{0:T(128)S(1)} %concatenate.15.refs_0_, ...), custom_call_target="tpu_custom_call" | custom-call | flops 7000000000 | bytes 21000000 | tf_op jit(solution)/shard_map/states/pallas_call | solution.py:36
  84.9 0.6 collective-permute-start.17
  85.5 1.5 %collective-permute-start.26 = (bf16[384,384]{1,0:T(8,128)(2,1)S(1)}, bf16[384,384]{1,0:T(8,128)(2,1)S(1)}, u32[]{:S(2)}, u32[]{:S(2)}) collective-permute-start(bf16[384,384]{1,0:T(8,128)(2,1)S(1)} %out_part.1.refs_1_), channel_id=1, source_target_pairs={{0,4},{4,0},{1,5},{5,1},{2,6},{6,2},{3,7},{7,3},{8,12},{12,8},{9,1... | collective-permute-start | bytes 884744 | tf_op jit(solution)/shard_map/ppermute | solution.py:63
  87.0 2.4 %collective-permute-done.22.refs_9_.refs_3_ = bf16[384,384]{1,0:T(8,128)(2,1)S(1)} collective-permute-done((bf16[384,384]{1,0:T(8,128)(2,1)S(1)}, bf16[384,384]{1,0:T(8,128)(2,1)S(1)}, u32[]{:S(2)}, u32[]{:S(2)}) %collective-permute-start.22) | collective-permute-done | bytes 294944 | tf_op jit(solution)/shard_map/ppermute | solution.py:599
  89.4 2.1 %collective-permute-start.27 = (bf16[384,384]{1,0:T(8,128)(2,1)S(1)}, bf16[384,384]{1,0:T(8,128)(2,1)S(1)}, u32[]{:S(2)}, u32[]{:S(2)}) collective-permute-start(bf16[384,384]{1,0:T(8,128)(2,1)S(1)} %collective-permute-done.22.refs_9_.refs_3_), channel_id=1, source_target_pairs={{0,4},{4,0},{1,5},{5,1},{2,6},{6,2},{3,7},{7,3},{8,12},{12,8},{9,1... | collective-permute-start | bytes 884744 | tf_op jit(solution)/shard_map/ppermute | solution.py:63
  91.6 0.7 gate_weights.1.refs_1_
  92.3 0.7 collective-permute-done.17.refs_2_
  93.0 0.6 compose.1.refs_8_
  93.6 4.0 %collective-permute-start.18 = (bf16[400,128]{1,0:T(8,128)(2,1)S(1)}, bf16[400,128]{1,0:T(8,128)(2,1)S(1)}, u32[]{:S(2)}, u32[]{:S(2)}) collective-permute-start(bf16[400,128]{1,0:T(8,128)(2,1)S(1)} %compose.1.refs_8_), channel_id=1, source_target_pairs={{0,16},{1,17},{2,18},{3,19},{4,20},{5,21},{6,22},{7,23},{8,24},{9,... | collective-permute-start | bytes 307208 | tf_op jit(solution)/shard_map/ppermute | solution.py:834
  97.6 6.0 %within_chunks.1.refs_4_ = f32[8,128,384]{2,1,0:T(8,128)S(1)} custom-call(s32[58]{0:T(128)S(1)} %concatenate.15.refs_0_, bf16[8,128,384]{2,1,0:T(8,128)(2,1)S(1)} %get-tuple-element.57.refs_1_, bf16[8,128,128]{2,1,0:T(8,128)(2,1)S(1)} %get-tuple-element.58.refs_2_, bf16[8,128,128]{2,1,0:T(8,128)(2,1)S(1)} %get-tuple-element.55.refs_3_.refs_2_, ...), custom_call_target="tpu_custom_call" | custom-call | flops 5000000000 | bytes 15000000 | tf_op jit(solution)/shard_map/within_chunks/pallas_call | solution.py:36
  103.7 0.9 entering_states.1
  104.9 3.2 %collective-permute-start.29 = (bf16[2,384,128]{2,1,0:T(8,128)(2,1)S(1)}, bf16[2,384,128]{2,1,0:T(8,128)(2,1)S(1)}, u32[]{:S(2)}, u32[]{:S(2)}) collective-permute-start(bf16[2,384,128]{2,1,0:T(8,128)(2,1)S(1)} %get-tuple-element.68), channel_id=1, source_target_pairs={{0,10},{2,8},{8,2},{10,0},{1,11},{3,9},{9,3},{11,1},{4,14},{6,12},... | collective-permute-start | bytes 589832 | tf_op jit(solution)/shard_map/ppermute | solution.py:859
  108.1 1.8 %gate_projection.1.refs_5_ = bf16[2,528,384]{2,1,0:T(8,128)(2,1)S(1)} custom-call(bf16[2,528,1536]{2,1,0:T(8,128)(2,1)S(1)} %assemble_rows.1.refs_0_, bf16[1536,384]{1,0:T(8,128)(2,1)S(1)} %gate_weights.1.refs_1_, bf16[8,384,128]{2,1,0:T(8,128)(2,1)S(1)} %get-tuple-element.54.refs_2_.refs_1_), custom_call_target="tpu_custom_call" | custom-call | flops 2500000000 | bytes 7500000 | tf_op jit(solution)/shard_map/gate_projection/pallas_call | solution.py:36
  110.0 0.9 columns.1.refs_3_
  110.9 1.2 collective-permute-done.25.refs_7_.refs_2_
  112.0 3.6 %finish.1 = (bf16[8,128,384]{2,1,0:T(8,128)(2,1)S(1)}, f32[8,8,128]{2,1,0:T(8,128)S(1)}) custom-call(s32[58]{0:T(128)S(1)} %concatenate.15.refs_0_, bf16[8,384,128]{2,1,0:T(8,128)(2,1)S(1)} %get-tuple-element.54.refs_2_.refs_1_, bf16[8,128,128]{2,1,0:T(8,128)(2,1)S(1)} %get-tuple-element.55.refs_3_.refs_2_, ...), custom_call_target="tpu_custom_call" | custom-call | flops 4000000000 | bytes 12000000 | tf_op jit(solution)/shard_map/finish/pallas_call | solution.py:36
  115.6 2.1 %mix_send.1.refs_4_ = bf16[4,144,1536]{2,1,0:T(8,128)(2,1)S(1)} custom-call(s32[58]{0:T(128)S(1)} %concatenate.15.refs_0_, bf16[8,128,384]{2,1,0:T(8,128)(2,1)S(1)} %get-tuple-element.65.refs_1_, f32[8,8,128]{2,1,0:T(8,128)S(1)} %get-tuple-element.66.refs_2_, bf16[1536,384]{1,0:T(8,128)(2,1)S(1)} %columns.1.refs_3_, ...), custom_call_target="tpu_custom_call" | custom-call | flops 2100000000 | bytes 6300000 | tf_op jit(solution)/shard_map/mix_send/pallas_call | solution.py:36
  117.9 2.1 %mix_keep.1.refs_0_ = bf16[4,144,1536]{2,1,0:T(8,128)(2,1)S(1)} custom-call(s32[58]{0:T(128)S(1)} %concatenate.15.refs_0_, bf16[8,128,384]{2,1,0:T(8,128)(2,1)S(1)} %get-tuple-element.65.refs_1_, f32[8,8,128]{2,1,0:T(8,128)S(1)} %get-tuple-element.66.refs_2_, bf16[1536,384]{1,0:T(8,128)(2,1)S(1)} %columns.1.refs_3_, bf16[4,144,1536]{2,1,0:T(8,128)(2,1)S(1)} %mix_send.1.refs_4_), custom_call_target="tpu_custom_call" | custom-call | flops 2100000000 | bytes 6300000 | tf_op jit(solution)/shard_map/mix_keep/pallas_call | solution.py:36
  120.0 1.5 %collective-permute-done.30.refs_1_ = bf16[4,144,1536]{2,1,0:T(8,128)(2,1)S(1)} collective-permute-done((bf16[4,144,1536]{2,1,0:T(8,128)(2,1)S(1)}, bf16[4,144,1536]{2,1,0:T(8,128)(2,1)S(1)}, u32[]{:S(2)}, u32[]{:S(2)}) %collective-permute-start.30) | collective-permute-done | bytes 1769504 | tf_op jit(solution)/shard_map/ppermute | solution.py:63
  122.5 10.8 %collective-permute-done.32.refs_3_ = bf16[2,128,768]{2,1,0:T(8,128)(2,1)S(1)} collective-permute-done((bf16[2,128,768]{2,1,0:T(8,128)(2,1)S(1)}, bf16[2,128,768]{2,1,0:T(8,128)(2,1)S(1)}, u32[]{:S(2)}, u32[]{:S(2)}) %collective-permute-start.32) | collective-permute-done | bytes 393248 | tf_op jit(solution)/shard_map/ppermute | solution.py:63
  133.3 0.9 collective-permute-done.31.refs_1_
  134.6 0.8 collective-permute-start.34
  135.4 1.8 %pages.1 = f32[2,4,384,128]{3,2,1,0:T(8,128)} custom-call(s32[58]{0:T(128)S(1)} %concatenate.15.refs_0_, bf16[2,384,128]{2,1,0:T(8,128)(2,1)S(1)} %get-tuple-element.77.refs_1_, bf16[2,384,128]{2,1,0:T(8,128)(2,1)S(1)} %collective-permute-done.25.refs_7_.refs_2_, bf16[2,384,128]{2,1,0:T(8,128)(2,1)S(1)} %collective-permute-done.28.refs_4_.refs_3_, ...), custom_call_target="tpu_custom_call" | custom-call | flops 1800000000 | bytes 5400000 | tf_op jit(solution)/shard_map/pages/pallas_call | solution.py:36
  137.2 3.4 %collective-permute-done.34.refs_3_ = bf16[128,768]{1,0:T(8,128)(2,1)S(1)} collective-permute-done((bf16[128,768]{1,0:T(8,128)(2,1)S(1)}, bf16[128,768]{1,0:T(8,128)(2,1)S(1)}, u32[]{:S(2)}, u32[]{:S(2)}) %collective-permute-start.34) | collective-permute-done | bytes 196640 | tf_op jit(solution)/shard_map/ppermute | solution.py:63
  141.1 0.9 add_last.1
  (72 shorter events, 4.7 us)
Async XLA Ops:
  0.6 69.1 %copy-start = (f32[4,24,64,128]{3,2,1,0:T(8,128)S(1)}, f32[4,24,64,128]{3,2,1,0:T(8,128)}, u32[]{:S(2)}) copy-start(f32[4,24,64,128]{3,2,1,0:T(8,128)} %param.34) | copy-start | bytes 9437188
  1.6 1.2 copy-start.2
  2.8 1.4 %copy-start.4 = (f32[48,3072]{1,0:T(8,128)S(1)}, f32[48,3072]{1,0:T(8,128)}, u32[]{:S(2)}) copy-start(f32[48,3072]{1,0:T(8,128)} %refs_0_.1) | copy-start | bytes 1769476
  2.8 1.4 %copy-start.5 = (f32[48,3072]{1,0:T(8,128)S(1)}, f32[48,3072]{1,0:T(8,128)}, u32[]{:S(2)}) copy-start(f32[48,3072]{1,0:T(8,128)} %refs_2_.1) | copy-start | bytes 1769476
  2.8 1.4 %copy-start.7 = (f32[48,304]{1,0:T(8,128)S(1)}, f32[48,304]{1,0:T(8,128)}, u32[]{:S(2)}) copy-start(f32[48,304]{1,0:T(8,128)} %refs_1_.4) | copy-start | bytes 175108
  3.6 0.6 copy-start.8
  4.2 12.7 %copy-start.14 = (f32[1536]{0:T(1024)S(1)}, f32[1536]{0:T(1024)}, u32[]{:S(2)}) copy-start(f32[1536]{0:T(1024)} %param.30) | copy-start | bytes 18436
  4.2 14.6 %copy-start.15 = (f32[4,256]{1,0:T(4,128)S(1)}, f32[4,256]{1,0:T(4,128)}, u32[]{:S(2)}) copy-start(f32[4,256]{1,0:T(4,128)} %param.24) | copy-start | bytes 12292
  4.8 0.9 copy-start.1
  5.7 17.5 %all-to-all-start = ((bf16[8,48,1024]{2,1,0:T(8,128)(2,1)}), bf16[8,48,1024]{2,1,0:T(8,128)(2,1)}, u32[]{:S(2)}, u32[]{:S(2)}) async-start(bf16[8,48,1024]{2,1,0:T(8,128)(2,1)} %copy-done.1), calls=%async_computation | async-start | bytes 1572864 | tf_op jit(solution)/shard_map/all_to_all | solution.py:686
  10.9 25.7 %collective-permute-start = (bf16[128,1536]{1,0:T(8,128)(2,1)S(1)}, bf16[128,1536]{1,0:T(8,128)(2,1)}, u32[]{:S(2)}, u32[]{:S(2)}) collective-permute-start(bf16[128,1536]{1,0:T(8,128)(2,1)S(1)} %get-tuple-element.40.refs_3_), channel_id=1, source_target_pairs={{0,2},{2,0},{1,3},{3,1},{4,6},{6,4},{5,7},{7,5},{8,10},{10,8},{9,1... | collective-permute-start | bytes 1179656 | tf_op jit(solution)/shard_map/ppermute | solution.py:63
  12.9 23.7 %collective-permute-start.1 = (bf16[128,1536]{1,0:T(8,128)(2,1)S(1)}, bf16[128,1536]{1,0:T(8,128)(2,1)}, u32[]{:S(2)}, u32[]{:S(2)}) collective-permute-start(bf16[128,1536]{1,0:T(8,128)(2,1)S(1)} %get-tuple-element.40.refs_3_), channel_id=1, source_target_pairs={{0,8},{8,0},{1,9},{9,1},{2,10},{10,2},{3,11},{11,3},{4,12},{12,4},... | collective-permute-start | bytes 1179656 | tf_op jit(solution)/shard_map/ppermute | solution.py:63
  14.4 14.4 %collective-permute-start.2 = (bf16[16,1536]{1,0:T(8,128)(2,1)}, bf16[16,1536]{1,0:T(8,128)(2,1)}, u32[]{:S(2)}, u32[]{:S(2)}) collective-permute-start(bf16[16,1536]{1,0:T(8,128)(2,1)} %copy-done.8), channel_id=1, source_target_pairs={{2,4},{6,8},{10,12},{14,16},{18,20},{22,24},{26,28},{3,5},{7,9},{1... | collective-permute-start | bytes 147464 | tf_op jit(solution)/shard_map/ppermute | solution.py:715
  15.7 13.2 %collective-permute-start.3 = (bf16[16,1536]{1,0:T(8,128)(2,1)}, bf16[16,1536]{1,0:T(8,128)(2,1)}, u32[]{:S(2)}, u32[]{:S(2)}) collective-permute-start(bf16[16,1536]{1,0:T(8,128)(2,1)} %copy-done.8), channel_id=1, source_target_pairs={{2,6},{6,10},{10,14},{14,18},{18,22},{22,26},{26,30},{3,7},{7,11},... | collective-permute-start | bytes 147464 | tf_op jit(solution)/shard_map/ppermute | solution.py:716
  23.1 5.7 %copy-start.11 = (f32[1,1536]{1,0:T(1,128)S(1)}, f32[1,1536]{1,0:T(1,128)}, u32[]{:S(2)}) copy-start(f32[1,1536]{1,0:T(1,128)} %broadcast_in_dim.10) | copy-start | bytes 18436
  23.2 5.7 %copy-start.12 = (f32[1,1536]{1,0:T(1,128)S(1)}, f32[1,1536]{1,0:T(1,128)}, u32[]{:S(2)}) copy-start(f32[1,1536]{1,0:T(1,128)} %broadcast_in_dim.9) | copy-start | bytes 18436
  23.2 5.7 %copy-start.13 = (f32[4,1536]{1,0:T(4,128)S(1)}, f32[4,1536]{1,0:T(4,128)}, u32[]{:S(2)}) copy-start(f32[4,1536]{1,0:T(4,128)} %param.23) | copy-start | bytes 73732
  25.2 0.7 copy-start.9
  25.9 17.9 %collective-permute-start.11 = (bf16[192,512]{1,0:T(8,128)(2,1)S(1)}, bf16[192,512]{1,0:T(8,128)(2,1)}, u32[]{:S(2)}, u32[]{:S(2)}) collective-permute-start(bf16[192,512]{1,0:T(8,128)(2,1)S(1)} %get-tuple-element.45), channel_id=1, source_target_pairs={{0,16},{16,0},{1,17},{17,1},{2,18},{18,2},{3,19},{19,3},{4,20},{20... | collective-permute-start | bytes 589832 | tf_op jit(solution)/shard_map/ppermute | solution.py:599
  28.8 17.3 %collective-permute-start.12 = (bf16[208,512]{1,0:T(8,128)(2,1)S(1)}, bf16[208,512]{1,0:T(8,128)(2,1)}, u32[]{:S(2)}, u32[]{:S(2)}) collective-permute-start(bf16[208,512]{1,0:T(8,128)(2,1)S(1)} %get-tuple-element.46), channel_id=1, source_target_pairs={{0,16},{16,0},{1,17},{17,1},{2,18},{18,2},{3,19},{19,3},{4,20},{20... | collective-permute-start | bytes 638984 | tf_op jit(solution)/shard_map/ppermute | solution.py:599
  28.9 21.5 %collective-permute-start.10 = (bf16[400,512]{1,0:T(8,128)(2,1)}, bf16[400,512]{1,0:T(8,128)(2,1)}, u32[]{:S(2)}, u32[]{:S(2)}) collective-permute-start(bf16[400,512]{1,0:T(8,128)(2,1)} %get-tuple-element.42.refs_5_.refs_1_), channel_id=1, source_target_pairs={{0,4},{4,0},{1,5},{5,1},{2,6},{6,2},{3,7},{7,3},{8,12},{12,8},{9,1... | collective-permute-start | bytes 1228808 | tf_op jit(solution)/shard_map/ppermute | solution.py:63
  38.6 11.0 %collective-permute-start.4 = (bf16[64,1536]{1,0:T(8,128)(2,1)}, bf16[64,1536]{1,0:T(8,128)(2,1)}, u32[]{:S(2)}, u32[]{:S(2)}) collective-permute-start(bf16[64,1536]{1,0:T(8,128)(2,1)} %get-tuple-element.43), channel_id=1, source_target_pairs={{0,2},{2,0},{1,3},{3,1},{4,6},{6,4},{5,7},{7,5},{8,10},{10,8},{9,1... | collective-permute-start | bytes 589832 | tf_op jit(solution)/shard_map/ppermute | solution.py:63
  42.4 7.3 %collective-permute-start.5 = (bf16[80,1536]{1,0:T(8,128)(2,1)}, bf16[80,1536]{1,0:T(8,128)(2,1)S(1)}, u32[]{:S(2)}, u32[]{:S(2)}) collective-permute-start(bf16[80,1536]{1,0:T(8,128)(2,1)} %get-tuple-element.44), channel_id=1, source_target_pairs={{0,8},{8,0},{1,9},{9,1},{2,10},{10,2},{3,11},{11,3},{4,12},{12,4},... | collective-permute-start | bytes 737288 | tf_op jit(solution)/shard_map/ppermute | solution.py:63
  43.8 6.7 %collective-permute-start.13 = (bf16[192,512]{1,0:T(8,128)(2,1)}, bf16[192,512]{1,0:T(8,128)(2,1)}, u32[]{:S(2)}, u32[]{:S(2)}) collective-permute-start(bf16[192,512]{1,0:T(8,128)(2,1)} %collective-permute-done.11.refs_3_), channel_id=1, source_target_pairs={{0,4},{4,0},{1,5},{5,1},{2,6},{6,2},{3,7},{7,3},{8,12},{12,8},{9,1... | collective-permute-start | bytes 589832 | tf_op jit(solution)/shard_map/ppermute | solution.py:63
  46.2 8.6 %collective-permute-start.14 = (bf16[208,512]{1,0:T(8,128)(2,1)}, bf16[208,512]{1,0:T(8,128)(2,1)}, u32[]{:S(2)}, u32[]{:S(2)}) collective-permute-start(bf16[208,512]{1,0:T(8,128)(2,1)} %collective-permute-done.12.refs_4_.refs_1_), channel_id=1, source_target_pairs={{0,4},{4,0},{1,5},{5,1},{2,6},{6,2},{3,7},{7,3},{8,12},{12,8},{9,1... | collective-permute-start | bytes 638984 | tf_op jit(solution)/shard_map/ppermute | solution.py:63
  48.6 1.0 copy-start.10
  49.6 6.9 %copy-start.3 = (bf16[256,1536]{1,0:T(8,128)(2,1)S(1)}, bf16[256,1536]{1,0:T(8,128)(2,1)}, u32[]{:S(2)}) copy-start(bf16[256,1536]{1,0:T(8,128)(2,1)} %refs_1_.5) | copy-start | bytes 2359300
  49.6 6.8 %collective-permute-start.6 = (bf16[128,1536]{1,0:T(8,128)(2,1)}, bf16[128,1536]{1,0:T(8,128)(2,1)S(1)}, u32[]{:S(2)}, u32[]{:S(2)}) collective-permute-start(bf16[128,1536]{1,0:T(8,128)(2,1)} %collective-permute-done.refs_1_.refs_2_), channel_id=1, source_target_pairs={{0,1},{1,0},{2,3},{3,2},{4,5},{5,4},{6,7},{7,6},{8,9},{9,8},{10,11... | collective-permute-start | bytes 1179656 | tf_op jit(solution)/shard_map/ppermute | solution.py:63
  49.7 6.7 %collective-permute-start.7 = (bf16[128,1536]{1,0:T(8,128)(2,1)}, bf16[128,1536]{1,0:T(8,128)(2,1)S(1)}, u32[]{:S(2)}, u32[]{:S(2)}) collective-permute-start(bf16[128,1536]{1,0:T(8,128)(2,1)} %collective-permute-done.1.refs_2_.refs_3_), channel_id=1, source_target_pairs={{0,1},{1,0},{2,3},{3,2},{4,5},{5,4},{6,7},{7,6},{8,9},{9,8},{10,11... | collective-permute-start | bytes 1179656 | tf_op jit(solution)/shard_map/ppermute | solution.py:63
  50.5 6.0 %collective-permute-start.8 = (bf16[64,1536]{1,0:T(8,128)(2,1)}, bf16[64,1536]{1,0:T(8,128)(2,1)S(1)}, u32[]{:S(2)}, u32[]{:S(2)}) collective-permute-start(bf16[64,1536]{1,0:T(8,128)(2,1)} %collective-permute-done.4.refs_4_), channel_id=1, source_target_pairs={{0,1},{1,0},{2,3},{3,2},{4,5},{5,4},{6,7},{7,6},{8,9},{9,8},{10,11... | collective-permute-start | bytes 589832 | tf_op jit(solution)/shard_map/ppermute | solution.py:63
  50.5 24.9 %collective-permute-start.16 = (bf16[384,384]{1,0:T(8,128)(2,1)S(1)}, bf16[384,384]{1,0:T(8,128)(2,1)S(1)}, u32[]{:S(2)}, u32[]{:S(2)}) collective-permute-start(bf16[384,384]{1,0:T(8,128)(2,1)S(1)} %gate_part.1.refs_1_), channel_id=1, source_target_pairs={{0,16},{16,0},{1,17},{17,1},{2,18},{18,2},{3,19},{19,3},{4,20},{20... | collective-permute-start | bytes 884744 | tf_op jit(solution)/shard_map/ppermute | solution.py:599
  54.7 1.7 %collective-permute-start.9 = (bf16[80,1536]{1,0:T(8,128)(2,1)S(1)}, bf16[80,1536]{1,0:T(8,128)(2,1)S(1)}, u32[]{:S(2)}, u32[]{:S(2)}) collective-permute-start(bf16[80,1536]{1,0:T(8,128)(2,1)S(1)} %collective-permute-done.5.refs_5_), channel_id=1, source_target_pairs={{0,1},{1,0},{2,3},{3,2},{4,5},{5,4},{6,7},{7,6},{8,9},{9,8},{10,11... | collective-permute-start | bytes 737288 | tf_op jit(solution)/shard_map/ppermute | solution.py:63
  57.9 3.3 %copy-start.6 = (f32[1536,96]{0,1:T(8,128)S(1)}, f32[1536,96]{0,1:T(8,128)}, u32[]{:S(2)}) copy-start(f32[1536,96]{0,1:T(8,128)} %param.31) | copy-start | bytes 1769476
  60.6 15.4 %collective-permute-start.15 = (bf16[2,528,128]{2,1,0:T(8,128)(2,1)S(1)}, bf16[2,528,128]{2,1,0:T(8,128)(2,1)S(1)}, u32[]{:S(2)}, u32[]{:S(2)}) collective-permute-start(bf16[2,528,128]{2,1,0:T(8,128)(2,1)S(1)} %get-tuple-element.48.refs_2_), channel_id=1, source_target_pairs={{0,1},{1,0},{2,3},{3,2},{4,5},{5,4},{6,7},{7,6},{8,9},{9,8},{10,11... | collective-permute-start | bytes 811016 | tf_op jit(solution)/shard_map/ppermute | solution.py:63
  61.7 8.0 %collective-permute-start.19 = (bf16[96,384]{1,0:T(8,128)(2,1)S(1)}, bf16[96,384]{1,0:T(8,128)(2,1)S(1)}, u32[]{:S(2)}, u32[]{:S(2)}) collective-permute-start(bf16[96,384]{1,0:T(8,128)(2,1)S(1)} %get-tuple-element.61), channel_id=1, source_target_pairs={{0,2},{2,0},{1,3},{3,1},{4,6},{6,4},{5,7},{7,5},{8,10},{10,8},{9,1... | collective-permute-start | bytes 221192 | tf_op jit(solution)/shard_map/ppermute | solution.py:63
  65.2 5.7 %collective-permute-start.20 = (bf16[96,384]{1,0:T(8,128)(2,1)S(1)}, bf16[96,384]{1,0:T(8,128)(2,1)S(1)}, u32[]{:S(2)}, u32[]{:S(2)}) collective-permute-start(bf16[96,384]{1,0:T(8,128)(2,1)S(1)} %get-tuple-element.62), channel_id=1, source_target_pairs={{0,8},{8,0},{1,9},{9,1},{2,10},{10,2},{3,11},{11,3},{4,12},{12,4},... | collective-permute-start | bytes 221192 | tf_op jit(solution)/shard_map/ppermute | solution.py:63
  68.3 6.3 %collective-permute-start.21 = (bf16[96,384]{1,0:T(8,128)(2,1)S(1)}, bf16[96,384]{1,0:T(8,128)(2,1)S(1)}, u32[]{:S(2)}, u32[]{:S(2)}) collective-permute-start(bf16[96,384]{1,0:T(8,128)(2,1)S(1)} %get-tuple-element.63), channel_id=1, source_target_pairs={{0,10},{2,8},{8,2},{10,0},{1,11},{3,9},{9,3},{11,1},{4,14},{6,12},... | collective-permute-start | bytes 221192 | tf_op jit(solution)/shard_map/ppermute | solution.py:743
  69.8 21.8 %collective-permute-start.23 = (bf16[384,384]{1,0:T(8,128)(2,1)S(1)}, bf16[384,384]{1,0:T(8,128)(2,1)S(1)}, u32[]{:S(2)}, u32[]{:S(2)}) collective-permute-start(bf16[384,384]{1,0:T(8,128)(2,1)S(1)} %gate_part.1.refs_1_), channel_id=1, source_target_pairs={{0,4},{4,0},{1,5},{5,1},{2,6},{6,2},{3,7},{7,3},{8,12},{12,8},{9,1... | collective-permute-start | bytes 884744 | tf_op jit(solution)/shard_map/ppermute | solution.py:63
  74.7 14.8 %collective-permute-start.22 = (bf16[384,384]{1,0:T(8,128)(2,1)S(1)}, bf16[384,384]{1,0:T(8,128)(2,1)S(1)}, u32[]{:S(2)}, u32[]{:S(2)}) collective-permute-start(bf16[384,384]{1,0:T(8,128)(2,1)S(1)} %out_part.1.refs_1_), channel_id=1, source_target_pairs={{0,16},{16,0},{1,17},{17,1},{2,18},{18,2},{3,19},{19,3},{4,20},{20... | collective-permute-start | bytes 884744 | tf_op jit(solution)/shard_map/ppermute | solution.py:599
  75.4 16.2 %collective-permute-start.24 = (bf16[384,384]{1,0:T(8,128)(2,1)S(1)}, bf16[384,384]{1,0:T(8,128)(2,1)S(1)}, u32[]{:S(2)}, u32[]{:S(2)}) collective-permute-start(bf16[384,384]{1,0:T(8,128)(2,1)S(1)} %collective-permute-done.16.refs_7_.refs_3_), channel_id=1, source_target_pairs={{0,4},{4,0},{1,5},{5,1},{2,6},{6,2},{3,7},{7,3},{8,12},{12,8},{9,1... | collective-permute-start | bytes 884744 | tf_op jit(solution)/shard_map/ppermute | solution.py:63
  84.9 8.0 %collective-permute-start.17 = (bf16[2,400,128]{2,1,0:T(8,128)(2,1)S(1)}, bf16[2,400,128]{2,1,0:T(8,128)(2,1)S(1)}, u32[]{:S(2)}, u32[]{:S(2)}) collective-permute-start(bf16[2,400,128]{2,1,0:T(8,128)(2,1)S(1)} %get-tuple-element.51.refs_1_.refs_5_), channel_id=1, source_target_pairs={{0,4},{4,0},{1,5},{5,1},{2,6},{6,2},{3,7},{7,3},{8,12},{12,8},{9,1... | collective-permute-start | bytes 614408 | tf_op jit(solution)/shard_map/ppermute | solution.py:63
  85.5 24.5 %collective-permute-start.26 = (bf16[384,384]{1,0:T(8,128)(2,1)S(1)}, bf16[384,384]{1,0:T(8,128)(2,1)S(1)}, u32[]{:S(2)}, u32[]{:S(2)}) collective-permute-start(bf16[384,384]{1,0:T(8,128)(2,1)S(1)} %out_part.1.refs_1_), channel_id=1, source_target_pairs={{0,4},{4,0},{1,5},{5,1},{2,6},{6,2},{3,7},{7,3},{8,12},{12,8},{9,1... | collective-permute-start | bytes 884744 | tf_op jit(solution)/shard_map/ppermute | solution.py:63
  89.4 20.5 %collective-permute-start.27 = (bf16[384,384]{1,0:T(8,128)(2,1)S(1)}, bf16[384,384]{1,0:T(8,128)(2,1)S(1)}, u32[]{:S(2)}, u32[]{:S(2)}) collective-permute-start(bf16[384,384]{1,0:T(8,128)(2,1)S(1)} %collective-permute-done.22.refs_9_.refs_3_), channel_id=1, source_target_pairs={{0,4},{4,0},{1,5},{5,1},{2,6},{6,2},{3,7},{7,3},{8,12},{12,8},{9,1... | collective-permute-start | bytes 884744 | tf_op jit(solution)/shard_map/ppermute | solution.py:63
  93.6 10.0 %collective-permute-start.18 = (bf16[400,128]{1,0:T(8,128)(2,1)S(1)}, bf16[400,128]{1,0:T(8,128)(2,1)S(1)}, u32[]{:S(2)}, u32[]{:S(2)}) collective-permute-start(bf16[400,128]{1,0:T(8,128)(2,1)S(1)} %compose.1.refs_8_), channel_id=1, source_target_pairs={{0,16},{1,17},{2,18},{3,19},{4,20},{5,21},{6,22},{7,23},{8,24},{9,... | collective-permute-start | bytes 307208 | tf_op jit(solution)/shard_map/ppermute | solution.py:834
  104.6 7.5 %collective-permute-start.25 = (bf16[2,384,128]{2,1,0:T(8,128)(2,1)S(1)}, bf16[2,384,128]{2,1,0:T(8,128)(2,1)S(1)}, u32[]{:S(2)}, u32[]{:S(2)}) collective-permute-start(bf16[2,384,128]{2,1,0:T(8,128)(2,1)S(1)} %get-tuple-element.64), channel_id=1, source_target_pairs={{0,2},{2,0},{1,3},{3,1},{4,6},{6,4},{5,7},{7,5},{8,10},{10,8},{9,1... | collective-permute-start | bytes 589832 | tf_op jit(solution)/shard_map/ppermute | solution.py:63
  104.7 10.9 %collective-permute-start.28 = (bf16[2,384,128]{2,1,0:T(8,128)(2,1)S(1)}, bf16[2,384,128]{2,1,0:T(8,128)(2,1)S(1)}, u32[]{:S(2)}, u32[]{:S(2)}) collective-permute-start(bf16[2,384,128]{2,1,0:T(8,128)(2,1)S(1)} %get-tuple-element.67), channel_id=1, source_target_pairs={{0,8},{8,0},{1,9},{9,1},{2,10},{10,2},{3,11},{11,3},{4,12},{12,4},... | collective-permute-start | bytes 589832 | tf_op jit(solution)/shard_map/ppermute | solution.py:63
  104.9 10.7 %collective-permute-start.29 = (bf16[2,384,128]{2,1,0:T(8,128)(2,1)S(1)}, bf16[2,384,128]{2,1,0:T(8,128)(2,1)S(1)}, u32[]{:S(2)}, u32[]{:S(2)}) collective-permute-start(bf16[2,384,128]{2,1,0:T(8,128)(2,1)S(1)} %get-tuple-element.68), channel_id=1, source_target_pairs={{0,10},{2,8},{8,2},{10,0},{1,11},{3,9},{9,3},{11,1},{4,14},{6,12},... | collective-permute-start | bytes 589832 | tf_op jit(solution)/shard_map/ppermute | solution.py:859
  117.8 3.8 %collective-permute-start.30 = (bf16[4,144,1536]{2,1,0:T(8,128)(2,1)S(1)}, bf16[4,144,1536]{2,1,0:T(8,128)(2,1)S(1)}, u32[]{:S(2)}, u32[]{:S(2)}) collective-permute-start(bf16[4,144,1536]{2,1,0:T(8,128)(2,1)S(1)} %mix_send.1.refs_4_), channel_id=1, source_target_pairs={{0,1},{1,0},{2,3},{3,2},{4,5},{5,4},{6,7},{7,6},{8,9},{9,8},{10,11... | collective-permute-start | bytes 5308424 | tf_op jit(solution)/shard_map/ppermute | solution.py:63
  121.9 12.3 %collective-permute-start.31 = (bf16[2,144,768]{2,1,0:T(8,128)(2,1)S(1)}, bf16[2,144,768]{2,1,0:T(8,128)(2,1)S(1)}, u32[]{:S(2)}, u32[]{:S(2)}) collective-permute-start(bf16[2,144,768]{2,1,0:T(8,128)(2,1)S(1)} %get-tuple-element.70.refs_5_), channel_id=1, source_target_pairs={{0,2},{2,0},{1,3},{3,1},{4,6},{6,4},{5,7},{7,5},{8,10},{10,8},{9,1... | collective-permute-start | bytes 1327112 | tf_op jit(solution)/shard_map/ppermute | solution.py:63
  122.4 10.9 %collective-permute-start.32 = (bf16[2,128,768]{2,1,0:T(8,128)(2,1)S(1)}, bf16[2,128,768]{2,1,0:T(8,128)(2,1)S(1)}, u32[]{:S(2)}, u32[]{:S(2)}) collective-permute-start(bf16[2,128,768]{2,1,0:T(8,128)(2,1)S(1)} %get-tuple-element.72), channel_id=1, source_target_pairs={{0,8},{8,0},{1,9},{9,1},{2,10},{10,2},{3,11},{11,3},{4,12},{12,4},... | collective-permute-start | bytes 1179656 | tf_op jit(solution)/shard_map/ppermute | solution.py:63
  134.4 6.7 %collective-permute-start.33 = (bf16[144,768]{1,0:T(8,128)(2,1)S(1)}, bf16[144,768]{1,0:T(8,128)(2,1)S(1)}, u32[]{:S(2)}, u32[]{:S(2)}) collective-permute-start(bf16[144,768]{1,0:T(8,128)(2,1)S(1)} %get-tuple-element.74), channel_id=1, source_target_pairs={{0,8},{8,0},{1,9},{9,1},{2,10},{10,2},{3,11},{11,3},{4,12},{12,4},... | collective-permute-start | bytes 663560 | tf_op jit(solution)/shard_map/ppermute | solution.py:63
  134.6 6.0 %collective-permute-start.34 = (bf16[128,768]{1,0:T(8,128)(2,1)S(1)}, bf16[128,768]{1,0:T(8,128)(2,1)S(1)}, u32[]{:S(2)}, u32[]{:S(2)}) collective-permute-start(bf16[128,768]{1,0:T(8,128)(2,1)S(1)} %get-tuple-element.76), channel_id=1, source_target_pairs={{0,2},{2,0},{1,3},{3,1},{4,6},{6,4},{5,7},{7,5},{8,10},{10,8},{9,1... | collective-permute-start | bytes 589832 | tf_op jit(solution)/shard_map/ppermute | solution.py:63

commit v4 on v3

--- a/solution.py
+++ b/solution.py
@@ -661,15 +661,6 @@
     aligned = rows % TILE == 0
     size = lax.axis_size(SEQ)
     half = tokens // 2
-    mine, tail = call(
-        functools.partial(rows_kernel, sizes),
-        "own_rows",
-        (shape((half, model), BF16), shape((TILE, model), BF16)),
-        [ints, hidden_in],
-        [pltpu.SemaphoreType.DMA((2,))],
-        fetch=True,
-    )
-    mine_b, mine_a = swap(mine, "b"), swap(mine, "a")
     inner_send = call(
         functools.partial(pack_kernel, heads),
         "pack_rows",
@@ -679,11 +670,22 @@
             *[pltpu.VMEM(x.shape, F32) for x in (inner_proj, small_proj, gate_proj)],
             pltpu.SemaphoreType.DMA((3,)),
         ],
-        after=[mine],
         us=2,
+        limit=56,
         fetch=True,
     )
     inner_got = lax.all_to_all(inner_send, GROUP, 0, 0, tiled=True)
+    mine, tail = call(
+        functools.partial(rows_kernel, sizes),
+        "own_rows",
+        (shape((half, model), BF16), shape((TILE, model), BF16)),
+        [ints, hidden_in],
+        [pltpu.SemaphoreType.DMA((2,))],
+        after=[inner_send],
+        limit=56,
+        fetch=True,
+    )
+    mine_b, mine_a = swap(mine, "b"), swap(mine, "a")
 
     if aligned:
         part, low, high, gate_part = call(
@@ -691,8 +693,8 @@
             "repack_inner",
             (
                 shape((8 * rows + TILE, width + N), BF16),
-                shape((4 * rows, width + N), BF16),
-                shape(((8 - 4) * rows + TILE, width + N), BF16),
+                shape((5 * rows, width + N), BF16),
+                shape(((8 - 5) * rows + TILE, width + N), BF16),
                 shape((8 * rows, width), BF16),
             ),
             [inner_got],
@@ -700,7 +702,7 @@
         marks, inner_parts = [(0, 0, 0), (0, 1, 0)], [part, swap(part, "y")]
         for s in range(1, t_count):
             low, high = round_t(low, t_count), round_t(high, t_count)
-            marks += [(s, 0, 0), (s, 0, 4), (s, 1, 0), (s, 1, 4)]
+            marks += [(s, 0, 0), (s, 0, 5), (s, 1, 0), (s, 1, 5)]
             inner_parts += [low, high, swap(low, "y"), swap(high, "y")]
         ready = [part]
     else:

time: 142 us -> 137 us (0.965)
  starting transfers between devices: 58.5 us -> 51.9 us
  local copies, waits for them, and re-layouts: 7.26 us -> 2.46 us
  waiting for transfers between devices: 31 us -> 35.7 us
  Pallas kernels: 42.7 us -> 45.2 us
    ppermute x26, waiting for transfers between devices: 21.5 us -> 25 us  [swap(): return lax.ppermute(x, axis, [(0, 1), (1, 0)])]
    unnamed x32 -> x40, local copies, waits for them, and re-layouts: 4.38 us -> 1.77 us
    pallas_call x24, Pallas kernels: 42.7 us -> 45.2 us  [call(): pl.pallas_call(kernel, name=name, out_shape=out_shape, in_specs=specs, ou...]
    ppermute x4, waiting for transfers between devices: 2.8 us -> 4.96 us  [round_t(): return lax.ppermute(x, 't', [(i, (i + 1) % count) for i in range(count)])]
    ppermute x1, waiting for transfers between devices: 3.79 us -> 1.74 us  [on_device(): lax.ppermute(out_send[3], ('a', 'b'), across)]
    broadcast_in_dim x2, local copies, waits for them, and re-layouts: 1.89 us -> 0.01 us  [on_device(): top = jnp.concatenate([conv_inner, bias_inner[None], norm_gain[None]])]
    ppermute x1, starting transfers between devices: 3.19 us -> 1.38 us  [on_device(): lax.ppermute(pages[3], ('a', 'b'), across)]
    ppermute x4, starting transfers between devices: 6.34 us -> 4.67 us  [round_t(): return lax.ppermute(x, 't', [(i, (i + 1) % count) for i in range(count)])]
  transfers between devices with their start and end apart: 36 -> 36, of which waited for: 14 -> 12; matrix products, arithmetic and copies ran while one was open for 2% -> 1% of each run, Pallas kernels for 27% -> 29%
where the time goes in v4:
time: 137 us; the launch traced here: 136 us
  starting transfers between devices  51.9 us (38%)
  Pallas kernels  45.2 us (33%)
  waiting for transfers between devices  35.7 us (26%)
  local copies, waits for them, and re-layouts  2.46 us (2%)
    pallas_call x24, Pallas kernels, call(): pl.pallas_call(kernel, name=name, out_shape=out_shape, in_specs=specs, ou...  45.2 us
    ppermute x26, starting transfers between devices, swap(): return lax.ppermute(x, axis, [(0, 1), (1, 0)])  35.2 us
    ppermute x26, waiting for transfers between devices, swap(): return lax.ppermute(x, axis, [(0, 1), (1, 0)])  25 us
    all_to_all x1, starting transfers between devices, on_device(): inner_got = lax.all_to_all(inner_send, GROUP, 0, 0, tiled=True)  5.24 us
    ppermute x4, waiting for transfers between devices, round_t(): return lax.ppermute(x, 't', [(i, (i + 1) % count) for i in range(count)])  4.96 us
    ppermute x4, starting transfers between devices, round_t(): return lax.ppermute(x, 't', [(i, (i + 1) % count) for i in range(count)])  4.67 us
    all_to_all x1, waiting for transfers between devices, on_device(): inner_got = lax.all_to_all(inner_send, GROUP, 0, 0, tiled=True)  3.92 us
  transfers between devices with their start and end apart: 36, of which 12 were waited for; matrix products, arithmetic and copies ran while one was open for 1% of the time, Pallas kernels for 29%

profile of v4, /device:TPU:0, one launch (start us, length us, event | category | flops | bytes accessed | tf_op | source)
XLA Modules:
  0.0 136.4 jit_solution(10517268179208746656)
XLA Ops:
  0.7 2.4 %pack_rows.1.refs_2_ = bf16[8,48,1024]{2,1,0:T(8,128)(2,1)} custom-call(f32[48,3072]{1,0:T(8,128)} %refs_0_.1, f32[48,304]{1,0:T(8,128)} %refs_1_.3, f32[48,3072]{1,0:T(8,128)} %refs_2_.1), custom_call_target="tpu_custom_call" | custom-call | flops 2000000000 | bytes 6000000 | tf_op jit(solution)/shard_map/pack_rows/pallas_call | solution.py:36
  3.1 5.2 %all-to-all-start = ((bf16[8,48,1024]{2,1,0:T(8,128)(2,1)}), bf16[8,48,1024]{2,1,0:T(8,128)(2,1)}, u32[]{:S(2)}, u32[]{:S(2)}) async-start(bf16[8,48,1024]{2,1,0:T(8,128)(2,1)} %pack_rows.1.refs_2_), calls=%async_computation | async-start | bytes 1572864 | tf_op jit(solution)/shard_map/all_to_all | solution.py:677
  8.3 0.6 concatenate.15.refs_0_
  9.0 2.6 %own_rows.1 = (bf16[128,1536]{1,0:T(8,128)(2,1)}, bf16[16,1536]{1,0:T(8,128)(2,1)}) custom-call(s32[58]{0:T(128)} %concatenate.15.refs_0_, bf16[256,1536]{1,0:T(8,128)(2,1)} %refs_1_.5, bf16[8,48,1024]{2,1,0:T(8,128)(2,1)} %pack_rows.1.refs_2_), custom_call_target="tpu_custom_call" | custom-call | flops 1000000000 | bytes 3000000 | tf_op jit(solution)/shard_map/own_rows/pallas_call | solution.py:36
  11.6 2.1 %collective-permute-start = (bf16[128,1536]{1,0:T(8,128)(2,1)}, bf16[128,1536]{1,0:T(8,128)(2,1)}, u32[]{:S(2)}, u32[]{:S(2)}) collective-permute-start(bf16[128,1536]{1,0:T(8,128)(2,1)} %get-tuple-element.40), channel_id=1, source_target_pairs={{0,2},{2,0},{1,3},{3,1},{4,6},{6,4},{5,7},{7,5},{8,10},{10,8},{9,1... | collective-permute-start | bytes 1179656 | tf_op jit(solution)/shard_map/ppermute | solution.py:63
  13.6 1.5 %collective-permute-start.1 = (bf16[128,1536]{1,0:T(8,128)(2,1)}, bf16[128,1536]{1,0:T(8,128)(2,1)}, u32[]{:S(2)}, u32[]{:S(2)}) collective-permute-start(bf16[128,1536]{1,0:T(8,128)(2,1)} %get-tuple-element.40), channel_id=1, source_target_pairs={{0,8},{8,0},{1,9},{9,1},{2,10},{10,2},{3,11},{11,3},{4,12},{12,4},... | collective-permute-start | bytes 1179656 | tf_op jit(solution)/shard_map/ppermute | solution.py:63
  15.1 0.7 collective-permute-start.2
  15.8 0.7 collective-permute-start.3
  16.6 3.9 %all-to-all-done.refs_0_ = bf16[8,48,1024]{2,1,0:T(8,128)(2,1)} async-done(((bf16[8,48,1024]{2,1,0:T(8,128)(2,1)}), bf16[8,48,1024]{2,1,0:T(8,128)(2,1)}, u32[]{:S(2)}, u32[]{:S(2)}) %all-to-all-start) | async-done | bytes 786464 | tf_op jit(solution)/shard_map/all_to_all | solution.py:677
  20.5 2.0 %repack_inner.1 = (bf16[400,512]{1,0:T(8,128)(2,1)}, bf16[240,512]{1,0:T(8,128)(2,1)S(1)}, bf16[160,512]{1,0:T(8,128)(2,1)S(1)}, bf16[384,384]{1,0:T(8,128)(2,1)S(1)}) custom-call(bf16[8,48,1024]{2,1,0:T(8,128)(2,1)} %all-to-all-done.refs_0_), custom_call_target="tpu_custom_call" | custom-call | flops 1000000000 | bytes 3000000 | tf_op jit(solution)/shard_map/repack_inner/pallas_call | solution.py:36
  22.5 0.7 copy-done.6
  23.3 2.9 %collective-permute-start.11 = (bf16[240,512]{1,0:T(8,128)(2,1)S(1)}, bf16[240,512]{1,0:T(8,128)(2,1)S(1)}, u32[]{:S(2)}, u32[]{:S(2)}) collective-permute-start(bf16[240,512]{1,0:T(8,128)(2,1)S(1)} %get-tuple-element.45), channel_id=1, source_target_pairs={{0,16},{16,0},{1,17},{17,1},{2,18},{18,2},{3,19},{19,3},{4,20},{20... | collective-permute-start | bytes 737288 | tf_op jit(solution)/shard_map/ppermute | solution.py:599
  26.3 7.7 %collective-permute-start.10 = (bf16[400,512]{1,0:T(8,128)(2,1)}, bf16[400,512]{1,0:T(8,128)(2,1)}, u32[]{:S(2)}, u32[]{:S(2)}) collective-permute-start(bf16[400,512]{1,0:T(8,128)(2,1)} %get-tuple-element.42.refs_5_.refs_1_), channel_id=1, source_target_pairs={{0,4},{4,0},{1,5},{5,1},{2,6},{6,2},{3,7},{7,3},{8,12},{12,8},{9,1... | collective-permute-start | bytes 1228808 | tf_op jit(solution)/shard_map/ppermute | solution.py:63
  33.9 1.9 %forward_rows.1 = (bf16[64,1536]{1,0:T(8,128)(2,1)}, bf16[80,1536]{1,0:T(8,128)(2,1)}) custom-call(s32[58]{0:T(128)S(1)} %copy-done.1, bf16[128,1536]{1,0:T(8,128)(2,1)} %collective-permute-done.refs_1_.refs_2_, bf16[128,1536]{1,0:T(8,128)(2,1)} %collective-permute-done.1.refs_2_.refs_3_, bf16[16,1536]{1,0:T(8,128)(2,1)S(1)} %collective-permute-done.2.refs_3_.refs_10_, ...), custom_call_target="tpu_custom_call" | custom-call | flops 1000000000 | bytes 3000000 | tf_op jit(solution)/shard_map/forward_rows/pallas_call | solution.py:36
  35.9 4.4 %collective-permute-start.4 = (bf16[64,1536]{1,0:T(8,128)(2,1)}, bf16[64,1536]{1,0:T(8,128)(2,1)}, u32[]{:S(2)}, u32[]{:S(2)}) collective-permute-start(bf16[64,1536]{1,0:T(8,128)(2,1)} %get-tuple-element.43), channel_id=1, source_target_pairs={{0,2},{2,0},{1,3},{3,1},{4,6},{6,4},{5,7},{7,5},{8,10},{10,8},{9,1... | collective-permute-start | bytes 589832 | tf_op jit(solution)/shard_map/ppermute | solution.py:63
  40.2 1.3 collective-permute-start.5
  41.6 2.4 %collective-permute-done.12.refs_4_.refs_1_ = bf16[160,512]{1,0:T(8,128)(2,1)} collective-permute-done((bf16[160,512]{1,0:T(8,128)(2,1)S(1)}, bf16[160,512]{1,0:T(8,128)(2,1)}, u32[]{:S(2)}, u32[]{:S(2)}) %collective-permute-start.12) | collective-permute-done | bytes 163872 | tf_op jit(solution)/shard_map/ppermute | solution.py:599
  44.0 1.6 %collective-permute-start.14 = (bf16[160,512]{1,0:T(8,128)(2,1)}, bf16[160,512]{1,0:T(8,128)(2,1)}, u32[]{:S(2)}, u32[]{:S(2)}) collective-permute-start(bf16[160,512]{1,0:T(8,128)(2,1)} %collective-permute-done.12.refs_4_.refs_1_), channel_id=1, source_target_pairs={{0,4},{4,0},{1,5},{5,1},{2,6},{6,2},{3,7},{7,3},{8,12},{12,8},{9,1... | collective-permute-start | bytes 491528 | tf_op jit(solution)/shard_map/ppermute | solution.py:63
  45.6 0.5 collective-permute-start.13
  46.0 1.0 copy-done.7
  47.1 1.1 collective-permute-done.5.refs_5_
  48.2 3.2 %collective-permute-done.14.refs_6_ = bf16[160,512]{1,0:T(8,128)(2,1)} collective-permute-done((bf16[160,512]{1,0:T(8,128)(2,1)}, bf16[160,512]{1,0:T(8,128)(2,1)}, u32[]{:S(2)}, u32[]{:S(2)}) %collective-permute-start.14) | collective-permute-done | bytes 163872 | tf_op jit(solution)/shard_map/ppermute | solution.py:63
  51.5 3.4 %collective-permute-done.13.refs_5_ = bf16[240,512]{1,0:T(8,128)(2,1)} collective-permute-done((bf16[240,512]{1,0:T(8,128)(2,1)S(1)}, bf16[240,512]{1,0:T(8,128)(2,1)}, u32[]{:S(2)}, u32[]{:S(2)}) %collective-permute-start.13) | collective-permute-done | bytes 245792 | tf_op jit(solution)/shard_map/ppermute | solution.py:63
  54.9 1.6 %inner_weights.1.refs_1_ = bf16[1536,640]{1,0:T(8,128)(2,1)S(1)} custom-call(s32[58]{0:T(128)S(1)} %copy-done.1, bf16[400,512]{1,0:T(8,128)(2,1)} %get-tuple-element.42.refs_5_.refs_1_, bf16[400,512]{1,0:T(8,128)(2,1)} %collective-permute-done.10.refs_2_, bf16[240,512]{1,0:T(8,128)(2,1)S(1)} %collective-permute-done.11.refs_3_, ...), custom_call_target="tpu_custom_call" | custom-call | flops 15000000512 | bytes 45000000 | tf_op jit(solution)/shard_map/inner_weights/pallas_call | solution.py:36
  56.6 1.5 %assemble_rows.1.refs_0_ = bf16[2,528,1536]{2,1,0:T(8,128)(2,1)S(1)} custom-call(s32[58]{0:T(128)S(1)} %copy-done.1, bf16[256,1536]{1,0:T(8,128)(2,1)S(1)} %copy-done.2, bf16[128,1536]{1,0:T(8,128)(2,1)} %collective-permute-done.refs_1_.refs_2_, bf16[128,1536]{1,0:T(8,128)(2,1)} %collective-permute-done.1.refs_2_.refs_3_, ...), custom_call_target="tpu_custom_call" | custom-call | flops 2000000000 | bytes 6000000 | tf_op jit(solution)/shard_map/assemble_rows/pallas_call | solution.py:36
  58.1 2.7 %inner_projection.1 = (bf16[2,528,384]{2,1,0:T(8,128)(2,1)S(1)}, bf16[2,528,128]{2,1,0:T(8,128)(2,1)S(1)}, f32[2,528,128]{2,1,0:T(8,128)S(1)}) custom-call(bf16[2,528,1536]{2,1,0:T(8,128)(2,1)S(1)} %assemble_rows.1.refs_0_, bf16[1536,640]{1,0:T(8,128)(2,1)S(1)} %inner_weights.1.refs_1_), custom_call_target="tpu_custom_call" | custom-call | flops 3500000000 | bytes 10500000 | tf_op jit(solution)/shard_map/inner_projection/pallas_call | solution.py:36
  60.8 0.5 collective-permute-start.15
  61.3 0.6 pack_out.1
  61.9 1.6 %collective-permute-start.19 = (bf16[96,384]{1,0:T(8,128)(2,1)S(1)}, bf16[96,384]{1,0:T(8,128)(2,1)S(1)}, u32[]{:S(2)}, u32[]{:S(2)}) collective-permute-start(bf16[96,384]{1,0:T(8,128)(2,1)S(1)} %get-tuple-element.61), channel_id=1, source_target_pairs={{0,2},{2,0},{1,3},{3,1},{4,6},{6,4},{5,7},{7,5},{8,10},{10,8},{9,1... | collective-permute-start | bytes 221192 | tf_op jit(solution)/shard_map/ppermute | solution.py:63
  63.4 2.6 %collective-permute-start.20 = (bf16[96,384]{1,0:T(8,128)(2,1)S(1)}, bf16[96,384]{1,0:T(8,128)(2,1)S(1)}, u32[]{:S(2)}, u32[]{:S(2)}) collective-permute-start(bf16[96,384]{1,0:T(8,128)(2,1)S(1)} %get-tuple-element.62), channel_id=1, source_target_pairs={{0,8},{8,0},{1,9},{9,1},{2,10},{10,2},{3,11},{11,3},{4,12},{12,4},... | collective-permute-start | bytes 221192 | tf_op jit(solution)/shard_map/ppermute | solution.py:63
  66.0 1.4 %collective-permute-start.21 = (bf16[96,384]{1,0:T(8,128)(2,1)S(1)}, bf16[96,384]{1,0:T(8,128)(2,1)S(1)}, u32[]{:S(2)}, u32[]{:S(2)}) collective-permute-start(bf16[96,384]{1,0:T(8,128)(2,1)S(1)} %get-tuple-element.63), channel_id=1, source_target_pairs={{0,10},{2,8},{8,2},{10,0},{1,11},{3,9},{9,3},{11,1},{4,14},{6,12},... | collective-permute-start | bytes 221192 | tf_op jit(solution)/shard_map/ppermute | solution.py:745
  67.5 0.4 collective-permute-start.23
  67.8 1.7 %collective-permute-start.24 = (bf16[384,384]{1,0:T(8,128)(2,1)S(1)}, bf16[384,384]{1,0:T(8,128)(2,1)S(1)}, u32[]{:S(2)}, u32[]{:S(2)}) collective-permute-start(bf16[384,384]{1,0:T(8,128)(2,1)S(1)} %collective-permute-done.16.refs_7_.refs_3_), channel_id=1, source_target_pairs={{0,4},{4,0},{1,5},{5,1},{2,6},{6,2},{3,7},{7,3},{8,12},{12,8},{9,1... | collective-permute-start | bytes 884744 | tf_op jit(solution)/shard_map/ppermute | solution.py:63
  69.6 1.7 %collective-permute-done.21.refs_3_ = bf16[96,384]{1,0:T(8,128)(2,1)S(1)} collective-permute-done((bf16[96,384]{1,0:T(8,128)(2,1)S(1)}, bf16[96,384]{1,0:T(8,128)(2,1)S(1)}, u32[]{:S(2)}, u32[]{:S(2)}) %collective-permute-start.21) | collective-permute-done | bytes 73760 | tf_op jit(solution)/shard_map/ppermute | solution.py:745
  71.4 1.7 %collective-permute-start.22 = (bf16[384,384]{1,0:T(8,128)(2,1)S(1)}, bf16[384,384]{1,0:T(8,128)(2,1)S(1)}, u32[]{:S(2)}, u32[]{:S(2)}) collective-permute-start(bf16[384,384]{1,0:T(8,128)(2,1)S(1)} %out_part.1.refs_1_), channel_id=1, source_target_pairs={{0,16},{16,0},{1,17},{17,1},{2,18},{18,2},{3,19},{19,3},{4,20},{20... | collective-permute-start | bytes 884744 | tf_op jit(solution)/shard_map/ppermute | solution.py:599
  73.1 8.5 %states.1 = (bf16[8,128,384]{2,1,0:T(8,128)(2,1)S(1)}, bf16[8,128,128]{2,1,0:T(8,128)(2,1)S(1)}, bf16[8,128,128]{2,1,0:T(8,128)(2,1)S(1)}, f32[8,128,128]{2,1,0:...) custom-call(s32[58]{0:T(128)S(1)} %copy-done.1, ...), custom_call_target="tpu_custom_call" | custom-call | flops 7000000000 | bytes 21000000 | tf_op jit(solution)/shard_map/states/pallas_call | solution.py:36
  81.6 0.3 collective-permute-start.17
  81.9 1.8 %collective-permute-start.26 = (bf16[384,384]{1,0:T(8,128)(2,1)S(1)}, bf16[384,384]{1,0:T(8,128)(2,1)S(1)}, u32[]{:S(2)}, u32[]{:S(2)}) collective-permute-start(bf16[384,384]{1,0:T(8,128)(2,1)S(1)} %out_part.1.refs_1_), channel_id=1, source_target_pairs={{0,4},{4,0},{1,5},{5,1},{2,6},{6,2},{3,7},{7,3},{8,12},{12,8},{9,1... | collective-permute-start | bytes 884744 | tf_op jit(solution)/shard_map/ppermute | solution.py:63
  83.7 0.7 gate_weights.1.refs_1_
  84.4 2.5 %collective-permute-done.22.refs_9_.refs_3_ = bf16[384,384]{1,0:T(8,128)(2,1)S(1)} collective-permute-done((bf16[384,384]{1,0:T(8,128)(2,1)S(1)}, bf16[384,384]{1,0:T(8,128)(2,1)S(1)}, u32[]{:S(2)}, u32[]{:S(2)}) %collective-permute-start.22) | collective-permute-done | bytes 294944 | tf_op jit(solution)/shard_map/ppermute | solution.py:599
  86.9 0.3 collective-permute-start.27
  87.2 2.5 %collective-permute-done.17.refs_2_ = bf16[2,400,128]{2,1,0:T(8,128)(2,1)S(1)} collective-permute-done((bf16[2,400,128]{2,1,0:T(8,128)(2,1)S(1)}, bf16[2,400,128]{2,1,0:T(8,128)(2,1)S(1)}, u32[]{:S(2)}, u32[]{:S(2)}) %collective-permute-start.17) | collective-permute-done | bytes 204832 | tf_op jit(solution)/shard_map/ppermute | solution.py:63
  89.7 0.6 compose.1.refs_8_
  90.3 2.6 %collective-permute-start.18 = (bf16[400,128]{1,0:T(8,128)(2,1)S(1)}, bf16[400,128]{1,0:T(8,128)(2,1)S(1)}, u32[]{:S(2)}, u32[]{:S(2)}) collective-permute-start(bf16[400,128]{1,0:T(8,128)(2,1)S(1)} %compose.1.refs_8_), channel_id=1, source_target_pairs={{0,16},{1,17},{2,18},{3,19},{4,20},{5,21},{6,22},{7,23},{8,24},{9,... | collective-permute-start | bytes 307208 | tf_op jit(solution)/shard_map/ppermute | solution.py:836
  93.0 5.5 %within_chunks.1.refs_4_ = f32[8,128,384]{2,1,0:T(8,128)S(1)} custom-call(s32[58]{0:T(128)S(1)} %copy-done.1, bf16[8,128,384]{2,1,0:T(8,128)(2,1)S(1)} %get-tuple-element.57.refs_1_, bf16[8,128,128]{2,1,0:T(8,128)(2,1)S(1)} %get-tuple-element.58.refs_2_, bf16[8,128,128]{2,1,0:T(8,128)(2,1)S(1)} %get-tuple-element.55.refs_3_.refs_2_, ...), custom_call_target="tpu_custom_call" | custom-call | flops 5000000000 | bytes 15000000 | tf_op jit(solution)/shard_map/within_chunks/pallas_call | solution.py:36
  98.5 0.9 entering_states.1
  99.4 2.0 %collective-permute-start.25 = (bf16[2,384,128]{2,1,0:T(8,128)(2,1)S(1)}, bf16[2,384,128]{2,1,0:T(8,128)(2,1)S(1)}, u32[]{:S(2)}, u32[]{:S(2)}) collective-permute-start(bf16[2,384,128]{2,1,0:T(8,128)(2,1)S(1)} %get-tuple-element.64), channel_id=1, source_target_pairs={{0,2},{2,0},{1,3},{3,1},{4,6},{6,4},{5,7},{7,5},{8,10},{10,8},{9,1... | collective-permute-start | bytes 589832 | tf_op jit(solution)/shard_map/ppermute | solution.py:63
  101.3 0.2 collective-permute-start.28
  101.5 1.4 %collective-permute-start.29 = (bf16[2,384,128]{2,1,0:T(8,128)(2,1)S(1)}, bf16[2,384,128]{2,1,0:T(8,128)(2,1)S(1)}, u32[]{:S(2)}, u32[]{:S(2)}) collective-permute-start(bf16[2,384,128]{2,1,0:T(8,128)(2,1)S(1)} %get-tuple-element.68), channel_id=1, source_target_pairs={{0,10},{2,8},{8,2},{10,0},{1,11},{3,9},{9,3},{11,1},{4,14},{6,12},... | collective-permute-start | bytes 589832 | tf_op jit(solution)/shard_map/ppermute | solution.py:861
  102.9 1.8 %gate_projection.1.refs_5_ = bf16[2,528,384]{2,1,0:T(8,128)(2,1)S(1)} custom-call(bf16[2,528,1536]{2,1,0:T(8,128)(2,1)S(1)} %assemble_rows.1.refs_0_, bf16[1536,384]{1,0:T(8,128)(2,1)S(1)} %gate_weights.1.refs_1_, bf16[8,384,128]{2,1,0:T(8,128)(2,1)S(1)} %get-tuple-element.54.refs_2_.refs_1_), custom_call_target="tpu_custom_call" | custom-call | flops 2500000000 | bytes 7500000 | tf_op jit(solution)/shard_map/gate_projection/pallas_call | solution.py:36
  104.8 0.9 columns.1.refs_3_
  105.7 3.6 %finish.1 = (bf16[8,128,384]{2,1,0:T(8,128)(2,1)S(1)}, f32[8,8,128]{2,1,0:T(8,128)S(1)}) custom-call(s32[58]{0:T(128)S(1)} %copy-done.1, bf16[8,384,128]{2,1,0:T(8,128)(2,1)S(1)} %get-tuple-element.54.refs_2_.refs_1_, bf16[8,128,128]{2,1,0:T(8,128)(2,1)S(1)} %get-tuple-element.55.refs_3_.refs_2_, f32[8,128,128]{2,1,0:T(8,128)S(1)} %get-tuple-element.56.refs_4_.refs_3_, ...), custom_call_target="tpu_custom_call" | custom-call | flops 4000000000 | bytes 12000000 | tf_op jit(solution)/shard_map/finish/pallas_call | solution.py:36
  109.3 2.1 %mix_send.1.refs_4_ = bf16[4,144,1536]{2,1,0:T(8,128)(2,1)S(1)} custom-call(s32[58]{0:T(128)S(1)} %copy-done.1, bf16[8,128,384]{2,1,0:T(8,128)(2,1)S(1)} %get-tuple-element.65.refs_1_, f32[8,8,128]{2,1,0:T(8,128)S(1)} %get-tuple-element.66.refs_2_, bf16[1536,384]{1,0:T(8,128)(2,1)S(1)} %columns.1.refs_3_, ...), custom_call_target="tpu_custom_call" | custom-call | flops 2100000000 | bytes 6300000 | tf_op jit(solution)/shard_map/mix_send/pallas_call | solution.py:36
  111.5 2.1 %mix_keep.1.refs_0_ = bf16[4,144,1536]{2,1,0:T(8,128)(2,1)S(1)} custom-call(s32[58]{0:T(128)S(1)} %copy-done.1, bf16[8,128,384]{2,1,0:T(8,128)(2,1)S(1)} %get-tuple-element.65.refs_1_, f32[8,8,128]{2,1,0:T(8,128)S(1)} %get-tuple-element.66.refs_2_, bf16[1536,384]{1,0:T(8,128)(2,1)S(1)} %columns.1.refs_3_, bf16[4,144,1536]{2,1,0:T(8,128)(2,1)S(1)} %mix_send.1.refs_4_), custom_call_target="tpu_custom_call" | custom-call | flops 2100000000 | bytes 6300000 | tf_op jit(solution)/shard_map/mix_keep/pallas_call | solution.py:36
  113.7 1.5 %collective-permute-done.30.refs_1_ = bf16[4,144,1536]{2,1,0:T(8,128)(2,1)S(1)} collective-permute-done((bf16[4,144,1536]{2,1,0:T(8,128)(2,1)S(1)}, bf16[4,144,1536]{2,1,0:T(8,128)(2,1)S(1)}, u32[]{:S(2)}, u32[]{:S(2)}) %collective-permute-start.30) | collective-permute-done | bytes 1769504 | tf_op jit(solution)/shard_map/ppermute | solution.py:63
  115.2 0.4 add_cores.1
  115.6 2.0 %collective-permute-start.31 = (bf16[2,144,768]{2,1,0:T(8,128)(2,1)S(1)}, bf16[2,144,768]{2,1,0:T(8,128)(2,1)S(1)}, u32[]{:S(2)}, u32[]{:S(2)}) collective-permute-start(bf16[2,144,768]{2,1,0:T(8,128)(2,1)S(1)} %get-tuple-element.70.refs_5_), channel_id=1, source_target_pairs={{0,2},{2,0},{1,3},{3,1},{4,6},{6,4},{5,7},{7,5},{8,10},{10,8},{9,1... | collective-permute-start | bytes 1327112 | tf_op jit(solution)/shard_map/ppermute | solution.py:63
  117.5 0.7 collective-permute-start.32
  118.3 10.1 %collective-permute-done.32.refs_3_ = bf16[2,128,768]{2,1,0:T(8,128)(2,1)S(1)} collective-permute-done((bf16[2,128,768]{2,1,0:T(8,128)(2,1)S(1)}, bf16[2,128,768]{2,1,0:T(8,128)(2,1)S(1)}, u32[]{:S(2)}, u32[]{:S(2)}) %collective-permute-start.32) | collective-permute-done | bytes 393248 | tf_op jit(solution)/shard_map/ppermute | solution.py:63
  128.6 1.1 collective-permute-start.33
  129.7 1.0 collective-permute-start.34
  130.7 1.8 %pages.1 = f32[2,4,384,128]{3,2,1,0:T(8,128)} custom-call(s32[58]{0:T(128)S(1)} %copy-done.1, bf16[2,384,128]{2,1,0:T(8,128)(2,1)S(1)} %get-tuple-element.77.refs_1_, bf16[2,384,128]{2,1,0:T(8,128)(2,1)S(1)} %collective-permute-done.25.refs_7_.refs_2_, bf16[2,384,128]{2,1,0:T(8,128)(2,1)S(1)} %collective-permute-done.28.refs_4_.refs_3_, ...), custom_call_target="tpu_custom_call" | custom-call | flops 1800000000 | bytes 5400000 | tf_op jit(solution)/shard_map/pages/pallas_call | solution.py:36
  132.5 3.0 %collective-permute-done.34.refs_3_ = bf16[128,768]{1,0:T(8,128)(2,1)S(1)} collective-permute-done((bf16[128,768]{1,0:T(8,128)(2,1)S(1)}, bf16[128,768]{1,0:T(8,128)(2,1)S(1)}, u32[]{:S(2)}, u32[]{:S(2)}) %collective-permute-start.34) | collective-permute-done | bytes 196640 | tf_op jit(solution)/shard_map/ppermute | solution.py:63
  135.6 0.9 add_last.1
  (80 shorter events, 0.8 us)
Async XLA Ops:
  0.6 66.8 %copy-start = (f32[4,24,64,128]{3,2,1,0:T(8,128)S(1)}, f32[4,24,64,128]{3,2,1,0:T(8,128)}, u32[]{:S(2)}) copy-start(f32[4,24,64,128]{3,2,1,0:T(8,128)} %param.34) | copy-start | bytes 9437188
  0.6 7.6 %copy-start.13 = (s32[32]{0:T(128)S(1)}, s32[32]{0:T(128)}, u32[]{:S(2)}) copy-start(s32[32]{0:T(128)} %param.22) | copy-start | bytes 388
  0.7 7.6 %copy-start.14 = (s32[8]{0:T(128)S(1)}, s32[8]{0:T(128)}, u32[]{:S(2)}) copy-start(s32[8]{0:T(128)} %param.32) | copy-start | bytes 100
  0.7 7.6 %copy-start.15 = (s32[8]{0:T(128)S(1)}, s32[8]{0:T(128)}, u32[]{:S(2)}) copy-start(s32[8]{0:T(128)} %param.33) | copy-start | bytes 100
  0.7 7.6 %copy-start.16 = (s32[2]{0:T(128)S(1)}, s32[2]{0:T(128)}, u32[]{:S(2)}) copy-start(s32[2]{0:T(128)} %param.35) | copy-start | bytes 28
  3.1 17.5 %all-to-all-start = ((bf16[8,48,1024]{2,1,0:T(8,128)(2,1)}), bf16[8,48,1024]{2,1,0:T(8,128)(2,1)}, u32[]{:S(2)}, u32[]{:S(2)}) async-start(bf16[8,48,1024]{2,1,0:T(8,128)(2,1)} %pack_rows.1.refs_2_), calls=%async_computation | async-start | bytes 1572864 | tf_op jit(solution)/shard_map/all_to_all | solution.py:677
  8.9 7.5 %copy-start.9 = (f32[1536]{0:T(1024)S(1)}, f32[1536]{0:T(1024)}, u32[]{:S(2)}) copy-start(f32[1536]{0:T(1024)} %param.30) | copy-start | bytes 18436
  9.0 7.5 %copy-start.10 = (f32[1536]{0:T(1024)S(1)}, f32[1536]{0:T(1024)}, u32[]{:S(2)}) copy-start(f32[1536]{0:T(1024)} %param.25) | copy-start | bytes 18436
  9.0 7.5 %copy-start.11 = (f32[4,256]{1,0:T(4,128)S(1)}, f32[4,256]{1,0:T(4,128)}, u32[]{:S(2)}) copy-start(f32[4,256]{1,0:T(4,128)} %param.24) | copy-start | bytes 12292
  9.0 7.5 %copy-start.12 = (f32[256]{0:T(256)S(1)}, f32[256]{0:T(256)}, u32[]{:S(2)}) copy-start(f32[256]{0:T(256)} %param.26) | copy-start | bytes 3076
  9.0 7.6 %copy-start.17 = (f32[24]{0:T(128)S(1)}, f32[24]{0:T(128)}, u32[]{:S(2)}) copy-start(f32[24]{0:T(128)} %param.29) | copy-start | bytes 292
  9.0 7.6 %copy-start.18 = (f32[24]{0:T(128)S(1)}, f32[24]{0:T(128)}, u32[]{:S(2)}) copy-start(f32[24]{0:T(128)} %param.28) | copy-start | bytes 292
  9.0 7.6 %copy-start.19 = (f32[24]{0:T(128)S(1)}, f32[24]{0:T(128)}, u32[]{:S(2)}) copy-start(f32[24]{0:T(128)} %param.27) | copy-start | bytes 292
  11.6 22.3 %collective-permute-start = (bf16[128,1536]{1,0:T(8,128)(2,1)}, bf16[128,1536]{1,0:T(8,128)(2,1)}, u32[]{:S(2)}, u32[]{:S(2)}) collective-permute-start(bf16[128,1536]{1,0:T(8,128)(2,1)} %get-tuple-element.40), channel_id=1, source_target_pairs={{0,2},{2,0},{1,3},{3,1},{4,6},{6,4},{5,7},{7,5},{8,10},{10,8},{9,1... | collective-permute-start | bytes 1179656 | tf_op jit(solution)/shard_map/ppermute | solution.py:63
  13.6 20.3 %collective-permute-start.1 = (bf16[128,1536]{1,0:T(8,128)(2,1)}, bf16[128,1536]{1,0:T(8,128)(2,1)}, u32[]{:S(2)}, u32[]{:S(2)}) collective-permute-start(bf16[128,1536]{1,0:T(8,128)(2,1)} %get-tuple-element.40), channel_id=1, source_target_pairs={{0,8},{8,0},{1,9},{9,1},{2,10},{10,2},{3,11},{11,3},{4,12},{12,4},... | collective-permute-start | bytes 1179656 | tf_op jit(solution)/shard_map/ppermute | solution.py:63
  15.1 11.1 %collective-permute-start.2 = (bf16[16,1536]{1,0:T(8,128)(2,1)}, bf16[16,1536]{1,0:T(8,128)(2,1)S(1)}, u32[]{:S(2)}, u32[]{:S(2)}) collective-permute-start(bf16[16,1536]{1,0:T(8,128)(2,1)} %get-tuple-element.41), channel_id=1, source_target_pairs={{2,4},{6,8},{10,12},{14,16},{18,20},{22,24},{26,28},{3,5},{7,9},{1... | collective-permute-start | bytes 147464 | tf_op jit(solution)/shard_map/ppermute | solution.py:717
  15.8 10.5 %collective-permute-start.3 = (bf16[16,1536]{1,0:T(8,128)(2,1)}, bf16[16,1536]{1,0:T(8,128)(2,1)S(1)}, u32[]{:S(2)}, u32[]{:S(2)}) collective-permute-start(bf16[16,1536]{1,0:T(8,128)(2,1)} %get-tuple-element.41), channel_id=1, source_target_pairs={{2,6},{6,10},{10,14},{14,18},{18,22},{22,26},{26,30},{3,7},{7,11},... | collective-permute-start | bytes 147464 | tf_op jit(solution)/shard_map/ppermute | solution.py:718
  16.6 9.6 %copy-start.8 = (f32[4,1536]{1,0:T(4,128)S(1)}, f32[4,1536]{1,0:T(4,128)}, u32[]{:S(2)}) copy-start(f32[4,1536]{1,0:T(4,128)} %param.23) | copy-start | bytes 73732
  16.6 17.3 %copy-start.1 = (s32[58]{0:T(128)S(1)}, s32[58]{0:T(128)}, u32[]{:S(2)}) copy-start(s32[58]{0:T(128)} %concatenate.15.refs_0_) | copy-start | bytes 700
  22.5 0.7 copy-start.6
  23.3 22.3 %collective-permute-start.11 = (bf16[240,512]{1,0:T(8,128)(2,1)S(1)}, bf16[240,512]{1,0:T(8,128)(2,1)S(1)}, u32[]{:S(2)}, u32[]{:S(2)}) collective-permute-start(bf16[240,512]{1,0:T(8,128)(2,1)S(1)} %get-tuple-element.45), channel_id=1, source_target_pairs={{0,16},{16,0},{1,17},{17,1},{2,18},{18,2},{3,19},{19,3},{4,20},{20... | collective-permute-start | bytes 737288 | tf_op jit(solution)/shard_map/ppermute | solution.py:599
  26.2 17.8 %collective-permute-start.12 = (bf16[160,512]{1,0:T(8,128)(2,1)S(1)}, bf16[160,512]{1,0:T(8,128)(2,1)}, u32[]{:S(2)}, u32[]{:S(2)}) collective-permute-start(bf16[160,512]{1,0:T(8,128)(2,1)S(1)} %get-tuple-element.46), channel_id=1, source_target_pairs={{0,16},{16,0},{1,17},{17,1},{2,18},{18,2},{3,19},{19,3},{4,20},{20... | collective-permute-start | bytes 491528 | tf_op jit(solution)/shard_map/ppermute | solution.py:599
  26.2 9.6 %copy-start.4 = (bf16[16,1536]{1,0:T(8,128)(2,1)}, bf16[16,1536]{1,0:T(8,128)(2,1)S(1)}, u32[]{:S(2)}) copy-start(bf16[16,1536]{1,0:T(8,128)(2,1)S(1)} %collective-permute-done.3.refs_4_.refs_11_) | copy-start | bytes 147460
  26.3 25.2 %collective-permute-start.10 = (bf16[400,512]{1,0:T(8,128)(2,1)}, bf16[400,512]{1,0:T(8,128)(2,1)}, u32[]{:S(2)}, u32[]{:S(2)}) collective-permute-start(bf16[400,512]{1,0:T(8,128)(2,1)} %get-tuple-element.42.refs_5_.refs_1_), channel_id=1, source_target_pairs={{0,4},{4,0},{1,5},{5,1},{2,6},{6,2},{3,7},{7,3},{8,12},{12,8},{9,1... | collective-permute-start | bytes 1228808 | tf_op jit(solution)/shard_map/ppermute | solution.py:63
  35.9 11.2 %collective-permute-start.4 = (bf16[64,1536]{1,0:T(8,128)(2,1)}, bf16[64,1536]{1,0:T(8,128)(2,1)}, u32[]{:S(2)}, u32[]{:S(2)}) collective-permute-start(bf16[64,1536]{1,0:T(8,128)(2,1)} %get-tuple-element.43), channel_id=1, source_target_pairs={{0,2},{2,0},{1,3},{3,1},{4,6},{6,4},{5,7},{7,5},{8,10},{10,8},{9,1... | collective-permute-start | bytes 589832 | tf_op jit(solution)/shard_map/ppermute | solution.py:63
  40.2 8.0 %collective-permute-start.5 = (bf16[80,1536]{1,0:T(8,128)(2,1)}, bf16[80,1536]{1,0:T(8,128)(2,1)}, u32[]{:S(2)}, u32[]{:S(2)}) collective-permute-start(bf16[80,1536]{1,0:T(8,128)(2,1)} %get-tuple-element.44), channel_id=1, source_target_pairs={{0,8},{8,0},{1,9},{9,1},{2,10},{10,2},{3,11},{11,3},{4,12},{12,4},... | collective-permute-start | bytes 737288 | tf_op jit(solution)/shard_map/ppermute | solution.py:63
  44.0 7.5 %collective-permute-start.14 = (bf16[160,512]{1,0:T(8,128)(2,1)}, bf16[160,512]{1,0:T(8,128)(2,1)}, u32[]{:S(2)}, u32[]{:S(2)}) collective-permute-start(bf16[160,512]{1,0:T(8,128)(2,1)} %collective-permute-done.12.refs_4_.refs_1_), channel_id=1, source_target_pairs={{0,4},{4,0},{1,5},{5,1},{2,6},{6,2},{3,7},{7,3},{8,12},{12,8},{9,1... | collective-permute-start | bytes 491528 | tf_op jit(solution)/shard_map/ppermute | solution.py:63
  45.6 9.3 %collective-permute-start.13 = (bf16[240,512]{1,0:T(8,128)(2,1)S(1)}, bf16[240,512]{1,0:T(8,128)(2,1)}, u32[]{:S(2)}, u32[]{:S(2)}) collective-permute-start(bf16[240,512]{1,0:T(8,128)(2,1)S(1)} %collective-permute-done.11.refs_3_), channel_id=1, source_target_pairs={{0,4},{4,0},{1,5},{5,1},{2,6},{6,2},{3,7},{7,3},{8,12},{12,8},{9,1... | collective-permute-start | bytes 737288 | tf_op jit(solution)/shard_map/ppermute | solution.py:63
  46.0 1.0 copy-start.7
  47.0 9.6 %copy-start.2 = (bf16[256,1536]{1,0:T(8,128)(2,1)S(1)}, bf16[256,1536]{1,0:T(8,128)(2,1)}, u32[]{:S(2)}) copy-start(bf16[256,1536]{1,0:T(8,128)(2,1)} %refs_1_.5) | copy-start | bytes 2359300
  47.0 9.6 %copy-start.5 = (bf16[16,1536]{1,0:T(8,128)(2,1)S(1)}, bf16[16,1536]{1,0:T(8,128)(2,1)}, u32[]{:S(2)}) copy-start(bf16[16,1536]{1,0:T(8,128)(2,1)} %copy-done.4) | copy-start | bytes 147460
  47.1 9.4 %collective-permute-start.6 = (bf16[128,1536]{1,0:T(8,128)(2,1)}, bf16[128,1536]{1,0:T(8,128)(2,1)S(1)}, u32[]{:S(2)}, u32[]{:S(2)}) collective-permute-start(bf16[128,1536]{1,0:T(8,128)(2,1)} %collective-permute-done.refs_1_.refs_2_), channel_id=1, source_target_pairs={{0,1},{1,0},{2,3},{3,2},{4,5},{5,4},{6,7},{7,6},{8,9},{9,8},{10,11... | collective-permute-start | bytes 1179656 | tf_op jit(solution)/shard_map/ppermute | solution.py:63
  48.2 8.3 %collective-permute-start.7 = (bf16[128,1536]{1,0:T(8,128)(2,1)}, bf16[128,1536]{1,0:T(8,128)(2,1)S(1)}, u32[]{:S(2)}, u32[]{:S(2)}) collective-permute-start(bf16[128,1536]{1,0:T(8,128)(2,1)} %collective-permute-done.1.refs_2_.refs_3_), channel_id=1, source_target_pairs={{0,1},{1,0},{2,3},{3,2},{4,5},{5,4},{6,7},{7,6},{8,9},{9,8},{10,11... | collective-permute-start | bytes 1179656 | tf_op jit(solution)/shard_map/ppermute | solution.py:63
  51.5 16.0 %collective-permute-start.16 = (bf16[384,384]{1,0:T(8,128)(2,1)S(1)}, bf16[384,384]{1,0:T(8,128)(2,1)S(1)}, u32[]{:S(2)}, u32[]{:S(2)}) collective-permute-start(bf16[384,384]{1,0:T(8,128)(2,1)S(1)} %gate_part.1.refs_1_), channel_id=1, source_target_pairs={{0,16},{16,0},{1,17},{17,1},{2,18},{18,2},{3,19},{19,3},{4,20},{20... | collective-permute-start | bytes 884744 | tf_op jit(solution)/shard_map/ppermute | solution.py:599
  51.5 5.0 %collective-permute-start.8 = (bf16[64,1536]{1,0:T(8,128)(2,1)}, bf16[64,1536]{1,0:T(8,128)(2,1)S(1)}, u32[]{:S(2)}, u32[]{:S(2)}) collective-permute-start(bf16[64,1536]{1,0:T(8,128)(2,1)} %collective-permute-done.4.refs_4_), channel_id=1, source_target_pairs={{0,1},{1,0},{2,3},{3,2},{4,5},{5,4},{6,7},{7,6},{8,9},{9,8},{10,11... | collective-permute-start | bytes 589832 | tf_op jit(solution)/shard_map/ppermute | solution.py:63
  54.9 1.7 %collective-permute-start.9 = (bf16[80,1536]{1,0:T(8,128)(2,1)}, bf16[80,1536]{1,0:T(8,128)(2,1)S(1)}, u32[]{:S(2)}, u32[]{:S(2)}) collective-permute-start(bf16[80,1536]{1,0:T(8,128)(2,1)} %collective-permute-done.5.refs_5_), channel_id=1, source_target_pairs={{0,1},{1,0},{2,3},{3,2},{4,5},{5,4},{6,7},{7,6},{8,9},{9,8},{10,11... | collective-permute-start | bytes 737288 | tf_op jit(solution)/shard_map/ppermute | solution.py:63
  58.1 3.2 %copy-start.3 = (f32[1536,96]{0,1:T(8,128)S(1)}, f32[1536,96]{0,1:T(8,128)}, u32[]{:S(2)}) copy-start(f32[1536,96]{0,1:T(8,128)} %param.31) | copy-start | bytes 1769476
  60.8 12.3 %collective-permute-start.15 = (bf16[2,528,128]{2,1,0:T(8,128)(2,1)S(1)}, bf16[2,528,128]{2,1,0:T(8,128)(2,1)S(1)}, u32[]{:S(2)}, u32[]{:S(2)}) collective-permute-start(bf16[2,528,128]{2,1,0:T(8,128)(2,1)S(1)} %get-tuple-element.48.refs_2_), channel_id=1, source_target_pairs={{0,1},{1,0},{2,3},{3,2},{4,5},{5,4},{6,7},{7,6},{8,9},{9,8},{10,11... | collective-permute-start | bytes 811016 | tf_op jit(solution)/shard_map/ppermute | solution.py:63
  61.9 6.0 %collective-permute-start.19 = (bf16[96,384]{1,0:T(8,128)(2,1)S(1)}, bf16[96,384]{1,0:T(8,128)(2,1)S(1)}, u32[]{:S(2)}, u32[]{:S(2)}) collective-permute-start(bf16[96,384]{1,0:T(8,128)(2,1)S(1)} %get-tuple-element.61), channel_id=1, source_target_pairs={{0,2},{2,0},{1,3},{3,1},{4,6},{6,4},{5,7},{7,5},{8,10},{10,8},{9,1... | collective-permute-start | bytes 221192 | tf_op jit(solution)/shard_map/ppermute | solution.py:63
  63.4 6.2 %collective-permute-start.20 = (bf16[96,384]{1,0:T(8,128)(2,1)S(1)}, bf16[96,384]{1,0:T(8,128)(2,1)S(1)}, u32[]{:S(2)}, u32[]{:S(2)}) collective-permute-start(bf16[96,384]{1,0:T(8,128)(2,1)S(1)} %get-tuple-element.62), channel_id=1, source_target_pairs={{0,8},{8,0},{1,9},{9,1},{2,10},{10,2},{3,11},{11,3},{4,12},{12,4},... | collective-permute-start | bytes 221192 | tf_op jit(solution)/shard_map/ppermute | solution.py:63
  66.0 5.3 %collective-permute-start.21 = (bf16[96,384]{1,0:T(8,128)(2,1)S(1)}, bf16[96,384]{1,0:T(8,128)(2,1)S(1)}, u32[]{:S(2)}, u32[]{:S(2)}) collective-permute-start(bf16[96,384]{1,0:T(8,128)(2,1)S(1)} %get-tuple-element.63), channel_id=1, source_target_pairs={{0,10},{2,8},{8,2},{10,0},{1,11},{3,9},{9,3},{11,1},{4,14},{6,12},... | collective-permute-start | bytes 221192 | tf_op jit(solution)/shard_map/ppermute | solution.py:745
  67.5 16.2 %collective-permute-start.23 = (bf16[384,384]{1,0:T(8,128)(2,1)S(1)}, bf16[384,384]{1,0:T(8,128)(2,1)S(1)}, u32[]{:S(2)}, u32[]{:S(2)}) collective-permute-start(bf16[384,384]{1,0:T(8,128)(2,1)S(1)} %gate_part.1.refs_1_), channel_id=1, source_target_pairs={{0,4},{4,0},{1,5},{5,1},{2,6},{6,2},{3,7},{7,3},{8,12},{12,8},{9,1... | collective-permute-start | bytes 884744 | tf_op jit(solution)/shard_map/ppermute | solution.py:63
  67.8 15.8 %collective-permute-start.24 = (bf16[384,384]{1,0:T(8,128)(2,1)S(1)}, bf16[384,384]{1,0:T(8,128)(2,1)S(1)}, u32[]{:S(2)}, u32[]{:S(2)}) collective-permute-start(bf16[384,384]{1,0:T(8,128)(2,1)S(1)} %collective-permute-done.16.refs_7_.refs_3_), channel_id=1, source_target_pairs={{0,4},{4,0},{1,5},{5,1},{2,6},{6,2},{3,7},{7,3},{8,12},{12,8},{9,1... | collective-permute-start | bytes 884744 | tf_op jit(solution)/shard_map/ppermute | solution.py:63
  71.4 15.5 %collective-permute-start.22 = (bf16[384,384]{1,0:T(8,128)(2,1)S(1)}, bf16[384,384]{1,0:T(8,128)(2,1)S(1)}, u32[]{:S(2)}, u32[]{:S(2)}) collective-permute-start(bf16[384,384]{1,0:T(8,128)(2,1)S(1)} %out_part.1.refs_1_), channel_id=1, source_target_pairs={{0,16},{16,0},{1,17},{17,1},{2,18},{18,2},{3,19},{19,3},{4,20},{20... | collective-permute-start | bytes 884744 | tf_op jit(solution)/shard_map/ppermute | solution.py:599
  81.6 8.1 %collective-permute-start.17 = (bf16[2,400,128]{2,1,0:T(8,128)(2,1)S(1)}, bf16[2,400,128]{2,1,0:T(8,128)(2,1)S(1)}, u32[]{:S(2)}, u32[]{:S(2)}) collective-permute-start(bf16[2,400,128]{2,1,0:T(8,128)(2,1)S(1)} %get-tuple-element.51.refs_1_.refs_5_), channel_id=1, source_target_pairs={{0,4},{4,0},{1,5},{5,1},{2,6},{6,2},{3,7},{7,3},{8,12},{12,8},{9,1... | collective-permute-start | bytes 614408 | tf_op jit(solution)/shard_map/ppermute | solution.py:63
  81.9 22.9 %collective-permute-start.26 = (bf16[384,384]{1,0:T(8,128)(2,1)S(1)}, bf16[384,384]{1,0:T(8,128)(2,1)S(1)}, u32[]{:S(2)}, u32[]{:S(2)}) collective-permute-start(bf16[384,384]{1,0:T(8,128)(2,1)S(1)} %out_part.1.refs_1_), channel_id=1, source_target_pairs={{0,4},{4,0},{1,5},{5,1},{2,6},{6,2},{3,7},{7,3},{8,12},{12,8},{9,1... | collective-permute-start | bytes 884744 | tf_op jit(solution)/shard_map/ppermute | solution.py:63
  86.9 17.9 %collective-permute-start.27 = (bf16[384,384]{1,0:T(8,128)(2,1)S(1)}, bf16[384,384]{1,0:T(8,128)(2,1)S(1)}, u32[]{:S(2)}, u32[]{:S(2)}) collective-permute-start(bf16[384,384]{1,0:T(8,128)(2,1)S(1)} %collective-permute-done.22.refs_9_.refs_3_), channel_id=1, source_target_pairs={{0,4},{4,0},{1,5},{5,1},{2,6},{6,2},{3,7},{7,3},{8,12},{12,8},{9,1... | collective-permute-start | bytes 884744 | tf_op jit(solution)/shard_map/ppermute | solution.py:63
  90.3 8.1 %collective-permute-start.18 = (bf16[400,128]{1,0:T(8,128)(2,1)S(1)}, bf16[400,128]{1,0:T(8,128)(2,1)S(1)}, u32[]{:S(2)}, u32[]{:S(2)}) collective-permute-start(bf16[400,128]{1,0:T(8,128)(2,1)S(1)} %compose.1.refs_8_), channel_id=1, source_target_pairs={{0,16},{1,17},{2,18},{3,19},{4,20},{5,21},{6,22},{7,23},{8,24},{9,... | collective-permute-start | bytes 307208 | tf_op jit(solution)/shard_map/ppermute | solution.py:836
  99.4 6.3 %collective-permute-start.25 = (bf16[2,384,128]{2,1,0:T(8,128)(2,1)S(1)}, bf16[2,384,128]{2,1,0:T(8,128)(2,1)S(1)}, u32[]{:S(2)}, u32[]{:S(2)}) collective-permute-start(bf16[2,384,128]{2,1,0:T(8,128)(2,1)S(1)} %get-tuple-element.64), channel_id=1, source_target_pairs={{0,2},{2,0},{1,3},{3,1},{4,6},{6,4},{5,7},{7,5},{8,10},{10,8},{9,1... | collective-permute-start | bytes 589832 | tf_op jit(solution)/shard_map/ppermute | solution.py:63
  101.3 7.9 %collective-permute-start.28 = (bf16[2,384,128]{2,1,0:T(8,128)(2,1)S(1)}, bf16[2,384,128]{2,1,0:T(8,128)(2,1)S(1)}, u32[]{:S(2)}, u32[]{:S(2)}) collective-permute-start(bf16[2,384,128]{2,1,0:T(8,128)(2,1)S(1)} %get-tuple-element.67), channel_id=1, source_target_pairs={{0,8},{8,0},{1,9},{9,1},{2,10},{10,2},{3,11},{11,3},{4,12},{12,4},... | collective-permute-start | bytes 589832 | tf_op jit(solution)/shard_map/ppermute | solution.py:63
  101.5 7.7 %collective-permute-start.29 = (bf16[2,384,128]{2,1,0:T(8,128)(2,1)S(1)}, bf16[2,384,128]{2,1,0:T(8,128)(2,1)S(1)}, u32[]{:S(2)}, u32[]{:S(2)}) collective-permute-start(bf16[2,384,128]{2,1,0:T(8,128)(2,1)S(1)} %get-tuple-element.68), channel_id=1, source_target_pairs={{0,10},{2,8},{8,2},{10,0},{1,11},{3,9},{9,3},{11,1},{4,14},{6,12},... | collective-permute-start | bytes 589832 | tf_op jit(solution)/shard_map/ppermute | solution.py:861
  111.4 3.8 %collective-permute-start.30 = (bf16[4,144,1536]{2,1,0:T(8,128)(2,1)S(1)}, bf16[4,144,1536]{2,1,0:T(8,128)(2,1)S(1)}, u32[]{:S(2)}, u32[]{:S(2)}) collective-permute-start(bf16[4,144,1536]{2,1,0:T(8,128)(2,1)S(1)} %mix_send.1.refs_4_), channel_id=1, source_target_pairs={{0,1},{1,0},{2,3},{3,2},{4,5},{5,4},{6,7},{7,6},{8,9},{9,8},{10,11... | collective-permute-start | bytes 5308424 | tf_op jit(solution)/shard_map/ppermute | solution.py:63
  115.6 12.9 %collective-permute-start.31 = (bf16[2,144,768]{2,1,0:T(8,128)(2,1)S(1)}, bf16[2,144,768]{2,1,0:T(8,128)(2,1)S(1)}, u32[]{:S(2)}, u32[]{:S(2)}) collective-permute-start(bf16[2,144,768]{2,1,0:T(8,128)(2,1)S(1)} %get-tuple-element.70.refs_5_), channel_id=1, source_target_pairs={{0,2},{2,0},{1,3},{3,1},{4,6},{6,4},{5,7},{7,5},{8,10},{10,8},{9,1... | collective-permute-start | bytes 1327112 | tf_op jit(solution)/shard_map/ppermute | solution.py:63
  117.5 10.9 %collective-permute-start.32 = (bf16[2,128,768]{2,1,0:T(8,128)(2,1)S(1)}, bf16[2,128,768]{2,1,0:T(8,128)(2,1)S(1)}, u32[]{:S(2)}, u32[]{:S(2)}) collective-permute-start(bf16[2,128,768]{2,1,0:T(8,128)(2,1)S(1)} %get-tuple-element.72), channel_id=1, source_target_pairs={{0,8},{8,0},{1,9},{9,1},{2,10},{10,2},{3,11},{11,3},{4,12},{12,4},... | collective-permute-start | bytes 1179656 | tf_op jit(solution)/shard_map/ppermute | solution.py:63
  128.6 7.0 %collective-permute-start.33 = (bf16[144,768]{1,0:T(8,128)(2,1)S(1)}, bf16[144,768]{1,0:T(8,128)(2,1)S(1)}, u32[]{:S(2)}, u32[]{:S(2)}) collective-permute-start(bf16[144,768]{1,0:T(8,128)(2,1)S(1)} %get-tuple-element.74), channel_id=1, source_target_pairs={{0,8},{8,0},{1,9},{9,1},{2,10},{10,2},{3,11},{11,3},{4,12},{12,4},... | collective-permute-start | bytes 663560 | tf_op jit(solution)/shard_map/ppermute | solution.py:63
  129.7 5.8 %collective-permute-start.34 = (bf16[128,768]{1,0:T(8,128)(2,1)S(1)}, bf16[128,768]{1,0:T(8,128)(2,1)S(1)}, u32[]{:S(2)}, u32[]{:S(2)}) collective-permute-start(bf16[128,768]{1,0:T(8,128)(2,1)S(1)} %get-tuple-element.76), channel_id=1, source_target_pairs={{0,2},{2,0},{1,3},{3,1},{4,6},{6,4},{5,7},{7,5},{8,10},{10,8},{9,1... | collective-permute-start | bytes 589832 | tf_op jit(solution)/shard_map/ppermute | solution.py:63

commit v5 on v4

--- a/solution.py
+++ b/solution.py
@@ -384,7 +384,7 @@
 
         return carry
 
-    lax.fori_loop(0, chunks, one, 0, unroll=2)
+    lax.fori_loop(0, chunks, one, 0, unroll=4)
     for run in range(2):
         factor = factor_ref[run * per_run]
         for i in range(run * per_run + 1, (run + 1) * per_run):
@@ -448,7 +448,7 @@
 
         return carry
 
-    lax.fori_loop(0, chunks, one, 0, unroll=2)
+    lax.fori_loop(0, chunks, one, 0, unroll=4)
 
 
 def onto(run, h, before):
@@ -532,7 +532,7 @@
         square_ref[i] = dot(ones, squares, NT, HIGHEST)
         return carry
 
-    lax.fori_loop(0, chunks, one, 0, unroll=2)
+    lax.fori_loop(0, chunks, one, 0, unroll=4)
 
 
 def columns_kernel(sizes, count, rows, ints, *refs):

time: 137 us -> 137 us (level)
    ppermute x1, starting transfers between devices: 2.62 us -> 4.07 us  [on_device(): block = lax.ppermute(block, 't', onward)]
  transfers between devices with their start and end apart: 36 -> 36, of which waited for: 12 -> 12; matrix products, arithmetic and copies ran while one was open for 1% -> 1% of each run, Pallas kernels for 29% -> 28%
where the time goes in v5:
time: 137 us
  starting transfers between devices  52.5 us (38%)
  Pallas kernels  44.1 us (32%)
  waiting for transfers between devices  36.5 us (27%)
  local copies, waits for them, and re-layouts  2.46 us (2%)
    pallas_call x24, Pallas kernels, call(): pl.pallas_call(kernel, name=name, out_shape=out_shape, in_specs=specs, ou...  44.1 us
    ppermute x26, starting transfers between devices, swap(): return lax.ppermute(x, axis, [(0, 1), (1, 0)])  34.4 us
    ppermute x26, waiting for transfers between devices, swap(): return lax.ppermute(x, axis, [(0, 1), (1, 0)])  25.4 us
    ppermute x4, waiting for transfers between devices, round_t(): return lax.ppermute(x, 't', [(i, (i + 1) % count) for i in range(count)])  5.46 us
    all_to_all x1, starting transfers between devices, on_device(): inner_got = lax.all_to_all(inner_send, GROUP, 0, 0, tiled=True)  5.24 us
    ppermute x4, starting transfers between devices, round_t(): return lax.ppermute(x, 't', [(i, (i + 1) % count) for i in range(count)])  4.67 us
    ppermute x1, starting transfers between devices, on_device(): block = lax.ppermute(block, 't', onward)  4.07 us
    all_to_all x1, waiting for transfers between devices, on_device(): inner_got = lax.all_to_all(inner_send, GROUP, 0, 0, tiled=True)  3.92 us
  transfers between devices with their start and end apart: 36, of which 12 were waited for; matrix products, arithmetic and copies ran while one was open for 1% of the time, Pallas kernels for 28%

profile of v5, /device:TPU:0, one launch (start us, length us, event | category | flops | bytes accessed | tf_op | source)
XLA Modules:
  0.0 136.8 jit_solution(15923365906806018850)
XLA Ops:
  0.7 2.4 %pack_rows.1.refs_2_ = bf16[8,48,1024]{2,1,0:T(8,128)(2,1)} custom-call(f32[48,3072]{1,0:T(8,128)} %refs_0_.1, f32[48,304]{1,0:T(8,128)} %refs_1_.3, f32[48,3072]{1,0:T(8,128)} %refs_2_.1), custom_call_target="tpu_custom_call" | custom-call | flops 2000000000 | bytes 6000000 | tf_op jit(solution)/shard_map/pack_rows/pallas_call | solution.py:36
  3.1 5.2 %all-to-all-start = ((bf16[8,48,1024]{2,1,0:T(8,128)(2,1)}), bf16[8,48,1024]{2,1,0:T(8,128)(2,1)}, u32[]{:S(2)}, u32[]{:S(2)}) async-start(bf16[8,48,1024]{2,1,0:T(8,128)(2,1)} %pack_rows.1.refs_2_), calls=%async_computation | async-start | bytes 1572864 | tf_op jit(solution)/shard_map/all_to_all | solution.py:677
  8.3 0.6 concatenate.15.refs_0_
  9.0 2.6 %own_rows.1 = (bf16[128,1536]{1,0:T(8,128)(2,1)}, bf16[16,1536]{1,0:T(8,128)(2,1)}) custom-call(s32[58]{0:T(128)} %concatenate.15.refs_0_, bf16[256,1536]{1,0:T(8,128)(2,1)} %refs_1_.5, bf16[8,48,1024]{2,1,0:T(8,128)(2,1)} %pack_rows.1.refs_2_), custom_call_target="tpu_custom_call" | custom-call | flops 1000000000 | bytes 3000000 | tf_op jit(solution)/shard_map/own_rows/pallas_call | solution.py:36
  11.6 2.1 %collective-permute-start = (bf16[128,1536]{1,0:T(8,128)(2,1)}, bf16[128,1536]{1,0:T(8,128)(2,1)}, u32[]{:S(2)}, u32[]{:S(2)}) collective-permute-start(bf16[128,1536]{1,0:T(8,128)(2,1)} %get-tuple-element.40), channel_id=1, source_target_pairs={{0,2},{2,0},{1,3},{3,1},{4,6},{6,4},{5,7},{7,5},{8,10},{10,8},{9,1... | collective-permute-start | bytes 1179656 | tf_op jit(solution)/shard_map/ppermute | solution.py:63
  13.6 1.5 %collective-permute-start.1 = (bf16[128,1536]{1,0:T(8,128)(2,1)}, bf16[128,1536]{1,0:T(8,128)(2,1)}, u32[]{:S(2)}, u32[]{:S(2)}) collective-permute-start(bf16[128,1536]{1,0:T(8,128)(2,1)} %get-tuple-element.40), channel_id=1, source_target_pairs={{0,8},{8,0},{1,9},{9,1},{2,10},{10,2},{3,11},{11,3},{4,12},{12,4},... | collective-permute-start | bytes 1179656 | tf_op jit(solution)/shard_map/ppermute | solution.py:63
  15.1 0.7 collective-permute-start.2
  15.8 0.7 collective-permute-start.3
  16.6 3.9 %all-to-all-done.refs_0_ = bf16[8,48,1024]{2,1,0:T(8,128)(2,1)} async-done(((bf16[8,48,1024]{2,1,0:T(8,128)(2,1)}), bf16[8,48,1024]{2,1,0:T(8,128)(2,1)}, u32[]{:S(2)}, u32[]{:S(2)}) %all-to-all-start) | async-done | bytes 786464 | tf_op jit(solution)/shard_map/all_to_all | solution.py:677
  20.5 2.0 %repack_inner.1 = (bf16[400,512]{1,0:T(8,128)(2,1)}, bf16[240,512]{1,0:T(8,128)(2,1)S(1)}, bf16[160,512]{1,0:T(8,128)(2,1)S(1)}, bf16[384,384]{1,0:T(8,128)(2,1)S(1)}) custom-call(bf16[8,48,1024]{2,1,0:T(8,128)(2,1)} %all-to-all-done.refs_0_), custom_call_target="tpu_custom_call" | custom-call | flops 1000000000 | bytes 3000000 | tf_op jit(solution)/shard_map/repack_inner/pallas_call | solution.py:36
  22.5 0.7 copy-done.6
  23.3 2.9 %collective-permute-start.11 = (bf16[240,512]{1,0:T(8,128)(2,1)S(1)}, bf16[240,512]{1,0:T(8,128)(2,1)S(1)}, u32[]{:S(2)}, u32[]{:S(2)}) collective-permute-start(bf16[240,512]{1,0:T(8,128)(2,1)S(1)} %get-tuple-element.45), channel_id=1, source_target_pairs={{0,16},{16,0},{1,17},{17,1},{2,18},{18,2},{3,19},{19,3},{4,20},{20... | collective-permute-start | bytes 737288 | tf_op jit(solution)/shard_map/ppermute | solution.py:599
  26.3 7.7 %collective-permute-start.10 = (bf16[400,512]{1,0:T(8,128)(2,1)}, bf16[400,512]{1,0:T(8,128)(2,1)}, u32[]{:S(2)}, u32[]{:S(2)}) collective-permute-start(bf16[400,512]{1,0:T(8,128)(2,1)} %get-tuple-element.42.refs_5_.refs_1_), channel_id=1, source_target_pairs={{0,4},{4,0},{1,5},{5,1},{2,6},{6,2},{3,7},{7,3},{8,12},{12,8},{9,1... | collective-permute-start | bytes 1228808 | tf_op jit(solution)/shard_map/ppermute | solution.py:63
  33.9 1.9 %forward_rows.1 = (bf16[64,1536]{1,0:T(8,128)(2,1)}, bf16[80,1536]{1,0:T(8,128)(2,1)}) custom-call(s32[58]{0:T(128)S(1)} %copy-done.1, bf16[128,1536]{1,0:T(8,128)(2,1)} %collective-permute-done.refs_1_.refs_2_, bf16[128,1536]{1,0:T(8,128)(2,1)} %collective-permute-done.1.refs_2_.refs_3_, bf16[16,1536]{1,0:T(8,128)(2,1)S(1)} %collective-permute-done.2.refs_3_.refs_10_, ...), custom_call_target="tpu_custom_call" | custom-call | flops 1000000000 | bytes 3000000 | tf_op jit(solution)/shard_map/forward_rows/pallas_call | solution.py:36
  35.9 4.4 %collective-permute-start.4 = (bf16[64,1536]{1,0:T(8,128)(2,1)}, bf16[64,1536]{1,0:T(8,128)(2,1)}, u32[]{:S(2)}, u32[]{:S(2)}) collective-permute-start(bf16[64,1536]{1,0:T(8,128)(2,1)} %get-tuple-element.43), channel_id=1, source_target_pairs={{0,2},{2,0},{1,3},{3,1},{4,6},{6,4},{5,7},{7,5},{8,10},{10,8},{9,1... | collective-permute-start | bytes 589832 | tf_op jit(solution)/shard_map/ppermute | solution.py:63
  40.2 1.3 collective-permute-start.5
  41.6 2.4 %collective-permute-done.12.refs_4_.refs_1_ = bf16[160,512]{1,0:T(8,128)(2,1)} collective-permute-done((bf16[160,512]{1,0:T(8,128)(2,1)S(1)}, bf16[160,512]{1,0:T(8,128)(2,1)}, u32[]{:S(2)}, u32[]{:S(2)}) %collective-permute-start.12) | collective-permute-done | bytes 163872 | tf_op jit(solution)/shard_map/ppermute | solution.py:599
  44.0 1.6 %collective-permute-start.14 = (bf16[160,512]{1,0:T(8,128)(2,1)}, bf16[160,512]{1,0:T(8,128)(2,1)}, u32[]{:S(2)}, u32[]{:S(2)}) collective-permute-start(bf16[160,512]{1,0:T(8,128)(2,1)} %collective-permute-done.12.refs_4_.refs_1_), channel_id=1, source_target_pairs={{0,4},{4,0},{1,5},{5,1},{2,6},{6,2},{3,7},{7,3},{8,12},{12,8},{9,1... | collective-permute-start | bytes 491528 | tf_op jit(solution)/shard_map/ppermute | solution.py:63
  45.6 0.5 collective-permute-start.13
  46.0 1.0 copy-done.7
  47.1 1.1 collective-permute-done.5.refs_5_
  48.2 3.2 %collective-permute-done.14.refs_6_ = bf16[160,512]{1,0:T(8,128)(2,1)} collective-permute-done((bf16[160,512]{1,0:T(8,128)(2,1)}, bf16[160,512]{1,0:T(8,128)(2,1)}, u32[]{:S(2)}, u32[]{:S(2)}) %collective-permute-start.14) | collective-permute-done | bytes 163872 | tf_op jit(solution)/shard_map/ppermute | solution.py:63
  51.5 3.4 %collective-permute-done.13.refs_5_ = bf16[240,512]{1,0:T(8,128)(2,1)} collective-permute-done((bf16[240,512]{1,0:T(8,128)(2,1)S(1)}, bf16[240,512]{1,0:T(8,128)(2,1)}, u32[]{:S(2)}, u32[]{:S(2)}) %collective-permute-start.13) | collective-permute-done | bytes 245792 | tf_op jit(solution)/shard_map/ppermute | solution.py:63
  54.9 1.6 %inner_weights.1.refs_1_ = bf16[1536,640]{1,0:T(8,128)(2,1)S(1)} custom-call(s32[58]{0:T(128)S(1)} %copy-done.1, bf16[400,512]{1,0:T(8,128)(2,1)} %get-tuple-element.42.refs_5_.refs_1_, bf16[400,512]{1,0:T(8,128)(2,1)} %collective-permute-done.10.refs_2_, bf16[240,512]{1,0:T(8,128)(2,1)S(1)} %collective-permute-done.11.refs_3_, ...), custom_call_target="tpu_custom_call" | custom-call | flops 15000000512 | bytes 45000000 | tf_op jit(solution)/shard_map/inner_weights/pallas_call | solution.py:36
  56.6 1.5 %assemble_rows.1.refs_0_ = bf16[2,528,1536]{2,1,0:T(8,128)(2,1)S(1)} custom-call(s32[58]{0:T(128)S(1)} %copy-done.1, bf16[256,1536]{1,0:T(8,128)(2,1)S(1)} %copy-done.2, bf16[128,1536]{1,0:T(8,128)(2,1)} %collective-permute-done.refs_1_.refs_2_, bf16[128,1536]{1,0:T(8,128)(2,1)} %collective-permute-done.1.refs_2_.refs_3_, ...), custom_call_target="tpu_custom_call" | custom-call | flops 2000000000 | bytes 6000000 | tf_op jit(solution)/shard_map/assemble_rows/pallas_call | solution.py:36
  58.1 2.7 %inner_projection.1 = (bf16[2,528,384]{2,1,0:T(8,128)(2,1)S(1)}, bf16[2,528,128]{2,1,0:T(8,128)(2,1)S(1)}, f32[2,528,128]{2,1,0:T(8,128)S(1)}) custom-call(bf16[2,528,1536]{2,1,0:T(8,128)(2,1)S(1)} %assemble_rows.1.refs_0_, bf16[1536,640]{1,0:T(8,128)(2,1)S(1)} %inner_weights.1.refs_1_), custom_call_target="tpu_custom_call" | custom-call | flops 3500000000 | bytes 10500000 | tf_op jit(solution)/shard_map/inner_projection/pallas_call | solution.py:36
  60.8 0.5 collective-permute-start.15
  61.3 0.6 pack_out.1
  61.9 1.6 %collective-permute-start.19 = (bf16[96,384]{1,0:T(8,128)(2,1)S(1)}, bf16[96,384]{1,0:T(8,128)(2,1)S(1)}, u32[]{:S(2)}, u32[]{:S(2)}) collective-permute-start(bf16[96,384]{1,0:T(8,128)(2,1)S(1)} %get-tuple-element.61), channel_id=1, source_target_pairs={{0,2},{2,0},{1,3},{3,1},{4,6},{6,4},{5,7},{7,5},{8,10},{10,8},{9,1... | collective-permute-start | bytes 221192 | tf_op jit(solution)/shard_map/ppermute | solution.py:63
  63.4 2.6 %collective-permute-start.20 = (bf16[96,384]{1,0:T(8,128)(2,1)S(1)}, bf16[96,384]{1,0:T(8,128)(2,1)S(1)}, u32[]{:S(2)}, u32[]{:S(2)}) collective-permute-start(bf16[96,384]{1,0:T(8,128)(2,1)S(1)} %get-tuple-element.62), channel_id=1, source_target_pairs={{0,8},{8,0},{1,9},{9,1},{2,10},{10,2},{3,11},{11,3},{4,12},{12,4},... | collective-permute-start | bytes 221192 | tf_op jit(solution)/shard_map/ppermute | solution.py:63
  66.0 1.4 %collective-permute-start.21 = (bf16[96,384]{1,0:T(8,128)(2,1)S(1)}, bf16[96,384]{1,0:T(8,128)(2,1)S(1)}, u32[]{:S(2)}, u32[]{:S(2)}) collective-permute-start(bf16[96,384]{1,0:T(8,128)(2,1)S(1)} %get-tuple-element.63), channel_id=1, source_target_pairs={{0,10},{2,8},{8,2},{10,0},{1,11},{3,9},{9,3},{11,1},{4,14},{6,12},... | collective-permute-start | bytes 221192 | tf_op jit(solution)/shard_map/ppermute | solution.py:745
  67.5 0.4 collective-permute-start.23
  67.8 1.7 %collective-permute-start.24 = (bf16[384,384]{1,0:T(8,128)(2,1)S(1)}, bf16[384,384]{1,0:T(8,128)(2,1)S(1)}, u32[]{:S(2)}, u32[]{:S(2)}) collective-permute-start(bf16[384,384]{1,0:T(8,128)(2,1)S(1)} %collective-permute-done.16.refs_7_.refs_3_), channel_id=1, source_target_pairs={{0,4},{4,0},{1,5},{5,1},{2,6},{6,2},{3,7},{7,3},{8,12},{12,8},{9,1... | collective-permute-start | bytes 884744 | tf_op jit(solution)/shard_map/ppermute | solution.py:63
  69.6 1.7 %collective-permute-done.21.refs_3_ = bf16[96,384]{1,0:T(8,128)(2,1)S(1)} collective-permute-done((bf16[96,384]{1,0:T(8,128)(2,1)S(1)}, bf16[96,384]{1,0:T(8,128)(2,1)S(1)}, u32[]{:S(2)}, u32[]{:S(2)}) %collective-permute-start.21) | collective-permute-done | bytes 73760 | tf_op jit(solution)/shard_map/ppermute | solution.py:745
  71.4 1.7 %collective-permute-start.22 = (bf16[384,384]{1,0:T(8,128)(2,1)S(1)}, bf16[384,384]{1,0:T(8,128)(2,1)S(1)}, u32[]{:S(2)}, u32[]{:S(2)}) collective-permute-start(bf16[384,384]{1,0:T(8,128)(2,1)S(1)} %out_part.1.refs_1_), channel_id=1, source_target_pairs={{0,16},{16,0},{1,17},{17,1},{2,18},{18,2},{3,19},{19,3},{4,20},{20... | collective-permute-start | bytes 884744 | tf_op jit(solution)/shard_map/ppermute | solution.py:599
  73.1 8.0 %states.1 = (bf16[8,128,384]{2,1,0:T(8,128)(2,1)S(1)}, bf16[8,128,128]{2,1,0:T(8,128)(2,1)S(1)}, bf16[8,128,128]{2,1,0:T(8,128)(2,1)S(1)}, f32[8,128,128]{2,1,0:...) custom-call(s32[58]{0:T(128)S(1)} %copy-done.1, ...), custom_call_target="tpu_custom_call" | custom-call | flops 7000000000 | bytes 21000000 | tf_op jit(solution)/shard_map/states/pallas_call | solution.py:36
  81.2 2.0 %collective-permute-start.26 = (bf16[384,384]{1,0:T(8,128)(2,1)S(1)}, bf16[384,384]{1,0:T(8,128)(2,1)S(1)}, u32[]{:S(2)}, u32[]{:S(2)}) collective-permute-start(bf16[384,384]{1,0:T(8,128)(2,1)S(1)} %out_part.1.refs_1_), channel_id=1, source_target_pairs={{0,4},{4,0},{1,5},{5,1},{2,6},{6,2},{3,7},{7,3},{8,12},{12,8},{9,1... | collective-permute-start | bytes 884744 | tf_op jit(solution)/shard_map/ppermute | solution.py:63
  83.2 0.7 gate_weights.1.refs_1_
  83.9 3.0 %collective-permute-done.22.refs_9_.refs_3_ = bf16[384,384]{1,0:T(8,128)(2,1)S(1)} collective-permute-done((bf16[384,384]{1,0:T(8,128)(2,1)S(1)}, bf16[384,384]{1,0:T(8,128)(2,1)S(1)}, u32[]{:S(2)}, u32[]{:S(2)}) %collective-permute-start.22) | collective-permute-done | bytes 294944 | tf_op jit(solution)/shard_map/ppermute | solution.py:599
  86.9 0.3 collective-permute-start.27
  87.2 2.0 %collective-permute-done.17.refs_2_ = bf16[2,400,128]{2,1,0:T(8,128)(2,1)S(1)} collective-permute-done((bf16[2,400,128]{2,1,0:T(8,128)(2,1)S(1)}, bf16[2,400,128]{2,1,0:T(8,128)(2,1)S(1)}, u32[]{:S(2)}, u32[]{:S(2)}) %collective-permute-start.17) | collective-permute-done | bytes 204832 | tf_op jit(solution)/shard_map/ppermute | solution.py:63
  89.2 0.6 compose.1.refs_8_
  89.8 4.1 %collective-permute-start.18 = (bf16[400,128]{1,0:T(8,128)(2,1)S(1)}, bf16[400,128]{1,0:T(8,128)(2,1)S(1)}, u32[]{:S(2)}, u32[]{:S(2)}) collective-permute-start(bf16[400,128]{1,0:T(8,128)(2,1)S(1)} %compose.1.refs_8_), channel_id=1, source_target_pairs={{0,16},{1,17},{2,18},{3,19},{4,20},{5,21},{6,22},{7,23},{8,24},{9,... | collective-permute-start | bytes 307208 | tf_op jit(solution)/shard_map/ppermute | solution.py:836
  93.9 5.2 %within_chunks.1.refs_4_ = f32[8,128,384]{2,1,0:T(8,128)S(1)} custom-call(s32[58]{0:T(128)S(1)} %copy-done.1, bf16[8,128,384]{2,1,0:T(8,128)(2,1)S(1)} %get-tuple-element.57.refs_1_, bf16[8,128,128]{2,1,0:T(8,128)(2,1)S(1)} %get-tuple-element.58.refs_2_, bf16[8,128,128]{2,1,0:T(8,128)(2,1)S(1)} %get-tuple-element.55.refs_3_.refs_2_, ...), custom_call_target="tpu_custom_call" | custom-call | flops 5000000000 | bytes 15000000 | tf_op jit(solution)/shard_map/within_chunks/pallas_call | solution.py:36
  99.1 1.1 entering_states.1
  100.2 2.0 %collective-permute-start.25 = (bf16[2,384,128]{2,1,0:T(8,128)(2,1)S(1)}, bf16[2,384,128]{2,1,0:T(8,128)(2,1)S(1)}, u32[]{:S(2)}, u32[]{:S(2)}) collective-permute-start(bf16[2,384,128]{2,1,0:T(8,128)(2,1)S(1)} %get-tuple-element.64), channel_id=1, source_target_pairs={{0,2},{2,0},{1,3},{3,1},{4,6},{6,4},{5,7},{7,5},{8,10},{10,8},{9,1... | collective-permute-start | bytes 589832 | tf_op jit(solution)/shard_map/ppermute | solution.py:63
  102.2 0.2 collective-permute-start.28
  102.4 1.4 %collective-permute-start.29 = (bf16[2,384,128]{2,1,0:T(8,128)(2,1)S(1)}, bf16[2,384,128]{2,1,0:T(8,128)(2,1)S(1)}, u32[]{:S(2)}, u32[]{:S(2)}) collective-permute-start(bf16[2,384,128]{2,1,0:T(8,128)(2,1)S(1)} %get-tuple-element.68), channel_id=1, source_target_pairs={{0,10},{2,8},{8,2},{10,0},{1,11},{3,9},{9,3},{11,1},{4,14},{6,12},... | collective-permute-start | bytes 589832 | tf_op jit(solution)/shard_map/ppermute | solution.py:861
  103.8 1.8 %gate_projection.1.refs_5_ = bf16[2,528,384]{2,1,0:T(8,128)(2,1)S(1)} custom-call(bf16[2,528,1536]{2,1,0:T(8,128)(2,1)S(1)} %assemble_rows.1.refs_0_, bf16[1536,384]{1,0:T(8,128)(2,1)S(1)} %gate_weights.1.refs_1_, bf16[8,384,128]{2,1,0:T(8,128)(2,1)S(1)} %get-tuple-element.54.refs_2_.refs_1_), custom_call_target="tpu_custom_call" | custom-call | flops 2500000000 | bytes 7500000 | tf_op jit(solution)/shard_map/gate_projection/pallas_call | solution.py:36
  105.6 0.9 columns.1.refs_3_
  106.5 3.1 %finish.1 = (bf16[8,128,384]{2,1,0:T(8,128)(2,1)S(1)}, f32[8,8,128]{2,1,0:T(8,128)S(1)}) custom-call(s32[58]{0:T(128)S(1)} %copy-done.1, bf16[8,384,128]{2,1,0:T(8,128)(2,1)S(1)} %get-tuple-element.54.refs_2_.refs_1_, bf16[8,128,128]{2,1,0:T(8,128)(2,1)S(1)} %get-tuple-element.55.refs_3_.refs_2_, f32[8,128,128]{2,1,0:T(8,128)S(1)} %get-tuple-element.56.refs_4_.refs_3_, ...), custom_call_target="tpu_custom_call" | custom-call | flops 4000000000 | bytes 12000000 | tf_op jit(solution)/shard_map/finish/pallas_call | solution.py:36
  109.6 2.1 %mix_send.1.refs_4_ = bf16[4,144,1536]{2,1,0:T(8,128)(2,1)S(1)} custom-call(s32[58]{0:T(128)S(1)} %copy-done.1, bf16[8,128,384]{2,1,0:T(8,128)(2,1)S(1)} %get-tuple-element.65.refs_1_, f32[8,8,128]{2,1,0:T(8,128)S(1)} %get-tuple-element.66.refs_2_, bf16[1536,384]{1,0:T(8,128)(2,1)S(1)} %columns.1.refs_3_, ...), custom_call_target="tpu_custom_call" | custom-call | flops 2100000000 | bytes 6300000 | tf_op jit(solution)/shard_map/mix_send/pallas_call | solution.py:36
  111.8 2.1 %mix_keep.1.refs_0_ = bf16[4,144,1536]{2,1,0:T(8,128)(2,1)S(1)} custom-call(s32[58]{0:T(128)S(1)} %copy-done.1, bf16[8,128,384]{2,1,0:T(8,128)(2,1)S(1)} %get-tuple-element.65.refs_1_, f32[8,8,128]{2,1,0:T(8,128)S(1)} %get-tuple-element.66.refs_2_, bf16[1536,384]{1,0:T(8,128)(2,1)S(1)} %columns.1.refs_3_, bf16[4,144,1536]{2,1,0:T(8,128)(2,1)S(1)} %mix_send.1.refs_4_), custom_call_target="tpu_custom_call" | custom-call | flops 2100000000 | bytes 6300000 | tf_op jit(solution)/shard_map/mix_keep/pallas_call | solution.py:36
  114.0 1.6 %collective-permute-done.30.refs_1_ = bf16[4,144,1536]{2,1,0:T(8,128)(2,1)S(1)} collective-permute-done((bf16[4,144,1536]{2,1,0:T(8,128)(2,1)S(1)}, bf16[4,144,1536]{2,1,0:T(8,128)(2,1)S(1)}, u32[]{:S(2)}, u32[]{:S(2)}) %collective-permute-start.30) | collective-permute-done | bytes 1769504 | tf_op jit(solution)/shard_map/ppermute | solution.py:63
  115.5 0.4 add_cores.1
  115.9 2.0 %collective-permute-start.31 = (bf16[2,144,768]{2,1,0:T(8,128)(2,1)S(1)}, bf16[2,144,768]{2,1,0:T(8,128)(2,1)S(1)}, u32[]{:S(2)}, u32[]{:S(2)}) collective-permute-start(bf16[2,144,768]{2,1,0:T(8,128)(2,1)S(1)} %get-tuple-element.70.refs_5_), channel_id=1, source_target_pairs={{0,2},{2,0},{1,3},{3,1},{4,6},{6,4},{5,7},{7,5},{8,10},{10,8},{9,1... | collective-permute-start | bytes 1327112 | tf_op jit(solution)/shard_map/ppermute | solution.py:63
  117.9 0.2 collective-permute-start.32
  118.1 10.6 %collective-permute-done.32.refs_3_ = bf16[2,128,768]{2,1,0:T(8,128)(2,1)S(1)} collective-permute-done((bf16[2,128,768]{2,1,0:T(8,128)(2,1)S(1)}, bf16[2,128,768]{2,1,0:T(8,128)(2,1)S(1)}, u32[]{:S(2)}, u32[]{:S(2)}) %collective-permute-start.32) | collective-permute-done | bytes 393248 | tf_op jit(solution)/shard_map/ppermute | solution.py:63
  128.7 0.2 add_second.1
  128.9 1.1 collective-permute-start.33
  130.0 0.7 collective-permute-start.34
  130.7 1.8 %pages.1 = f32[2,4,384,128]{3,2,1,0:T(8,128)} custom-call(s32[58]{0:T(128)S(1)} %copy-done.1, bf16[2,384,128]{2,1,0:T(8,128)(2,1)S(1)} %get-tuple-element.77.refs_1_, bf16[2,384,128]{2,1,0:T(8,128)(2,1)S(1)} %collective-permute-done.25.refs_7_.refs_2_, bf16[2,384,128]{2,1,0:T(8,128)(2,1)S(1)} %collective-permute-done.28.refs_4_.refs_3_, ...), custom_call_target="tpu_custom_call" | custom-call | flops 1800000000 | bytes 5400000 | tf_op jit(solution)/shard_map/pages/pallas_call | solution.py:36
  132.5 3.3 %collective-permute-done.34.refs_3_ = bf16[128,768]{1,0:T(8,128)(2,1)S(1)} collective-permute-done((bf16[128,768]{1,0:T(8,128)(2,1)S(1)}, bf16[128,768]{1,0:T(8,128)(2,1)S(1)}, u32[]{:S(2)}, u32[]{:S(2)}) %collective-permute-start.34) | collective-permute-done | bytes 196640 | tf_op jit(solution)/shard_map/ppermute | solution.py:63
  135.9 0.9 add_last.1
  (80 shorter events, 0.7 us)
Async XLA Ops:
  0.6 66.8 %copy-start = (f32[4,24,64,128]{3,2,1,0:T(8,128)S(1)}, f32[4,24,64,128]{3,2,1,0:T(8,128)}, u32[]{:S(2)}) copy-start(f32[4,24,64,128]{3,2,1,0:T(8,128)} %param.34) | copy-start | bytes 9437188
  0.6 7.6 %copy-start.13 = (s32[32]{0:T(128)S(1)}, s32[32]{0:T(128)}, u32[]{:S(2)}) copy-start(s32[32]{0:T(128)} %param.22) | copy-start | bytes 388
  0.7 7.6 %copy-start.14 = (s32[8]{0:T(128)S(1)}, s32[8]{0:T(128)}, u32[]{:S(2)}) copy-start(s32[8]{0:T(128)} %param.32) | copy-start | bytes 100
  0.7 7.6 %copy-start.15 = (s32[8]{0:T(128)S(1)}, s32[8]{0:T(128)}, u32[]{:S(2)}) copy-start(s32[8]{0:T(128)} %param.33) | copy-start | bytes 100
  0.7 7.6 %copy-start.16 = (s32[2]{0:T(128)S(1)}, s32[2]{0:T(128)}, u32[]{:S(2)}) copy-start(s32[2]{0:T(128)} %param.35) | copy-start | bytes 28
  3.1 17.5 %all-to-all-start = ((bf16[8,48,1024]{2,1,0:T(8,128)(2,1)}), bf16[8,48,1024]{2,1,0:T(8,128)(2,1)}, u32[]{:S(2)}, u32[]{:S(2)}) async-start(bf16[8,48,1024]{2,1,0:T(8,128)(2,1)} %pack_rows.1.refs_2_), calls=%async_computation | async-start | bytes 1572864 | tf_op jit(solution)/shard_map/all_to_all | solution.py:677
  8.9 7.5 %copy-start.9 = (f32[1536]{0:T(1024)S(1)}, f32[1536]{0:T(1024)}, u32[]{:S(2)}) copy-start(f32[1536]{0:T(1024)} %param.30) | copy-start | bytes 18436
  9.0 7.5 %copy-start.10 = (f32[1536]{0:T(1024)S(1)}, f32[1536]{0:T(1024)}, u32[]{:S(2)}) copy-start(f32[1536]{0:T(1024)} %param.25) | copy-start | bytes 18436
  9.0 7.5 %copy-start.11 = (f32[4,256]{1,0:T(4,128)S(1)}, f32[4,256]{1,0:T(4,128)}, u32[]{:S(2)}) copy-start(f32[4,256]{1,0:T(4,128)} %param.24) | copy-start | bytes 12292
  9.0 7.5 %copy-start.12 = (f32[256]{0:T(256)S(1)}, f32[256]{0:T(256)}, u32[]{:S(2)}) copy-start(f32[256]{0:T(256)} %param.26) | copy-start | bytes 3076
  9.0 7.6 %copy-start.17 = (f32[24]{0:T(128)S(1)}, f32[24]{0:T(128)}, u32[]{:S(2)}) copy-start(f32[24]{0:T(128)} %param.29) | copy-start | bytes 292
  9.0 7.6 %copy-start.18 = (f32[24]{0:T(128)S(1)}, f32[24]{0:T(128)}, u32[]{:S(2)}) copy-start(f32[24]{0:T(128)} %param.28) | copy-start | bytes 292
  9.0 7.6 %copy-start.19 = (f32[24]{0:T(128)S(1)}, f32[24]{0:T(128)}, u32[]{:S(2)}) copy-start(f32[24]{0:T(128)} %param.27) | copy-start | bytes 292
  11.6 22.3 %collective-permute-start = (bf16[128,1536]{1,0:T(8,128)(2,1)}, bf16[128,1536]{1,0:T(8,128)(2,1)}, u32[]{:S(2)}, u32[]{:S(2)}) collective-permute-start(bf16[128,1536]{1,0:T(8,128)(2,1)} %get-tuple-element.40), channel_id=1, source_target_pairs={{0,2},{2,0},{1,3},{3,1},{4,6},{6,4},{5,7},{7,5},{8,10},{10,8},{9,1... | collective-permute-start | bytes 1179656 | tf_op jit(solution)/shard_map/ppermute | solution.py:63
  13.6 20.3 %collective-permute-start.1 = (bf16[128,1536]{1,0:T(8,128)(2,1)}, bf16[128,1536]{1,0:T(8,128)(2,1)}, u32[]{:S(2)}, u32[]{:S(2)}) collective-permute-start(bf16[128,1536]{1,0:T(8,128)(2,1)} %get-tuple-element.40), channel_id=1, source_target_pairs={{0,8},{8,0},{1,9},{9,1},{2,10},{10,2},{3,11},{11,3},{4,12},{12,4},... | collective-permute-start | bytes 1179656 | tf_op jit(solution)/shard_map/ppermute | solution.py:63
  15.1 11.1 %collective-permute-start.2 = (bf16[16,1536]{1,0:T(8,128)(2,1)}, bf16[16,1536]{1,0:T(8,128)(2,1)S(1)}, u32[]{:S(2)}, u32[]{:S(2)}) collective-permute-start(bf16[16,1536]{1,0:T(8,128)(2,1)} %get-tuple-element.41), channel_id=1, source_target_pairs={{2,4},{6,8},{10,12},{14,16},{18,20},{22,24},{26,28},{3,5},{7,9},{1... | collective-permute-start | bytes 147464 | tf_op jit(solution)/shard_map/ppermute | solution.py:717
  15.8 10.5 %collective-permute-start.3 = (bf16[16,1536]{1,0:T(8,128)(2,1)}, bf16[16,1536]{1,0:T(8,128)(2,1)S(1)}, u32[]{:S(2)}, u32[]{:S(2)}) collective-permute-start(bf16[16,1536]{1,0:T(8,128)(2,1)} %get-tuple-element.41), channel_id=1, source_target_pairs={{2,6},{6,10},{10,14},{14,18},{18,22},{22,26},{26,30},{3,7},{7,11},... | collective-permute-start | bytes 147464 | tf_op jit(solution)/shard_map/ppermute | solution.py:718
  16.6 9.6 %copy-start.8 = (f32[4,1536]{1,0:T(4,128)S(1)}, f32[4,1536]{1,0:T(4,128)}, u32[]{:S(2)}) copy-start(f32[4,1536]{1,0:T(4,128)} %param.23) | copy-start | bytes 73732
  16.6 17.3 %copy-start.1 = (s32[58]{0:T(128)S(1)}, s32[58]{0:T(128)}, u32[]{:S(2)}) copy-start(s32[58]{0:T(128)} %concatenate.15.refs_0_) | copy-start | bytes 700
  22.5 0.7 copy-start.6
  23.3 22.3 %collective-permute-start.11 = (bf16[240,512]{1,0:T(8,128)(2,1)S(1)}, bf16[240,512]{1,0:T(8,128)(2,1)S(1)}, u32[]{:S(2)}, u32[]{:S(2)}) collective-permute-start(bf16[240,512]{1,0:T(8,128)(2,1)S(1)} %get-tuple-element.45), channel_id=1, source_target_pairs={{0,16},{16,0},{1,17},{17,1},{2,18},{18,2},{3,19},{19,3},{4,20},{20... | collective-permute-start | bytes 737288 | tf_op jit(solution)/shard_map/ppermute | solution.py:599
  26.2 17.8 %collective-permute-start.12 = (bf16[160,512]{1,0:T(8,128)(2,1)S(1)}, bf16[160,512]{1,0:T(8,128)(2,1)}, u32[]{:S(2)}, u32[]{:S(2)}) collective-permute-start(bf16[160,512]{1,0:T(8,128)(2,1)S(1)} %get-tuple-element.46), channel_id=1, source_target_pairs={{0,16},{16,0},{1,17},{17,1},{2,18},{18,2},{3,19},{19,3},{4,20},{20... | collective-permute-start | bytes 491528 | tf_op jit(solution)/shard_map/ppermute | solution.py:599
  26.2 9.6 %copy-start.4 = (bf16[16,1536]{1,0:T(8,128)(2,1)}, bf16[16,1536]{1,0:T(8,128)(2,1)S(1)}, u32[]{:S(2)}) copy-start(bf16[16,1536]{1,0:T(8,128)(2,1)S(1)} %collective-permute-done.3.refs_4_.refs_11_) | copy-start | bytes 147460
  26.3 25.2 %collective-permute-start.10 = (bf16[400,512]{1,0:T(8,128)(2,1)}, bf16[400,512]{1,0:T(8,128)(2,1)}, u32[]{:S(2)}, u32[]{:S(2)}) collective-permute-start(bf16[400,512]{1,0:T(8,128)(2,1)} %get-tuple-element.42.refs_5_.refs_1_), channel_id=1, source_target_pairs={{0,4},{4,0},{1,5},{5,1},{2,6},{6,2},{3,7},{7,3},{8,12},{12,8},{9,1... | collective-permute-start | bytes 1228808 | tf_op jit(solution)/shard_map/ppermute | solution.py:63
  35.9 11.2 %collective-permute-start.4 = (bf16[64,1536]{1,0:T(8,128)(2,1)}, bf16[64,1536]{1,0:T(8,128)(2,1)}, u32[]{:S(2)}, u32[]{:S(2)}) collective-permute-start(bf16[64,1536]{1,0:T(8,128)(2,1)} %get-tuple-element.43), channel_id=1, source_target_pairs={{0,2},{2,0},{1,3},{3,1},{4,6},{6,4},{5,7},{7,5},{8,10},{10,8},{9,1... | collective-permute-start | bytes 589832 | tf_op jit(solution)/shard_map/ppermute | solution.py:63
  40.2 8.0 %collective-permute-start.5 = (bf16[80,1536]{1,0:T(8,128)(2,1)}, bf16[80,1536]{1,0:T(8,128)(2,1)}, u32[]{:S(2)}, u32[]{:S(2)}) collective-permute-start(bf16[80,1536]{1,0:T(8,128)(2,1)} %get-tuple-element.44), channel_id=1, source_target_pairs={{0,8},{8,0},{1,9},{9,1},{2,10},{10,2},{3,11},{11,3},{4,12},{12,4},... | collective-permute-start | bytes 737288 | tf_op jit(solution)/shard_map/ppermute | solution.py:63
  44.0 7.5 %collective-permute-start.14 = (bf16[160,512]{1,0:T(8,128)(2,1)}, bf16[160,512]{1,0:T(8,128)(2,1)}, u32[]{:S(2)}, u32[]{:S(2)}) collective-permute-start(bf16[160,512]{1,0:T(8,128)(2,1)} %collective-permute-done.12.refs_4_.refs_1_), channel_id=1, source_target_pairs={{0,4},{4,0},{1,5},{5,1},{2,6},{6,2},{3,7},{7,3},{8,12},{12,8},{9,1... | collective-permute-start | bytes 491528 | tf_op jit(solution)/shard_map/ppermute | solution.py:63
  45.6 9.3 %collective-permute-start.13 = (bf16[240,512]{1,0:T(8,128)(2,1)S(1)}, bf16[240,512]{1,0:T(8,128)(2,1)}, u32[]{:S(2)}, u32[]{:S(2)}) collective-permute-start(bf16[240,512]{1,0:T(8,128)(2,1)S(1)} %collective-permute-done.11.refs_3_), channel_id=1, source_target_pairs={{0,4},{4,0},{1,5},{5,1},{2,6},{6,2},{3,7},{7,3},{8,12},{12,8},{9,1... | collective-permute-start | bytes 737288 | tf_op jit(solution)/shard_map/ppermute | solution.py:63
  46.0 1.0 copy-start.7
  47.0 9.6 %copy-start.2 = (bf16[256,1536]{1,0:T(8,128)(2,1)S(1)}, bf16[256,1536]{1,0:T(8,128)(2,1)}, u32[]{:S(2)}) copy-start(bf16[256,1536]{1,0:T(8,128)(2,1)} %refs_1_.5) | copy-start | bytes 2359300
  47.0 9.6 %copy-start.5 = (bf16[16,1536]{1,0:T(8,128)(2,1)S(1)}, bf16[16,1536]{1,0:T(8,128)(2,1)}, u32[]{:S(2)}) copy-start(bf16[16,1536]{1,0:T(8,128)(2,1)} %copy-done.4) | copy-start | bytes 147460
  47.1 9.4 %collective-permute-start.6 = (bf16[128,1536]{1,0:T(8,128)(2,1)}, bf16[128,1536]{1,0:T(8,128)(2,1)S(1)}, u32[]{:S(2)}, u32[]{:S(2)}) collective-permute-start(bf16[128,1536]{1,0:T(8,128)(2,1)} %collective-permute-done.refs_1_.refs_2_), channel_id=1, source_target_pairs={{0,1},{1,0},{2,3},{3,2},{4,5},{5,4},{6,7},{7,6},{8,9},{9,8},{10,11... | collective-permute-start | bytes 1179656 | tf_op jit(solution)/shard_map/ppermute | solution.py:63
  48.2 8.3 %collective-permute-start.7 = (bf16[128,1536]{1,0:T(8,128)(2,1)}, bf16[128,1536]{1,0:T(8,128)(2,1)S(1)}, u32[]{:S(2)}, u32[]{:S(2)}) collective-permute-start(bf16[128,1536]{1,0:T(8,128)(2,1)} %collective-permute-done.1.refs_2_.refs_3_), channel_id=1, source_target_pairs={{0,1},{1,0},{2,3},{3,2},{4,5},{5,4},{6,7},{7,6},{8,9},{9,8},{10,11... | collective-permute-start | bytes 1179656 | tf_op jit(solution)/shard_map/ppermute | solution.py:63
  51.5 16.0 %collective-permute-start.16 = (bf16[384,384]{1,0:T(8,128)(2,1)S(1)}, bf16[384,384]{1,0:T(8,128)(2,1)S(1)}, u32[]{:S(2)}, u32[]{:S(2)}) collective-permute-start(bf16[384,384]{1,0:T(8,128)(2,1)S(1)} %gate_part.1.refs_1_), channel_id=1, source_target_pairs={{0,16},{16,0},{1,17},{17,1},{2,18},{18,2},{3,19},{19,3},{4,20},{20... | collective-permute-start | bytes 884744 | tf_op jit(solution)/shard_map/ppermute | solution.py:599
  51.5 5.0 %collective-permute-start.8 = (bf16[64,1536]{1,0:T(8,128)(2,1)}, bf16[64,1536]{1,0:T(8,128)(2,1)S(1)}, u32[]{:S(2)}, u32[]{:S(2)}) collective-permute-start(bf16[64,1536]{1,0:T(8,128)(2,1)} %collective-permute-done.4.refs_4_), channel_id=1, source_target_pairs={{0,1},{1,0},{2,3},{3,2},{4,5},{5,4},{6,7},{7,6},{8,9},{9,8},{10,11... | collective-permute-start | bytes 589832 | tf_op jit(solution)/shard_map/ppermute | solution.py:63
  54.9 1.7 %collective-permute-start.9 = (bf16[80,1536]{1,0:T(8,128)(2,1)}, bf16[80,1536]{1,0:T(8,128)(2,1)S(1)}, u32[]{:S(2)}, u32[]{:S(2)}) collective-permute-start(bf16[80,1536]{1,0:T(8,128)(2,1)} %collective-permute-done.5.refs_5_), channel_id=1, source_target_pairs={{0,1},{1,0},{2,3},{3,2},{4,5},{5,4},{6,7},{7,6},{8,9},{9,8},{10,11... | collective-permute-start | bytes 737288 | tf_op jit(solution)/shard_map/ppermute | solution.py:63
  58.1 3.2 %copy-start.3 = (f32[1536,96]{0,1:T(8,128)S(1)}, f32[1536,96]{0,1:T(8,128)}, u32[]{:S(2)}) copy-start(f32[1536,96]{0,1:T(8,128)} %param.31) | copy-start | bytes 1769476
  60.8 12.3 %collective-permute-start.15 = (bf16[2,528,128]{2,1,0:T(8,128)(2,1)S(1)}, bf16[2,528,128]{2,1,0:T(8,128)(2,1)S(1)}, u32[]{:S(2)}, u32[]{:S(2)}) collective-permute-start(bf16[2,528,128]{2,1,0:T(8,128)(2,1)S(1)} %get-tuple-element.48.refs_2_), channel_id=1, source_target_pairs={{0,1},{1,0},{2,3},{3,2},{4,5},{5,4},{6,7},{7,6},{8,9},{9,8},{10,11... | collective-permute-start | bytes 811016 | tf_op jit(solution)/shard_map/ppermute | solution.py:63
  61.9 6.0 %collective-permute-start.19 = (bf16[96,384]{1,0:T(8,128)(2,1)S(1)}, bf16[96,384]{1,0:T(8,128)(2,1)S(1)}, u32[]{:S(2)}, u32[]{:S(2)}) collective-permute-start(bf16[96,384]{1,0:T(8,128)(2,1)S(1)} %get-tuple-element.61), channel_id=1, source_target_pairs={{0,2},{2,0},{1,3},{3,1},{4,6},{6,4},{5,7},{7,5},{8,10},{10,8},{9,1... | collective-permute-start | bytes 221192 | tf_op jit(solution)/shard_map/ppermute | solution.py:63
  63.4 6.2 %collective-permute-start.20 = (bf16[96,384]{1,0:T(8,128)(2,1)S(1)}, bf16[96,384]{1,0:T(8,128)(2,1)S(1)}, u32[]{:S(2)}, u32[]{:S(2)}) collective-permute-start(bf16[96,384]{1,0:T(8,128)(2,1)S(1)} %get-tuple-element.62), channel_id=1, source_target_pairs={{0,8},{8,0},{1,9},{9,1},{2,10},{10,2},{3,11},{11,3},{4,12},{12,4},... | collective-permute-start | bytes 221192 | tf_op jit(solution)/shard_map/ppermute | solution.py:63
  66.0 5.3 %collective-permute-start.21 = (bf16[96,384]{1,0:T(8,128)(2,1)S(1)}, bf16[96,384]{1,0:T(8,128)(2,1)S(1)}, u32[]{:S(2)}, u32[]{:S(2)}) collective-permute-start(bf16[96,384]{1,0:T(8,128)(2,1)S(1)} %get-tuple-element.63), channel_id=1, source_target_pairs={{0,10},{2,8},{8,2},{10,0},{1,11},{3,9},{9,3},{11,1},{4,14},{6,12},... | collective-permute-start | bytes 221192 | tf_op jit(solution)/shard_map/ppermute | solution.py:745
  67.5 15.7 %collective-permute-start.23 = (bf16[384,384]{1,0:T(8,128)(2,1)S(1)}, bf16[384,384]{1,0:T(8,128)(2,1)S(1)}, u32[]{:S(2)}, u32[]{:S(2)}) collective-permute-start(bf16[384,384]{1,0:T(8,128)(2,1)S(1)} %gate_part.1.refs_1_), channel_id=1, source_target_pairs={{0,4},{4,0},{1,5},{5,1},{2,6},{6,2},{3,7},{7,3},{8,12},{12,8},{9,1... | collective-permute-start | bytes 884744 | tf_op jit(solution)/shard_map/ppermute | solution.py:63
  67.8 15.3 %collective-permute-start.24 = (bf16[384,384]{1,0:T(8,128)(2,1)S(1)}, bf16[384,384]{1,0:T(8,128)(2,1)S(1)}, u32[]{:S(2)}, u32[]{:S(2)}) collective-permute-start(bf16[384,384]{1,0:T(8,128)(2,1)S(1)} %collective-permute-done.16.refs_7_.refs_3_), channel_id=1, source_target_pairs={{0,4},{4,0},{1,5},{5,1},{2,6},{6,2},{3,7},{7,3},{8,12},{12,8},{9,1... | collective-permute-start | bytes 884744 | tf_op jit(solution)/shard_map/ppermute | solution.py:63
  71.4 15.5 %collective-permute-start.22 = (bf16[384,384]{1,0:T(8,128)(2,1)S(1)}, bf16[384,384]{1,0:T(8,128)(2,1)S(1)}, u32[]{:S(2)}, u32[]{:S(2)}) collective-permute-start(bf16[384,384]{1,0:T(8,128)(2,1)S(1)} %out_part.1.refs_1_), channel_id=1, source_target_pairs={{0,16},{16,0},{1,17},{17,1},{2,18},{18,2},{3,19},{19,3},{4,20},{20... | collective-permute-start | bytes 884744 | tf_op jit(solution)/shard_map/ppermute | solution.py:599
  81.1 8.1 %collective-permute-start.17 = (bf16[2,400,128]{2,1,0:T(8,128)(2,1)S(1)}, bf16[2,400,128]{2,1,0:T(8,128)(2,1)S(1)}, u32[]{:S(2)}, u32[]{:S(2)}) collective-permute-start(bf16[2,400,128]{2,1,0:T(8,128)(2,1)S(1)} %get-tuple-element.51.refs_1_.refs_5_), channel_id=1, source_target_pairs={{0,4},{4,0},{1,5},{5,1},{2,6},{6,2},{3,7},{7,3},{8,12},{12,8},{9,1... | collective-permute-start | bytes 614408 | tf_op jit(solution)/shard_map/ppermute | solution.py:63
  81.2 24.4 %collective-permute-start.26 = (bf16[384,384]{1,0:T(8,128)(2,1)S(1)}, bf16[384,384]{1,0:T(8,128)(2,1)S(1)}, u32[]{:S(2)}, u32[]{:S(2)}) collective-permute-start(bf16[384,384]{1,0:T(8,128)(2,1)S(1)} %out_part.1.refs_1_), channel_id=1, source_target_pairs={{0,4},{4,0},{1,5},{5,1},{2,6},{6,2},{3,7},{7,3},{8,12},{12,8},{9,1... | collective-permute-start | bytes 884744 | tf_op jit(solution)/shard_map/ppermute | solution.py:63
  86.9 18.7 %collective-permute-start.27 = (bf16[384,384]{1,0:T(8,128)(2,1)S(1)}, bf16[384,384]{1,0:T(8,128)(2,1)S(1)}, u32[]{:S(2)}, u32[]{:S(2)}) collective-permute-start(bf16[384,384]{1,0:T(8,128)(2,1)S(1)} %collective-permute-done.22.refs_9_.refs_3_), channel_id=1, source_target_pairs={{0,4},{4,0},{1,5},{5,1},{2,6},{6,2},{3,7},{7,3},{8,12},{12,8},{9,1... | collective-permute-start | bytes 884744 | tf_op jit(solution)/shard_map/ppermute | solution.py:63
  89.8 9.2 %collective-permute-start.18 = (bf16[400,128]{1,0:T(8,128)(2,1)S(1)}, bf16[400,128]{1,0:T(8,128)(2,1)S(1)}, u32[]{:S(2)}, u32[]{:S(2)}) collective-permute-start(bf16[400,128]{1,0:T(8,128)(2,1)S(1)} %compose.1.refs_8_), channel_id=1, source_target_pairs={{0,16},{1,17},{2,18},{3,19},{4,20},{5,21},{6,22},{7,23},{8,24},{9,... | collective-permute-start | bytes 307208 | tf_op jit(solution)/shard_map/ppermute | solution.py:836
  100.2 6.3 %collective-permute-start.25 = (bf16[2,384,128]{2,1,0:T(8,128)(2,1)S(1)}, bf16[2,384,128]{2,1,0:T(8,128)(2,1)S(1)}, u32[]{:S(2)}, u32[]{:S(2)}) collective-permute-start(bf16[2,384,128]{2,1,0:T(8,128)(2,1)S(1)} %get-tuple-element.64), channel_id=1, source_target_pairs={{0,2},{2,0},{1,3},{3,1},{4,6},{6,4},{5,7},{7,5},{8,10},{10,8},{9,1... | collective-permute-start | bytes 589832 | tf_op jit(solution)/shard_map/ppermute | solution.py:63
  102.2 7.4 %collective-permute-start.28 = (bf16[2,384,128]{2,1,0:T(8,128)(2,1)S(1)}, bf16[2,384,128]{2,1,0:T(8,128)(2,1)S(1)}, u32[]{:S(2)}, u32[]{:S(2)}) collective-permute-start(bf16[2,384,128]{2,1,0:T(8,128)(2,1)S(1)} %get-tuple-element.67), channel_id=1, source_target_pairs={{0,8},{8,0},{1,9},{9,1},{2,10},{10,2},{3,11},{11,3},{4,12},{12,4},... | collective-permute-start | bytes 589832 | tf_op jit(solution)/shard_map/ppermute | solution.py:63
  102.4 7.2 %collective-permute-start.29 = (bf16[2,384,128]{2,1,0:T(8,128)(2,1)S(1)}, bf16[2,384,128]{2,1,0:T(8,128)(2,1)S(1)}, u32[]{:S(2)}, u32[]{:S(2)}) collective-permute-start(bf16[2,384,128]{2,1,0:T(8,128)(2,1)S(1)} %get-tuple-element.68), channel_id=1, source_target_pairs={{0,10},{2,8},{8,2},{10,0},{1,11},{3,9},{9,3},{11,1},{4,14},{6,12},... | collective-permute-start | bytes 589832 | tf_op jit(solution)/shard_map/ppermute | solution.py:861
  111.8 3.8 %collective-permute-start.30 = (bf16[4,144,1536]{2,1,0:T(8,128)(2,1)S(1)}, bf16[4,144,1536]{2,1,0:T(8,128)(2,1)S(1)}, u32[]{:S(2)}, u32[]{:S(2)}) collective-permute-start(bf16[4,144,1536]{2,1,0:T(8,128)(2,1)S(1)} %mix_send.1.refs_4_), channel_id=1, source_target_pairs={{0,1},{1,0},{2,3},{3,2},{4,5},{5,4},{6,7},{7,6},{8,9},{9,8},{10,11... | collective-permute-start | bytes 5308424 | tf_op jit(solution)/shard_map/ppermute | solution.py:63
  115.9 12.9 %collective-permute-start.31 = (bf16[2,144,768]{2,1,0:T(8,128)(2,1)S(1)}, bf16[2,144,768]{2,1,0:T(8,128)(2,1)S(1)}, u32[]{:S(2)}, u32[]{:S(2)}) collective-permute-start(bf16[2,144,768]{2,1,0:T(8,128)(2,1)S(1)} %get-tuple-element.70.refs_5_), channel_id=1, source_target_pairs={{0,2},{2,0},{1,3},{3,1},{4,6},{6,4},{5,7},{7,5},{8,10},{10,8},{9,1... | collective-permute-start | bytes 1327112 | tf_op jit(solution)/shard_map/ppermute | solution.py:63
  117.9 10.9 %collective-permute-start.32 = (bf16[2,128,768]{2,1,0:T(8,128)(2,1)S(1)}, bf16[2,128,768]{2,1,0:T(8,128)(2,1)S(1)}, u32[]{:S(2)}, u32[]{:S(2)}) collective-permute-start(bf16[2,128,768]{2,1,0:T(8,128)(2,1)S(1)} %get-tuple-element.72), channel_id=1, source_target_pairs={{0,8},{8,0},{1,9},{9,1},{2,10},{10,2},{3,11},{11,3},{4,12},{12,4},... | collective-permute-start | bytes 1179656 | tf_op jit(solution)/shard_map/ppermute | solution.py:63
  128.9 7.0 %collective-permute-start.33 = (bf16[144,768]{1,0:T(8,128)(2,1)S(1)}, bf16[144,768]{1,0:T(8,128)(2,1)S(1)}, u32[]{:S(2)}, u32[]{:S(2)}) collective-permute-start(bf16[144,768]{1,0:T(8,128)(2,1)S(1)} %get-tuple-element.74), channel_id=1, source_target_pairs={{0,8},{8,0},{1,9},{9,1},{2,10},{10,2},{3,11},{11,3},{4,12},{12,4},... | collective-permute-start | bytes 663560 | tf_op jit(solution)/shard_map/ppermute | solution.py:63
  130.0 5.8 %collective-permute-start.34 = (bf16[128,768]{1,0:T(8,128)(2,1)S(1)}, bf16[128,768]{1,0:T(8,128)(2,1)S(1)}, u32[]{:S(2)}, u32[]{:S(2)}) collective-permute-start(bf16[128,768]{1,0:T(8,128)(2,1)S(1)} %get-tuple-element.76), channel_id=1, source_target_pairs={{0,2},{2,0},{1,3},{3,1},{4,6},{6,4},{5,7},{7,5},{8,10},{10,8},{9,1... | collective-permute-start | bytes 589832 | tf_op jit(solution)/shard_map/ppermute | solution.py:63
